TPU v7x, 32 devices: a whole 2x2x4 slice. The times are simulated.
32 devices in a mesh: head: 4 (over y, x), blk: 8 (over z, core).
Axes of the slice: x: 2, y: 2, z: 4, core: 2. Of those that a mesh axis runs over, the one named last changes fastest.
Arguments:
- doc_x: bfloat16 [8192, 1024], P('blk'), may hold values from -6 to 6
- doc_seg: int32 [8192], P('blk'), may hold values from 0 to 127, as said below
- doc_query: int32 [128], replicated, may hold values from 0 to 7
- doc_var: int32 [8192], P('blk'), may hold values from 0 to 7
- query_len: int32 [8], replicated, may hold values from 256 to 512, as said below
- block_perm: int32 [8], replicated, may hold values from 0 to 7, each once
- cache_k: bfloat16 [4096, 1024], P('blk', 'head'), may hold values from -164 to 164
- cache_v: bfloat16 [4096, 1024], P('blk', 'head'), may hold values from -6 to 6
- cache_var: int32 [4096], P('blk'), may hold values from 0 to 7
- w_query: bfloat16 [1024, 1024], P(None, 'head'), may hold values from -0.1875 to 0.1875
- w_key: bfloat16 [1024, 1024], P(None, 'head'), may hold values from -0.5 to 0.5
- w_value: bfloat16 [1024, 1024], P(None, 'head'), may hold values from -0.1875 to 0.1875
- w_out: bfloat16 [1024, 1024], P('head'), may hold values from -0.1875 to 0.1875
- var_bias: float32 [2, 16], P(None, 'head'), may hold values from -1 to 1
- norm_gain: float32 [1024], replicated, may hold values from 0.1 to 1.9
- readout: float32 [1024], replicated, may hold values from -1.5 to 1.5
Outputs:
- update: float32 [8192, 1024], P('blk', 'head')
- pooled: float32 [128], P('blk')
Inputs may be any that keep to these rules, and one draw needn't show every extreme that they name: `doc_seg`: index i of blk holds documents i * 16 to (i + 1) * 16 - 1 whole; its 1024 tokens form 8 runs of 128 tokens, run j holding its documents 2j and 2j + 1, both of one query, and the 8 runs of one index belong to 8 different queries. query_len[0] = 512.
All inputs are finite; a program needn't handle non-finite values.
Results may differ from a plain program's by a relative error of at most 0.012.
The roundings to bfloat16 on the way count: a program that leaves them out, or rounds other values in their place, can miss the bound.
Values may be sent and summed in bfloat16 or wider, within the bound.
No kernel may reach another device: no remote copies, remote signals or barrier semaphores. Data moves between devices by JAX's collectives and lax.ppermute only.
A program may use at most 128 MiB of HBM per device.

v0:
```python
import jax
import jax.numpy as jnp
from jax import lax
from jax.sharding import PartitionSpec as P

D = 1024
DH = 64
QUERIES = 8


def rotary(projected, positions):
    row_count = projected.shape[0]
    head_count = projected.shape[1] // DH
    half_size = DH // 2
    shaped = projected.reshape(row_count, head_count, DH)
    frequency = 10000.0 ** (-jnp.arange(half_size, dtype=jnp.float32) / half_size)
    angles = positions.astype(jnp.float32)[:, None] * frequency[None, :]
    cosine = jnp.cos(angles)[:, None, :]
    sine_part = jnp.sin(angles)[:, None, :]
    first_half = shaped[:, :, :half_size]
    second_half = shaped[:, :, half_size:]
    turned = jnp.concatenate(
        [
            first_half * cosine - second_half * sine_part,
            second_half * cosine + first_half * sine_part,
        ],
        axis=2,
    )
    return turned.reshape(row_count, head_count * DH)


def softmax_part(scores, allowed):
    scores = jnp.where(allowed, scores, -1e30)
    peak = jnp.max(scores, axis=-1)
    weights = jnp.where(allowed, jnp.exp(scores - peak[..., None]), 0.0)
    return (peak, jnp.sum(weights, axis=-1), weights.astype(jnp.bfloat16))


def cache_part(
    recv_q, recv_var, cache_keys, cache_values, cache_var, row_valid, bias_same, bias_other
):
    source_count = recv_q.shape[0]
    item_count = recv_q.shape[1]
    col_count = recv_q.shape[2]
    head_count = cache_keys.shape[1]
    total_rows = source_count * item_count
    block_rows = 512
    block_count = total_rows // block_rows
    flat_q = recv_q.reshape(block_count, block_rows, head_count, DH)
    flat_var = recv_var.reshape(block_count, block_rows).astype(jnp.int32)

    def one_block(block_inputs):
        block_q, block_var = block_inputs
        scores = (
            jnp.einsum("thd,rhd->htr", block_q, cache_keys, preferred_element_type=jnp.float32)
            * 0.125
        )
        scores = scores + jnp.where(
            (block_var[:, None] == cache_var[None, :])[None], bias_same, bias_other
        )
        allowed = jnp.broadcast_to(row_valid[None, None, :], scores.shape)
        peak, total_weight, weights = softmax_part(scores, allowed)
        mixed = jnp.einsum(
            "htr,rhd->thd", weights, cache_values, preferred_element_type=jnp.float32
        )
        return (peak.T, total_weight.T, mixed.reshape(block_rows, col_count))

    maxima, totals, sums = lax.map(one_block, (flat_q, flat_var))
    return (
        maxima.reshape(source_count, item_count, head_count),
        totals.reshape(source_count, item_count, head_count),
        sums.reshape(source_count, item_count, col_count),
    )


def body(
    doc_x,
    doc_seg,
    doc_query,
    doc_var,
    query_len,
    block_perm,
    cache_k,
    cache_v,
    cache_var,
    w_query,
    w_key,
    w_value,
    w_out,
    var_bias,
    norm_gain,
    readout,
):
    row_count = doc_x.shape[0]
    col_count = w_query.shape[1]
    head_count = col_count // DH
    cache_count = cache_k.shape[0]
    blk_count = lax.axis_size("blk")
    blk_index = lax.axis_index("blk")
    head_index = lax.axis_index("head")
    blocks_each = blk_count // QUERIES
    slot_count = QUERIES
    slot_rows = row_count // slot_count
    doc_count = 2 * slot_count
    first_doc = blk_index * doc_count
    local_seg = doc_seg - first_doc
    member = (local_seg[:, None] == jnp.arange(doc_count, dtype=jnp.int32)[None, :]).astype(
        jnp.int32
    )
    lengths = jnp.sum(member, axis=0)
    starts = jnp.cumsum(lengths) - lengths
    first_pos = jnp.dot(member, starts)
    own_docs_query = lax.dynamic_slice_in_dim(doc_query, first_doc, doc_count)
    query_table = (own_docs_query[:, None] == jnp.arange(QUERIES, dtype=jnp.int32)[None, :]).astype(
        jnp.int32
    )
    doc_len = jnp.sum(query_table * query_len[None, :], axis=1)
    tok_len = jnp.dot(member, doc_len)
    positions = tok_len + jnp.arange(row_count, dtype=jnp.int32) - first_pos
    query_rot = rotary(
        jnp.dot(doc_x, w_query, preferred_element_type=jnp.float32), positions
    ).astype(jnp.bfloat16)
    key_rot = rotary(jnp.dot(doc_x, w_key, preferred_element_type=jnp.float32), positions).astype(
        jnp.bfloat16
    )
    value_proj = jnp.dot(doc_x, w_value, preferred_element_type=jnp.float32).astype(jnp.bfloat16)
    bias_same = var_bias[0][:, None, None]
    bias_other = var_bias[1][:, None, None]
    shaped_q = query_rot.reshape(slot_count, slot_rows, head_count, DH)
    shaped_k = key_rot.reshape(slot_count, slot_rows, head_count, DH)
    shaped_v = value_proj.reshape(slot_count, slot_rows, head_count, DH)
    slot_seg = local_seg.reshape(slot_count, slot_rows)
    slot_var = doc_var.reshape(slot_count, slot_rows)
    self_scores = (
        jnp.einsum("gthd,gshd->ghts", shaped_q, shaped_k, preferred_element_type=jnp.float32)
        * 0.125
    )
    self_scores = self_scores + jnp.where(
        (slot_var[:, :, None] == slot_var[:, None, :])[:, None], bias_same[None], bias_other[None]
    )
    self_allowed = (slot_seg[:, :, None] == slot_seg[:, None, :])[:, None]
    self_peak, self_total, self_weights = softmax_part(self_scores, self_allowed)
    self_sum = jnp.einsum(
        "ghts,gshd->gthd", self_weights, shaped_v, preferred_element_type=jnp.float32
    )
    self_peak = self_peak.transpose(0, 2, 1)
    self_total = self_total.transpose(0, 2, 1)
    slot_query = own_docs_query.reshape(slot_count, 2)[:, 0]
    block_query = block_perm // blocks_each
    slot_match = block_query[:, None] == slot_query[None, :]
    slot_pick = jnp.sum(
        slot_match.astype(jnp.int32) * jnp.arange(slot_count, dtype=jnp.int32)[None, :], axis=1
    )
    send_q = jnp.take(query_rot.reshape(slot_count, slot_rows, col_count), slot_pick, axis=0)
    send_var = jnp.take(slot_var, slot_pick, axis=0).astype(jnp.bfloat16)
    my_block = lax.dynamic_slice_in_dim(block_perm, blk_index, 1)[0]
    my_query = my_block // blocks_each
    first_row = my_block % blocks_each * cache_count
    my_len = lax.dynamic_slice_in_dim(query_len, my_query, 1)[0]
    row_valid = first_row + jnp.arange(cache_count, dtype=jnp.int32) < my_len
    cache_keys = cache_k.reshape(cache_count, head_count, DH)
    cache_values = cache_v.reshape(cache_count, head_count, DH)
    recv_q, recv_var = (
        lax.all_to_all(send_q, "blk", split_axis=0, concat_axis=0, tiled=True),
        lax.all_to_all(send_var, "blk", split_axis=0, concat_axis=0, tiled=True),
    )
    maxima, totals, sums = cache_part(
        recv_q, recv_var, cache_keys, cache_values, cache_var, row_valid, bias_same, bias_other
    )
    got_max, got_total, got_sum = (
        lax.all_to_all(maxima, "blk", split_axis=0, concat_axis=0, tiled=True),
        lax.all_to_all(totals, "blk", split_axis=0, concat_axis=0, tiled=True),
        lax.all_to_all(sums, "blk", split_axis=0, concat_axis=0, tiled=True),
    )
    match_float = slot_match.astype(jnp.float32)
    spread_max = jnp.where(slot_match[:, :, None, None], got_max[:, None], -1e30)
    cache_peak = jnp.max(spread_max, axis=0)
    peak = jnp.maximum(cache_peak, self_peak)
    device_peak = jnp.take(peak, slot_pick, axis=0)
    factor = jnp.exp(got_max - device_peak)
    cache_total = jnp.einsum(
        "dg,dth->gth", match_float, got_total * factor, precision=lax.Precision.HIGHEST
    )
    scaled_sum = got_sum.reshape(blk_count, slot_rows, head_count, DH) * factor[..., None]
    cache_sum = jnp.einsum(
        "dg,dthe->gthe", match_float, scaled_sum, precision=lax.Precision.HIGHEST
    )
    self_factor = jnp.exp(self_peak - peak)
    numerator = cache_sum + self_sum * self_factor[..., None]
    denominator = cache_total + self_total * self_factor
    attended = (
        (numerator / denominator[..., None]).reshape(row_count, col_count).astype(jnp.bfloat16)
    )
    partial_update = jnp.dot(attended, w_out, preferred_element_type=jnp.float32)
    x_float = doc_x.astype(jnp.float32)
    whole_sum = lax.psum(partial_update, "head")
    hidden = x_float + whole_sum
    square_sum = jnp.sum(hidden * hidden, axis=1)
    weighted = jnp.sum(hidden * norm_gain * readout, axis=1)
    update = lax.dynamic_slice_in_dim(whole_sum, head_index * col_count, col_count, 1)
    token_score = weighted * lax.rsqrt(square_sum / D + 1e-06)
    pooled_sum = jnp.dot(token_score, member.astype(jnp.float32), precision=lax.Precision.HIGHEST)
    return (update, pooled_sum / lengths.astype(jnp.float32))


def solution(mesh):
    return jax.shard_map(
        body,
        mesh=mesh,
        in_specs=(
            P("blk", None),
            P("blk"),
            P(),
            P("blk"),
            P(),
            P(),
            P("blk", "head"),
            P("blk", "head"),
            P("blk"),
            P(None, "head"),
            P(None, "head"),
            P(None, "head"),
            P("head", None),
            P(None, "head"),
            P(),
            P(),
        ),
        out_specs=(P("blk", "head"), P("blk")),
        check_vma=False,
    )
```

profile of v0, /device:TPU:0, one launch (start us, length us, event | category | flops | bytes accessed | tf_op | source)
XLA Modules:
  0.0 253.8 jit_solution(5256641520441733673)
XLA Ops:
  7.2 0.8 dynamic_slice.20
  8.2 0.7 select_reduce_fusion.2
  9.0 1.2 gather_fusion.1
  10.9 6.3 %all-to-all-start.1 = ((bf16[8,1,128]{2,1,0:T(2,128)(2,1)}), bf16[8,1,128]{2,1,0:T(2,128)(2,1)S(1)}, u32[]{:S(2)}, u32[]{:S(2)}) async-start(bf16[8,1,128]{2,1,0:T(2,128)(2,1)} %copy.100), calls=%async_computation.1 | async-start | bytes 8192 | tf_op jit(solution)/shard_map/all_to_all | solution.py:165
  17.2 0.7 select_reduce_fusion.1
  19.9 2.6 %fusion.55 = f32[1024,256]{0,1:T(8,128)S(1)} fusion(bf16[1024,1024]{1,0:T(8,128)(2,1)} %param.18, bf16[1024,256]{1,0:T(8,128)(2,1)} %param.27), kind=kOutput, calls=%fused_computation.114 | convolution fusion | flops 536870912 | bytes 3670016 | tf_op jit(solution)/shard_map/dot_general | solution.py:121
  23.5 1.1 copy.97
  24.6 1.6 gather_fusion
  26.2 2.8 %fusion.56 = f32[1024,256]{0,1:T(8,128)} fusion(bf16[1024,1024]{1,0:T(8,128)(2,1)S(1)} %copy-done.1, bf16[1024,256]{1,0:T(8,128)(2,1)} %param.28), kind=kOutput, calls=%fused_computation.115 | convolution fusion | flops 536870912 | bytes 3670016 | tf_op jit(solution)/shard_map/dot_general | solution.py:123
  29.0 0.9 broadcast_select_fusion
  29.9 5.1 %all-to-all-start = ((bf16[8,128,256]{2,1,0:T(8,128)(2,1)}), bf16[8,128,256]{2,1,0:T(8,128)(2,1)S(1)}, u32[]{:S(2)}, u32[]{:S(2)}) async-start(bf16[8,128,256]{2,1,0:T(8,128)(2,1)} %broadcast_select_fusion), calls=%async_computation | async-start | bytes 1048576 | tf_op jit(solution)/shard_map/all_to_all | solution.py:164
  38.5 1.8 copy.99
  40.3 1.8 copy.101
  42.3 2.2 subtract_convert_fusion
  44.5 2.5 %convolution_convert_fusion = bf16[1024,256]{1,0:T(8,128)(2,1)} fusion(bf16[1024,1024]{1,0:T(8,128)(2,1)S(1)} %copy-done.1, bf16[1024,256]{1,0:T(8,128)(2,1)} %param.29), kind=kOutput, calls=%fused_computation.33 | convolution fusion | flops 537133056 | bytes 3145728 | tf_op jit(solution)/shard_map/dot_general | solution.py:126
  47.6 2.8 %all-to-all-done = bf16[8,128,256]{2,1,0:T(8,128)(2,1)S(1)} async-done(((bf16[8,128,256]{2,1,0:T(8,128)(2,1)}), bf16[8,128,256]{2,1,0:T(8,128)(2,1)S(1)}, u32[]{:S(2)}, u32[]{:S(2)}) %all-to-all-start) | async-done | bytes 524320 | tf_op jit(solution)/shard_map/all_to_all | solution.py:164
  50.4 1.4 reshape.307
  51.8 2.3 copy.102
  54.0 25.6 %while.15 = (s32[]{:T(128)}, f32[2,512,4]{1,2,0:T(4,128)}, f32[2,512,4]{1,2,0:T(4,128)}, f32[2,512,256]{2,1,0:T(8,128)}, bf16[2,512,4,64]{1,3,2,0:T(8,128)(2,1)}...) while((s32[]{:T(128)}, f32[2,512,4]{1,2,0:T(4,128)}, ...), condition=%wide.region_7.8_spmd.clone, body=%wide.region_4.7_spmd.clone.sunk | while | flops 288616960 | bytes 18164980 | solution.py:68
  55.4 0.9 broadcast_compare_fusion.5
  56.3 2.6 %fusion.79 = (f32[4,512]{1,0:T(4,128)S(1)}, f32[4,512,512]{1,2,0:T(8,128)S(1)}) fusion(f32[4]{0:T(128)} %bitcast.137, f32[4]{0:T(128)} %bitcast.138, pred[512]{0:T(512)(128)(4,1)S(1)} %iota_compare_fusion.7, pred[512,512]{0,1:T(8,128)(4,1)S(1)} %broadcast_compare_fusion.5, bf16[512,4,64]{0,2,1:T(8,128)(2,1)} %get-tuple-element.302, ...), kind=kOutput, calls=%fused_computation.8.clone.1 | convolution fusion | flops 139458560 | bytes 4990468 | tf_op jit(solution)/shard_map/while/body/eval_jaxpr/thd,rhd->htr/dot_general | solution.py:55
  58.9 2.1 fusion.80
  61.0 3.1 %fusion.81 = f32[4,512,64]{1,2,0:T(8,128)} fusion(bf16[512,4,64]{0,2,1:T(8,128)(2,1)S(1)} %copy-done.7, f32[4,512,512]{1,2,0:T(8,128)S(1)} %get-tuple-element.267, f32[4,512]{1,0:T(4,128)S(1)} %get-tuple-element.268, f32[4]{0:T(128)} %bitcast.137, f32[4]{0:T(128)} %bitcast.138, pred[512]{0:T(512)(128)(4,1)S(1)} %iota_compare_fusion.7, ...), kind=kOutput, calls=%fused_computation.9.clone.1 | convolution fusion | flops 141557760 | bytes 5251616 | tf_op jit(solution)/shard_map/while/body/eval_jaxpr/htr,rhd->thd/dot_general | solution.py:63
  64.2 1.2 copy.162
  66.0 0.8 constant_dynamic-update-slice_fusion.2
  68.2 0.9 broadcast_compare_fusion.5
  69.1 2.6 %fusion.79 = (f32[4,512]{1,0:T(4,128)S(1)}, f32[4,512,512]{1,2,0:T(8,128)S(1)}) fusion(f32[4]{0:T(128)} %bitcast.137, f32[4]{0:T(128)} %bitcast.138, pred[512]{0:T(512)(128)(4,1)S(1)} %iota_compare_fusion.7, pred[512,512]{0,1:T(8,128)(4,1)S(1)} %broadcast_compare_fusion.5, bf16[512,4,64]{0,2,1:T(8,128)(2,1)} %get-tuple-element.302, ...), kind=kOutput, calls=%fused_computation.8.clone.1 | convolution fusion | flops 139458560 | bytes 4990468 | tf_op jit(solution)/shard_map/while/body/eval_jaxpr/thd,rhd->htr/dot_general | solution.py:55
  71.7 2.1 fusion.80
  73.8 3.1 %fusion.81 = f32[4,512,64]{1,2,0:T(8,128)} fusion(bf16[512,4,64]{0,2,1:T(8,128)(2,1)S(1)} %copy-done.7, f32[4,512,512]{1,2,0:T(8,128)S(1)} %get-tuple-element.267, f32[4,512]{1,0:T(4,128)S(1)} %get-tuple-element.268, f32[4]{0:T(128)} %bitcast.137, f32[4]{0:T(128)} %bitcast.138, pred[512]{0:T(512)(128)(4,1)S(1)} %iota_compare_fusion.7, ...), kind=kOutput, calls=%fused_computation.9.clone.1 | convolution fusion | flops 141557760 | bytes 5251616 | tf_op jit(solution)/shard_map/while/body/eval_jaxpr/htr,rhd->thd/dot_general | solution.py:63
  76.9 1.2 copy.162
  78.8 0.8 constant_dynamic-update-slice_fusion.2
  79.6 3.3 %all-to-all-start.3 = ((f32[8,128,4]{1,2,0:T(4,128)}), f32[8,128,4]{1,2,0:T(4,128)S(1)}, u32[]{:S(2)}, u32[]{:S(2)}) async-start(f32[8,128,4]{1,2,0:T(4,128)} %bitcast.155), calls=%async_computation.3 | async-start | bytes 32768 | tf_op jit(solution)/shard_map/all_to_all | solution.py:171
  83.6 4.9 %all-to-all-done.3 = f32[8,128,4]{1,2,0:T(4,128)S(1)} async-done(((f32[8,128,4]{1,2,0:T(4,128)}), f32[8,128,4]{1,2,0:T(4,128)S(1)}, u32[]{:S(2)}, u32[]{:S(2)}) %all-to-all-start.3) | async-done | bytes 16416 | tf_op jit(solution)/shard_map/all_to_all | solution.py:171
  88.5 3.3 %all-to-all-start.4 = ((f32[8,128,4]{1,2,0:T(4,128)}), f32[8,128,4]{1,2,0:T(4,128)S(1)}, u32[]{:S(2)}, u32[]{:S(2)}) async-start(f32[8,128,4]{1,2,0:T(4,128)} %bitcast.154), calls=%async_computation.4 | async-start | bytes 32768 | tf_op jit(solution)/shard_map/all_to_all | solution.py:172
  91.8 0.7 broadcast_compare_fusion.3
  92.7 2.8 %reshape.308 = bf16[8,128,4,64]{3,2,1,0:T(4,128)(2,1)} reshape(bf16[1024,256]{1,0:T(8,128)(2,1)} %convolution_convert_fusion) | data formatting | bytes 1048576 | tf_op jit(solution)/shard_map/reshape | solution.py:131
  95.4 2.0 all-to-all-done.4
  97.4 4.2 %all-to-all-start.2 = ((f32[8,128,256]{2,1,0:T(8,128)}), f32[8,128,256]{2,1,0:T(8,128)}, u32[]{:S(2)}, u32[]{:S(2)}) async-start(f32[8,128,256]{2,1,0:T(8,128)} %bitcast.148), calls=%async_computation.2 | async-start | bytes 2097152 | tf_op jit(solution)/shard_map/all_to_all | solution.py:173
  102.1 2.0 fusion.53
  104.7 1.5 fusion.19
  107.3 21.0 %all-to-all-done.2 = f32[8,128,256]{2,1,0:T(8,128)} async-done(((f32[8,128,256]{2,1,0:T(8,128)}), f32[8,128,256]{2,1,0:T(8,128)}, u32[]{:S(2)}, u32[]{:S(2)}) %all-to-all-start.2) | async-done | bytes 1048608 | tf_op jit(solution)/shard_map/all_to_all | solution.py:173
  128.3 2.5 copy.104
  130.8 1.3 broadcast_multiply_fusion
  132.1 2.9 %fusion.17 = bf16[8,128,4,64]{1,0,3,2:T(8,128)(2,1)S(1)} fusion(f32[8,4,64,128]{3,2,1,0:T(8,128)} %fusion.19, f32[8,128,4,64]{1,3,2,0:T(8,128)S(1)} %broadcast_multiply_fusion, f32[8,128,4]{1,0,2:T(8,128)S(1)} %convolution_add_fusion.1, f32[8,128,4]{1,0,2:T(8,128)S(1)} %get-tuple-element.180, s32[8]{0:T(128)S(1)} %copy-done.18, s32[8]{0:T(128)S(1)} %copy-done.14), kind=kOutput, calls=%fused_computation.32 | convolution fusion | flops 26214464 | bytes 2654272 | tf_op jit(solution)/shard_map/dg,dthe->gthe/dot_general | solution.py:185
  135.1 2.7 %fusion.26 = f32[1024,1024]{1,0:T(8,128)} fusion(bf16[256,1024]{1,0:T(8,128)(2,1)S(1)} %copy-done, bf16[32,8,8,128]{3,2,1,0:T(8,128)(2,1)S(1)} %bitcast.147), kind=kOutput, calls=%fused_computation.45 | convolution fusion | flops 536870912 | bytes 5242880 | tf_op jit(solution)/shard_map/dot_general | solution.py:194
  137.8 102.9 %all-reduce.2.cloned.1.call-done = f32[1024,1024]{1,0:T(8,128)} async-done(((f32[1024,1024]{1,0:T(8,128)}), f32[1024,1024]{1,0:T(8,128)}) %all-reduce.2.cloned.1.call-update) | async-done | bytes 4194320 | tf_op jit(solution)/shard_map/psum | solution.py:196
  240.7 3.3 %multiply_reduce_fusion = (f32[1024]{0:T(1024)S(1)}, f32[1024]{0:T(1024)S(1)}) fusion(f32[1024,1024]{1,0:T(8,128)} %all-reduce.2.cloned.1.call-done, bf16[1024,1024]{1,0:T(8,128)(2,1)S(1)} %copy-done.1, f32[1024]{0:T(1024)S(1)} %copy-done.15, f32[1024]{0:T(1024)S(1)} %copy-done.16), kind=kLoop, calls=%fused_computation.23 | loop fusion | flops 7337984 | bytes 6307840 | tf_op jit(solution)/shard_map/reduce_sum | solution.py:198
  244.7 2.3 constant_dynamic-slice_fusion.1
  (98 shorter events, 13.8 us)
Async XLA Ops:
  7.2 127.9 %copy-start = (bf16[256,1024]{1,0:T(8,128)(2,1)S(1)}, bf16[256,1024]{1,0:T(8,128)(2,1)}, u32[]{:S(2)}) copy-start(bf16[256,1024]{1,0:T(8,128)(2,1)} %param.30) | copy-start | bytes 1572868
  8.2 0.8 copy-start.13
  8.9 20.1 %copy-start.11 = (pred[8]{0:T(512)(128)(4,1)}, pred[8]{0:T(512)(128)(4,1)S(1)}, u32[]{:S(2)}) copy-start(pred[8]{0:T(512)(128)(4,1)S(1)} %compare_and_fusion) | copy-start | bytes 28
  9.0 15.6 %copy-start.10 = (s32[1024]{0:T(1024)}, s32[1024]{0:T(1024)S(1)}, u32[]{:S(2)}) copy-start(s32[1024]{0:T(1024)S(1)} %pad_clamp_fusion) | copy-start | bytes 12292
  10.9 19.0 %all-to-all-start.1 = ((bf16[8,1,128]{2,1,0:T(2,128)(2,1)}), bf16[8,1,128]{2,1,0:T(2,128)(2,1)S(1)}, u32[]{:S(2)}, u32[]{:S(2)}) async-start(bf16[8,1,128]{2,1,0:T(2,128)(2,1)} %copy.100), calls=%async_computation.1 | async-start | bytes 8192 | tf_op jit(solution)/shard_map/all_to_all | solution.py:165
  18.7 0.7 copy-start.8
  18.8 3.9 %copy-start.19 = (s32[16]{0:T(128)}, s32[16]{0:T(128)S(1)}, u32[]{:S(2)}) copy-start(s32[16]{0:T(128)S(1)} %convert_reduce_fusion) | copy-start | bytes 196
  19.9 6.3 %copy-start.1 = (bf16[1024,1024]{1,0:T(8,128)(2,1)S(1)}, bf16[1024,1024]{1,0:T(8,128)(2,1)}, u32[]{:S(2)}) copy-start(bf16[1024,1024]{1,0:T(8,128)(2,1)} %param.18) | copy-start | bytes 6291460
  22.7 0.7 copy-start.3
  22.7 0.8 copy-start.5
  23.5 11.6 %copy-start.21 = (f32[2,4]{1,0:T(2,128)S(1)}, f32[2,4]{1,0:T(2,128)}, u32[]{:S(2)}) copy-start(f32[2,4]{1,0:T(2,128)} %param.31) | copy-start | bytes 100
  23.5 12.2 %copy-start.17 = (s32[8]{0:T(128)S(1)}, s32[8]{0:T(128)}, u32[]{:S(2)}) copy-start(s32[8]{0:T(128)} %param.23) | copy-start | bytes 100
  23.5 14.4 %copy-start.22 = (s32[8]{0:T(128)S(1)}, s32[8]{0:T(128)}, u32[]{:S(2)}) copy-start(s32[8]{0:T(128)} %param.22) | copy-start | bytes 100
  24.6 17.5 %copy-start.6 = (s32[1024]{0:T(1024)S(1)}, s32[1024]{0:T(1024)}, u32[]{:S(2)}) copy-start(s32[1024]{0:T(1024)} %param.21) | copy-start | bytes 12292
  29.9 20.5 %all-to-all-start = ((bf16[8,128,256]{2,1,0:T(8,128)(2,1)}), bf16[8,128,256]{2,1,0:T(8,128)(2,1)S(1)}, u32[]{:S(2)}, u32[]{:S(2)}) async-start(bf16[8,128,256]{2,1,0:T(8,128)(2,1)} %broadcast_select_fusion), calls=%async_computation | async-start | bytes 1048576 | tf_op jit(solution)/shard_map/all_to_all | solution.py:164
  54.0 48.1 %copy-start.4 = (bf16[1024,4,32]{0,2,1:T(8,128)(2,1)S(1)}, bf16[1024,4,32]{0,2,1:T(8,128)(2,1)}, u32[]{:S(2)}) copy-start(bf16[1024,4,32]{0,2,1:T(8,128)(2,1)} %copy-done.3) | copy-start | bytes 786436
  56.3 4.7 %copy-start.7 = (bf16[512,4,64]{0,2,1:T(8,128)(2,1)S(1)}, bf16[512,4,64]{0,2,1:T(8,128)(2,1)}, u32[]{:S(2)}) copy-start(bf16[512,4,64]{0,2,1:T(8,128)(2,1)} %get-tuple-element.307) | copy-start | bytes 786436 | tf_op jit(solution)/shard_map/while
  69.1 4.7 %copy-start.7 = (bf16[512,4,64]{0,2,1:T(8,128)(2,1)S(1)}, bf16[512,4,64]{0,2,1:T(8,128)(2,1)}, u32[]{:S(2)}) copy-start(bf16[512,4,64]{0,2,1:T(8,128)(2,1)} %get-tuple-element.307) | copy-start | bytes 786436 | tf_op jit(solution)/shard_map/while
  79.6 8.9 %all-to-all-start.3 = ((f32[8,128,4]{1,2,0:T(4,128)}), f32[8,128,4]{1,2,0:T(4,128)S(1)}, u32[]{:S(2)}, u32[]{:S(2)}) async-start(f32[8,128,4]{1,2,0:T(4,128)} %bitcast.155), calls=%async_computation.3 | async-start | bytes 32768 | tf_op jit(solution)/shard_map/all_to_all | solution.py:171
  88.5 8.9 %all-to-all-start.4 = ((f32[8,128,4]{1,2,0:T(4,128)}), f32[8,128,4]{1,2,0:T(4,128)S(1)}, u32[]{:S(2)}, u32[]{:S(2)}) async-start(f32[8,128,4]{1,2,0:T(4,128)} %bitcast.154), calls=%async_computation.4 | async-start | bytes 32768 | tf_op jit(solution)/shard_map/all_to_all | solution.py:172
  97.4 30.8 %all-to-all-start.2 = ((f32[8,128,256]{2,1,0:T(8,128)}), f32[8,128,256]{2,1,0:T(8,128)}, u32[]{:S(2)}, u32[]{:S(2)}) async-start(f32[8,128,256]{2,1,0:T(8,128)} %bitcast.148), calls=%async_computation.2 | async-start | bytes 2097152 | tf_op jit(solution)/shard_map/all_to_all | solution.py:173
  101.7 139.0 %all-reduce.2.cloned.1.call-start = ((), (), s32[]{:S(2)}) async-start(), calls=%async_computation.5 | async-start | bytes 8388608 | tf_op jit(solution)/shard_map/psum | solution.py:196
  102.1 2.5 copy-start.2
  104.1 2.8 %copy-start.12 = (pred[8]{0:T(512)(128)(4,1)S(1)}, pred[8]{0:T(512)(128)(4,1)}, u32[]{:S(2)}) copy-start(pred[8]{0:T(512)(128)(4,1)} %copy-done.11) | copy-start | bytes 28
  104.2 2.9 %copy-start.14 = (s32[8]{0:T(128)S(1)}, s32[8]{0:T(128)}, u32[]{:S(2)}) copy-start(s32[8]{0:T(128)} %copy-done.13) | copy-start | bytes 100
  104.2 2.9 %copy-start.18 = (s32[8]{0:T(128)S(1)}, s32[8]{0:T(128)}, u32[]{:S(2)}) copy-start(s32[8]{0:T(128)} %param.23) | copy-start | bytes 100
  137.8 102.9 %copy-start.15 = (f32[1024]{0:T(1024)S(1)}, f32[1024]{0:T(1024)}, u32[]{:S(2)}) copy-start(f32[1024]{0:T(1024)} %param.33) | copy-start | bytes 12292
  137.8 102.9 %copy-start.16 = (f32[1024]{0:T(1024)S(1)}, f32[1024]{0:T(1024)}, u32[]{:S(2)}) copy-start(f32[1024]{0:T(1024)} %param.32) | copy-start | bytes 12292
  137.8 106.2 %copy-start.9 = (s32[1024]{0:T(1024)S(1)}, s32[1024]{0:T(1024)}, u32[]{:S(2)}) copy-start(s32[1024]{0:T(1024)} %copy-done.8) | copy-start | bytes 12292
  137.8 106.2 %copy-start.20 = (s32[16]{0:T(128)S(1)}, s32[16]{0:T(128)}, u32[]{:S(2)}) copy-start(s32[16]{0:T(128)} %copy-done.19) | copy-start | bytes 196
Sparse Core Ops, SparseCore 0:
  137.9 102.7 all-reduce.1
where the time goes:
time: 255 us; the launch traced here: 254 us
  waiting for transfers between devices  134 us (53%)
  local copies, waits for them, and re-layouts  31.1 us (12%)
  matrix products  29.7 us (12%)
  starting transfers between devices  22.5 us (9%)
  other arithmetic  20.8 us (8%)
  between operations  16.1 us (6%)
    psum x1, waiting for transfers between devices, body(): whole_sum = lax.psum(partial_update, 'head')  103 us
    all_to_all x1, waiting for transfers between devices, body(): lax.all_to_all(sums, 'blk', split_axis=0, concat_axis=0, tiled=True)  21 us
    unnamed x48, local copies, waits for them, and re-layouts  6.67 us
    all_to_all x1, starting transfers between devices, body(): lax.all_to_all(send_var, 'blk', split_axis=0, concat_axis=0, tiled=True)  6.33 us
    dot_general x2, matrix products, one_block(): jnp.einsum('htr,rhd->thd', weights, cache_values, preferred_element_type=...  6.23 us
    dynamic_update_slice x6, local copies, waits for them, and re-layouts, cache_part(): maxima, totals, sums = lax.map(one_block, (flat_q, flat_var))  5.35 us
    dot_general x2, matrix products, one_block(): jnp.einsum('thd,rhd->htr', block_q, cache_keys, preferred_element_type=jn...  5.15 us
  transfers between devices with their start and end apart: 6, of which 5 were waited for; matrix products, arithmetic and copies ran while one was open for 13% of the time, Pallas kernels for 0%

commit v1 on v0

v1 whole, which is shorter than its diff:
```python
import functools

import jax
import jax.numpy as jnp
import numpy as np
from jax import lax
from jax.experimental import pallas as pl
from jax.experimental.pallas import tpu as pltpu
from jax.sharding import PartitionSpec as P

DH = 64
QUERIES = 8
LANES = 128
EXTRA = 16
NEVER = -1e30
BF = jnp.bfloat16
F32 = jnp.float32
VMEM = pl.BlockSpec(memory_space=pltpu.VMEM)
SMEM = pl.BlockSpec(memory_space=pltpu.SMEM)
LIMIT = 32 * 1024 * 1024


def offset_tables(slot_rows):
    half = DH // 2
    freq = (10000.0 ** (-np.arange(half, dtype=np.float64) / half)).astype(np.float32)
    lane_freq = np.tile(freq, LANES // half)
    angles = np.arange(slot_rows, dtype=np.float64)[:, None] * lane_freq[None, :].astype(np.float64)
    sign = np.where(np.arange(LANES) % DH < half, -1.0, 1.0).astype(np.float32)
    rows = np.zeros((8, LANES), np.float32)
    rows[0] = lane_freq
    rows[1] = sign
    return np.cos(angles).astype(np.float32), np.sin(angles).astype(np.float32), rows


def dot(a, b):
    return jnp.dot(a, b, preferred_element_type=F32)


def dot_t(a, b):
    return lax.dot_general(a, b, (((1,), (1,)), ((), ())), preferred_element_type=F32)


def slot_of(p, doc_query, block_perm, slots, bpq):
    blk = lax.axis_index("blk")
    wanted = block_perm[blk ^ p] // bpq
    slot = jnp.int32(0)
    for j in range(slots):
        slot = slot + jnp.where(doc_query[blk * 2 * slots + 2 * j] == wanted, j, 0)
    return slot


def start_tables(doc_query, query_len, seg_ref, rows_ref, base_ref):
    slots, width = seg_ref.shape
    blk = lax.axis_index("blk")
    row = lax.broadcasted_iota(jnp.int32, (slots, width), 0)
    length = jnp.zeros((slots, width), F32)
    for j in range(slots):
        value = query_len[doc_query[blk * 2 * slots + 2 * j]].astype(F32)
        length = jnp.where(row == j, value, length)
    second = (seg_ref[...] & 1).astype(F32)
    count = width - jnp.sum(second, axis=1, keepdims=True)
    count = jnp.broadcast_to(count, (slots, width))
    freq = rows_ref[0:1, :]
    one, two = length * freq, (length - count) * freq
    base_ref[0] = jnp.cos(one)
    base_ref[1] = jnp.sin(one)
    base_ref[2] = jnp.cos(two)
    base_ref[3] = jnp.sin(two)
    base_ref[4] = count


def slot_tables(slot, base_ref, cos_ref, sin_ref, rows_ref):
    shape = cos_ref.shape
    rows = [base_ref[i, pl.ds(slot, 1), :] for i in range(5)]
    token = lax.broadcasted_iota(jnp.int32, shape, 0).astype(F32)
    first = token < rows[4]
    base_cos = jnp.where(first, rows[0], rows[2])
    base_sin = jnp.where(first, rows[1], rows[3])
    off_cos, off_sin = cos_ref[...], sin_ref[...]
    cos = base_cos * off_cos - base_sin * off_sin
    sin = (base_sin * off_cos + base_cos * off_sin) * rows_ref[1:2, :]
    return cos, sin


def turn(value, cos, sin):
    lane = lax.broadcasted_iota(jnp.int32, cos.shape, 1)
    low = lane % DH < DH // 2
    parts = []
    for at in range(0, value.shape[1], LANES):
        part = value[:, at : at + LANES]
        other = jnp.where(
            low, pltpu.roll(part, LANES - DH // 2, 1), pltpu.roll(part, DH // 2, 1)
        )
        parts.append(part * cos + other * sin)
    return jnp.concatenate(parts, axis=1)


def query_kernel(
    bpq, doc_query, query_len, block_perm, x_ref, w_ref, seg_ref, var_ref, cos_ref, sin_ref,
    rows_ref, *refs
):
    pick_ref, base_ref, y_ref = refs[0], refs[-2], refs[-1]
    q_refs = refs[1:-2]
    slots, width = seg_ref.shape
    start_tables(doc_query, query_len, seg_ref, rows_ref, base_ref)
    y_ref[...] = dot(x_ref[...], w_ref[...])
    for k, q_ref in enumerate(q_refs):
        for j in range(2):
            slot = slot_of(2 * k + j, doc_query, block_perm, slots, bpq)
            pick_ref[2 * k + j] = slot
            cos, sin = slot_tables(slot, base_ref, cos_ref, sin_ref, rows_ref)
            at = pl.ds(pl.multiple_of(slot * width, width), width)
            turned = turn(y_ref[at, :], cos, sin)
            q_ref[j * width : (j + 1) * width, :] = (turned * 0.125).astype(BF)
            var = var_ref[pl.ds(slot, 1), :].astype(F32)
            q_ref[2 * width :, j * width : (j + 1) * width] = jnp.broadcast_to(
                var, (EXTRA, width)
            ).astype(BF)


def pack_kernel(k_ref, v_ref, var_ref, out_ref):
    rows, cols = k_ref.shape
    out_ref[0:rows, :] = k_ref[...]
    for i in range(rows // cols):
        block = v_ref[i * cols : (i + 1) * cols, :].astype(F32)
        out_ref[rows + i * cols : rows + (i + 1) * cols, :] = block.T.astype(BF)
    parts = rows // LANES
    var = var_ref[...].astype(F32)
    var = jnp.concatenate([var, jnp.zeros((EXTRA - parts, LANES), F32)], axis=0)
    out_ref[2 * rows :, :] = jnp.concatenate([var, var], axis=1).astype(BF)


def by_head(query):
    lane = lax.broadcasted_iota(jnp.int32, query.shape, 1) // DH
    heads = query.shape[1] // DH
    return jnp.concatenate(
        [jnp.where(lane == h, query, jnp.zeros_like(query)) for h in range(heads)], axis=0
    )


def attend(scores, same, allowed, bias_ref, values, out_ref, at):
    width = same.shape[1]
    stats = []
    for h in range(scores.shape[1] // width):
        part = scores[:, h * width : (h + 1) * width]
        part = part + jnp.where(same, bias_ref[0, h], bias_ref[1, h])
        part = jnp.where(allowed, part, NEVER)
        peak = jnp.max(part, axis=0, keepdims=True)
        weight = jnp.exp(part - peak)
        total = jnp.sum(weight, axis=0, keepdims=True)
        weight = weight.astype(BF)
        mixed = None
        key = 0
        for value in values:
            keys = value.shape[1]
            term = dot(value[h * DH : (h + 1) * DH, :], weight[key : key + keys, :])
            mixed = term if mixed is None else mixed + term
            key += keys
        mixed = mixed * (1.0 / total)
        out_ref[h * DH : (h + 1) * DH, at] = mixed.astype(out_ref.dtype)
        stats.append(peak + jnp.log(total))
    return stats


def cache_kernel(bpq, query_len, block_perm, bias_ref, q_ref, own_ref, other_ref, out_ref):
    blk = lax.axis_index("blk")
    width = q_ref.shape[0] // 2 - EXTRA // 2
    cols = q_ref.shape[1]
    rows = (own_ref.shape[0] - EXTRA) // 2
    for j, ref in enumerate((own_ref, other_ref)):
        block = block_perm[blk ^ j]
        usable = query_len[block // bpq] - block % bpq * rows
        var = ref[2 * rows :, 0:LANES].astype(F32)
        var = jnp.concatenate([var, jnp.zeros((LANES - EXTRA, LANES), F32)], axis=0).T
        key_var = jnp.concatenate(
            [jnp.broadcast_to(var[:, i : i + 1], (LANES, width)) for i in range(rows // LANES)],
            axis=0,
        )
        tok_var = q_ref[2 * width :, j * width : (j + 1) * width].astype(F32)[0:1, :]
        same = key_var == tok_var
        allowed = lax.broadcasted_iota(jnp.int32, (rows, width), 0) < usable
        scores = dot_t(ref[0:rows, :], by_head(q_ref[j * width : (j + 1) * width, :]))
        values = [ref[rows + i * cols : rows + (i + 1) * cols, :] for i in range(rows // cols)]
        at = slice(j * width, (j + 1) * width)
        stats = attend(scores, same, allowed, bias_ref, values, out_ref, at)
        full = jnp.concatenate(stats, axis=0)
        high = full.astype(BF).astype(F32)
        middle = (full - high).astype(BF).astype(F32)
        low = full - high - middle
        pad = jnp.zeros((EXTRA - 3 * len(stats), width), F32)
        out_ref[cols:, at] = jnp.concatenate([high, middle, low, pad], axis=0).astype(BF)


def own_kernel(
    doc_query, query_len, bias_ref, home_ref, x_ref, wk_ref, wv_ref, seg_ref, var_ref, cos_ref,
    sin_ref, rows_ref, *refs
):
    out_ref, base_ref, k_ref, v_ref = refs[-4:]
    q_refs = refs[:-4]
    slots, width = seg_ref.shape
    cols = wk_ref.shape[1]
    start_tables(doc_query, query_len, seg_ref, rows_ref, base_ref)
    k_ref[...] = dot(x_ref[...], wk_ref[...])
    v_ref[...] = dot(x_ref[...], wv_ref[...])
    for n in range(slots):
        slot = home_ref[n]
        cos, sin = slot_tables(slot, base_ref, cos_ref, sin_ref, rows_ref)
        at = pl.ds(pl.multiple_of(slot * width, width), width)
        key = turn(k_ref[at, :], cos, sin).astype(BF)
        value = v_ref[at, :].T.astype(BF)
        query = q_refs[n // 2][n % 2 * width : (n % 2 + 1) * width, :]
        scores = dot_t(key, by_head(query))
        var = jnp.broadcast_to(var_ref[pl.ds(slot, 1), :].astype(F32), (width, width))
        same = var.T == var
        count = base_ref[4, pl.ds(slot, 1), :]
        key_second = lax.broadcasted_iota(jnp.int32, (width, width), 0).astype(F32) >= count
        tok_second = lax.broadcasted_iota(jnp.int32, (width, width), 1).astype(F32) >= count
        allowed = jnp.logical_not(jnp.logical_xor(key_second, tok_second))
        part_ref = out_ref.at[n]
        stats = attend(scores, same, allowed, bias_ref, [value], part_ref, slice(None))
        stats = jnp.concatenate(stats + [jnp.zeros((8 - len(stats), width), F32)], axis=0)
        part_ref[cols:, :] = stats


def merge_kernel(first, got_ref, own_ref, out_ref):
    cols = got_ref.shape[0] - EXTRA
    heads = cols // DH
    width = got_ref.shape[1] // 2
    for j in range(2):
        at = slice(j * width, (j + 1) * width)
        stats = got_ref[cols:, at].astype(F32)
        there = stats[0:heads] + stats[heads : 2 * heads] + stats[2 * heads : 3 * heads]
        here = own_ref[first + j, cols : cols + heads, :]
        peak = jnp.maximum(there, here)
        there, here = jnp.exp(there - peak), jnp.exp(here - peak)
        inverse = 1.0 / (there + here)
        there, here = there * inverse, here * inverse
        parts = []
        for h in range(heads):
            row = slice(h * DH, (h + 1) * DH)
            parts.append(
                got_ref[row, at].astype(F32) * there[h : h + 1]
                + own_ref[first + j, row, :] * here[h : h + 1]
            )
        out_ref[at, :] = jnp.concatenate(parts, axis=0).T.astype(BF)


def output_kernel(head_count, first, home_ref, *refs):
    att_refs, w_refs = refs[:head_count], refs[head_count : 2 * head_count]
    x_ref, seg_ref, gain_ref, read_ref = refs[2 * head_count : 2 * head_count + 4]
    update_ref, pooled_ref, sum_ref = refs[-3:]
    step = pl.program_id(0)
    slot = home_ref[first + step]
    total = dot(att_refs[0][...], w_refs[0][...])
    for att_ref, w_ref in zip(att_refs[1:], w_refs[1:]):
        total = total + dot(att_ref[...], w_ref[...])
    sum_ref[...] = total
    cols = update_ref.shape[1]
    head = lax.axis_index("head")
    update_ref[...] = sum_ref[:, pl.ds(pl.multiple_of(head * cols, cols), cols)]
    hidden = x_ref[...].astype(F32) + total
    square = jnp.sum(hidden * hidden, axis=1, keepdims=True)
    weighted = jnp.sum(hidden * (gain_ref[...] * read_ref[...]), axis=1, keepdims=True)
    score = weighted * lax.rsqrt(square / hidden.shape[1] + 1e-06)
    width = score.shape[0]
    second = (seg_ref[pl.ds(slot, 1), :] & 1).astype(F32)
    count_two = jnp.sum(second, axis=1, keepdims=True)
    count_one = width - count_two
    token = lax.broadcasted_iota(jnp.int32, score.shape, 0).astype(F32)
    is_first = token < count_one
    sum_one = jnp.sum(jnp.where(is_first, score, 0.0), axis=0, keepdims=True)
    sum_two = jnp.sum(jnp.where(is_first, 0.0, score), axis=0, keepdims=True)
    lane = lax.broadcasted_iota(jnp.int32, (1, LANES), 1)
    pooled_ref[0] = jnp.where(lane == 0, sum_one / count_one, sum_two / count_two)


def call(kernel, out, ins, scratch=(), flops=0, bytes_accessed=0, **kwargs):
    return pl.pallas_call(
        kernel,
        out_shape=out,
        in_specs=ins,
        scratch_shapes=list(scratch),
        compiler_params=pltpu.CompilerParams(vmem_limit_bytes=LIMIT),
        cost_estimate=pl.CostEstimate(
            flops=flops, bytes_accessed=bytes_accessed, transcendentals=0
        ),
        **kwargs,
    )


def partner(value, axis, k):
    count = lax.axis_size(axis)
    return lax.ppermute(value, axis, [(i, i ^ k) for i in range(count)])


def spread_merge(backs, own, pick, slots, bpq):
    cols = backs[0].shape[0] - EXTRA
    width = backs[0].shape[1] // 2
    heads = cols // DH
    parts = jnp.stack(backs).reshape(len(backs), cols + EXTRA, 2, width)
    parts = parts.transpose(0, 2, 1, 3).reshape(2 * len(backs), cols + EXTRA, width)
    order = jnp.argsort(pick, stable=True)
    parts = jnp.take(parts, order, axis=0).reshape(slots, bpq, cols + EXTRA, width)
    stats = parts[:, :, cols : cols + 3 * heads].astype(F32)
    stats = stats.reshape(slots, bpq, 3, heads, width).sum(axis=2)
    stats = jnp.concatenate([stats, own[:, None, cols : cols + heads]], axis=1)
    weight = jnp.exp(stats - jnp.max(stats, axis=1, keepdims=True))
    weight = weight / jnp.sum(weight, axis=1, keepdims=True)
    values = jnp.concatenate([parts[:, :, :cols].astype(F32), own[:, None, :cols]], axis=1)
    values = values.reshape(slots, bpq + 1, heads, DH, width)
    mixed = jnp.sum(values * weight[:, :, :, None, :], axis=1).reshape(slots, cols, width)
    mixed = mixed.transpose(0, 2, 1).astype(BF)
    return [mixed[2 * k : 2 * k + 2].reshape(2 * width, cols) for k in range(slots // 2)]


def body(
    doc_x, doc_seg, doc_query, doc_var, query_len, block_perm, cache_k, cache_v, cache_var,
    w_query, w_key, w_value, w_out, var_bias, norm_gain, readout,
):
    rows, depth = doc_x.shape
    cols = w_query.shape[1]
    blocks = lax.axis_size("blk")
    head_count = lax.axis_size("head")
    bpq = blocks // QUERIES
    slots = QUERIES
    width = rows // slots
    chunks = blocks // 2
    cache_rows = cache_k.shape[0]
    seg = doc_seg.reshape(slots, width)
    var = doc_var.reshape(slots, width)
    cos, sin, freq_rows = offset_tables(width)
    sds = jax.ShapeDtypeStruct
    chunk_shape = sds((2 * width + EXTRA, cols), BF)
    base = pltpu.VMEM((5, slots, width), F32)

    w_parts = [w_out] + [partner(w_out, "head", r) for r in range(1, head_count)]

    pick, *queries = call(
        functools.partial(query_kernel, bpq),
        [sds((blocks,), jnp.int32)] + [chunk_shape] * chunks,
        [SMEM] * 3 + [VMEM] * 7,
        [base, pltpu.VMEM((rows, cols), F32)],
        flops=2 * rows * depth * cols,
        bytes_accessed=2 * rows * depth,
        out_specs=[SMEM] + [VMEM] * chunks,
        name="query",
    )(doc_query, query_len, block_perm, doc_x, w_query, seg, var, cos, sin, freq_rows)

    asked = [queries[0]] + [partner(queries[k], "blk", 2 * k) for k in range(1, chunks)]

    packed = call(
        pack_kernel,
        sds((2 * cache_rows + EXTRA, cols), BF),
        [VMEM] * 3,
        bytes_accessed=8 * cache_rows * cols,
        out_specs=VMEM,
        name="pack",
    )(cache_k, cache_v, cache_var.reshape(cache_rows // LANES, LANES))
    packed_other = partner(packed, "blk", 1)

    if bpq == 1:
        home = pick
        home_queries = queries
    else:
        home = jnp.arange(slots, dtype=jnp.int32)
        every = jnp.stack([q[: 2 * width] for q in queries]).reshape(blocks, width, cols)
        every = jnp.take(every, jnp.argsort(pick, stable=True)[::bpq], axis=0)
        home_queries = [
            every[2 * k : 2 * k + 2].reshape(2 * width, cols) for k in range(slots // 2)
        ]

    own = call(
        own_kernel,
        sds((slots, cols + 8, width), F32),
        [SMEM] * 4 + [VMEM] * (8 + len(home_queries)),
        [base, pltpu.VMEM((rows, cols), F32), pltpu.VMEM((rows, cols), F32)],
        flops=6 * rows * depth * cols,
        bytes_accessed=2 * rows * depth,
        out_specs=VMEM,
        name="own_documents",
    )(
        doc_query, query_len, var_bias, home, doc_x, w_key, w_value, seg, var, cos, sin,
        freq_rows, *home_queries,
    )

    def from_cache(query):
        return call(
            functools.partial(cache_kernel, bpq),
            chunk_shape,
            [SMEM] * 3 + [VMEM] * 3,
            flops=16 * width * cache_rows * cols,
            bytes_accessed=8 * cache_rows * cols,
            out_specs=VMEM,
            name="cache_part",
        )(query_len, block_perm, var_bias, query, packed, packed_other)

    parts = [from_cache(query) for query in asked]
    backs = [parts[0]] + [partner(parts[k], "blk", 2 * k) for k in range(1, chunks)]

    if bpq == 1:
        attended = [
            call(
                functools.partial(merge_kernel, 2 * k),
                sds((2 * width, cols), BF),
                [VMEM] * 2,
                bytes_accessed=4 * rows * cols,
                out_specs=VMEM,
                name="merge",
            )(backs[k], own)
            for k in range(chunks)
        ]
    else:
        attended = spread_merge(backs, own, pick, slots, bpq)

    gain, read = norm_gain.reshape(1, depth), readout.reshape(1, depth)
    update = pooled = None
    for k in range(slots // 2):
        atts = [attended[k]] + [partner(attended[k], "head", r) for r in range(1, head_count)]
        chained = [] if update is None else [update, pooled]
        arguments = atts + w_parts + [doc_x, seg, gain, read]
        whole = lambda i, home: (0, 0)
        at_slot = functools.partial(lambda k, i, home: (home[2 * k + i], 0), k)
        update, pooled = pl.pallas_call(
            functools.partial(output_kernel, head_count, 2 * k),
            out_shape=[sds((rows, cols), F32), sds((slots, 1, LANES), F32)],
            grid_spec=pltpu.PrefetchScalarGridSpec(
                num_scalar_prefetch=1,
                grid=(2,),
                in_specs=[pl.BlockSpec((width, cols), lambda i, home: (i, 0))] * head_count
                + [pl.BlockSpec((cols, depth), whole)] * head_count
                + [
                    pl.BlockSpec((width, depth), at_slot),
                    pl.BlockSpec((slots, width), whole),
                    pl.BlockSpec((1, depth), whole),
                    pl.BlockSpec((1, depth), whole),
                ]
                + [pl.BlockSpec(memory_space=pl.ANY)] * len(chained),
                out_specs=[
                    pl.BlockSpec((width, cols), at_slot),
                    pl.BlockSpec(
                        (1, 1, LANES),
                        functools.partial(lambda k, i, home: (home[2 * k + i], 0, 0), k),
                    ),
                ],
                scratch_shapes=[pltpu.VMEM((width, depth), F32)],
            ),
            input_output_aliases=(
                {1 + len(arguments): 0, 2 + len(arguments): 1} if chained else {}
            ),
            compiler_params=pltpu.CompilerParams(vmem_limit_bytes=LIMIT),
            cost_estimate=pl.CostEstimate(
                flops=4 * width * depth * depth,
                bytes_accessed=2 * depth * depth,
                transcendentals=0,
            ),
            name="output",
        )(home, *arguments, *chained)
    return (update, pooled[:, 0, :2].reshape(2 * slots))


def solution(mesh):
    return jax.shard_map(
        body,
        mesh=mesh,
        in_specs=(
            P("blk", None), P("blk"), P(), P("blk"), P(), P(), P("blk", "head"),
            P("blk", "head"), P("blk"), P(None, "head"), P(None, "head"), P(None, "head"),
            P("head", None), P(None, "head"), P(), P(),
        ),
        out_specs=(P("blk", "head"), P("blk")),
        check_vma=False,
    )
```

time: 255 us -> 82.3 us (0.32)
  waiting for transfers between devices: 134 us -> 11.6 us
  matrix products: 29.7 us -> 0 us
  Pallas kernels: 0 us -> 25 us
  other arithmetic: 20.8 us -> 0 us
  local copies, waits for them, and re-layouts: 31.1 us -> 11.6 us
  between operations: 16.1 us -> 0.91 us
  starting transfers between devices: 22.5 us -> 32.7 us
    psum x1 -> x0, waiting for transfers between devices: 103 us -> none  [body(): whole_sum = lax.psum(partial_update, 'head')]
    ppermute x0 -> x22, starting transfers between devices: none -> 32.7 us  [partner(): return lax.ppermute(value, axis, [(i, i ^ k) for i in range(count)])]
    all_to_all x5 -> x0, waiting for transfers between devices: 30.6 us -> none  [the longest x1 21 us: body(): lax.all_to_all(sums, 'blk', split_axis=0, concat_axis=0, tiled=True)]
    dot_general x15 -> x0, matrix products: 29.7 us -> none  [the longest x2 6.23 us: one_block(): jnp.einsum('htr,rhd->thd', weights, cache_values, preferred_element_type=...]
    pallas_call x0 -> x15, Pallas kernels: none -> 25 us  [the longest x4 9.79 us: body(): pl.pallas_call(functools.partial(output_kernel, head_count, 2 * k), out_s...]
    all_to_all x5 -> x0, starting transfers between devices: 22.3 us -> none  [the longest x1 6.33 us: body(): lax.all_to_all(send_var, 'blk', split_axis=0, concat_axis=0, tiled=True)]
    ppermute x0 -> x22, waiting for transfers between devices: none -> 11.6 us  [partner(): return lax.ppermute(value, axis, [(i, i ^ k) for i in range(count)])]
    reduce_sum x7 -> x0, other arithmetic: 9.58 us -> none  [the longest x3 4.72 us: softmax_part(): return (peak, jnp.sum(weights, axis=-1), weights.astype(jnp.bfloat16))]
  transfers between devices with their start and end apart: 6 -> 22, of which waited for: 5 -> 4; matrix products, arithmetic and copies ran while one was open for 13% -> 0% of each run, Pallas kernels for 0% -> 27%
where the time goes in v1:
time: 82.3 us; the launch traced here: 81.8 us
  starting transfers between devices  32.7 us (40%)
  Pallas kernels  25 us (30%)
  local copies, waits for them, and re-layouts  11.6 us (14%)
  waiting for transfers between devices  11.6 us (14%)
  between operations  0.91 us (1%)
    ppermute x22, starting transfers between devices, partner(): return lax.ppermute(value, axis, [(i, i ^ k) for i in range(count)])  32.7 us
    ppermute x22, waiting for transfers between devices, partner(): return lax.ppermute(value, axis, [(i, i ^ k) for i in range(count)])  11.6 us
    unnamed x54, local copies, waits for them, and re-layouts  11 us
    pallas_call x4, Pallas kernels, body(): pl.pallas_call(functools.partial(output_kernel, head_count, 2 * k), out_s...  9.79 us
    pallas_call x4, Pallas kernels, from_cache(): call(functools.partial(cache_kernel, bpq), chunk_shape, [SMEM] * 3 + [VME...  7.84 us
    pallas_call x1, Pallas kernels, body(): call(own_kernel, sds((slots, cols + 8, width), F32), [SMEM] * 4 + [VMEM]...  4.5 us
    pallas_call x1, Pallas kernels, body(): call(functools.partial(query_kernel, bpq), [sds((blocks,), jnp.int32)] +...  2.25 us
  transfers between devices with their start and end apart: 22, of which 4 were waited for; matrix products, arithmetic and copies ran while one was open for 0% of the time, Pallas kernels for 27%

profile of v1, /device:TPU:0, one launch (start us, length us, event | category | flops | bytes accessed | tf_op | source)
XLA Modules:
  0.0 81.8 jit_solution(2712576940244296440)
XLA Ops:
  0.7 1.0 %copy-done.4 = bf16[512,256]{1,0:T(8,128)(2,1)S(1)} copy-done((bf16[512,256]{1,0:T(8,128)(2,1)S(1)}, bf16[512,256]{1,0:T(8,128)(2,1)}, u32[]{:S(2)}) %copy-start.4) | copy-done | bytes 262168
  1.6 0.9 %copy-done.5 = bf16[512,256]{1,0:T(8,128)(2,1)S(1)} copy-done((bf16[512,256]{1,0:T(8,128)(2,1)S(1)}, bf16[512,256]{1,0:T(8,128)(2,1)}, u32[]{:S(2)}) %copy-start.5) | copy-done | bytes 262168
  2.6 0.7 copy-done.23
  3.4 0.5 collective-permute-start.1
  3.9 3.5 %collective-permute-start.8 = (bf16[256,1024]{1,0:T(8,128)(2,1)}, bf16[256,1024]{1,0:T(8,128)(2,1)S(1)}, u32[]{:S(2)}, u32[]{:S(2)}) collective-permute-start(bf16[256,1024]{1,0:T(8,128)(2,1)} %refs_4_.7), channel_id=1, source_target_pairs={{0,24},{8,16},{16,8},{24,0},{1,25},{9,17},{17,9},{25,1},{2,26},{10... | collective-permute-start | bytes 1572872 | tf_op jit(solution)/shard_map/ppermute | solution.py:293
  7.4 0.5 collective-permute-start.7
  8.1 1.6 %copy-done = bf16[1024,1024]{1,0:T(8,128)(2,1)S(1)} copy-done((bf16[1024,1024]{1,0:T(8,128)(2,1)S(1)}, bf16[1024,1024]{1,0:T(8,128)(2,1)}, u32[]{:S(2)}) %copy-start) | copy-done | bytes 2097176
  9.7 1.0 %copy-done.3 = bf16[1024,256]{1,0:T(8,128)(2,1)S(1)} copy-done((bf16[1024,256]{1,0:T(8,128)(2,1)S(1)}, bf16[1024,256]{1,0:T(8,128)(2,1)}, u32[]{:S(2)}) %copy-start.3) | copy-done | bytes 524312
  10.7 0.7 copy-done.6
  11.4 0.8 %copy-done.8 = f32[128,128]{1,0:T(8,128)S(1)} copy-done((f32[128,128]{1,0:T(8,128)S(1)}, f32[128,128]{1,0:T(8,128)}, u32[]{:S(2)}) %copy-start.8) | copy-done | bytes 65560
  12.2 0.8 %copy-done.10 = f32[128,128]{1,0:T(8,128)S(1)} copy-done((f32[128,128]{1,0:T(8,128)S(1)}, f32[128,128]{1,0:T(8,128)}, u32[]{:S(2)}) %copy-start.10) | copy-done | bytes 65560
  13.1 0.7 copy-done.15
  13.7 0.7 copy-done.17
  14.4 0.7 copy-done.19
  15.1 0.7 copy-done.21
  15.8 0.7 copy-done.24
  16.5 2.3 %query.1 = (s32[8]{0:T(128)S(1)}, bf16[272,256]{1,0:T(8,128)(2,1)S(1)}, bf16[272,256]{1,0:T(8,128)(2,1)S(1)}, bf16[272,256]{1,0:T(8,128)(2,1)S(1)}, bf16[272,256]{1,0:T(8,128)(2,1)S(1)}) custom-call(s32[128]{0:T(128)S(1)} %copy-done.24, s32[8]{0:T(128)S(1)} %copy-done.15, s32[8]{0:T(128)S(1)} %copy-done.17, bf16[1024,1024]{1,0:T(8,128)(2,1)S(1)} %copy-done, ...), custom_call_target="tpu_custom_call" | custom-call | flops 536870912 | bytes 2097152 | tf_op jit(solution)/shard_map/query/pallas_call | solution.py:338
  18.7 2.0 %collective-permute-start.14 = (bf16[272,256]{1,0:T(8,128)(2,1)S(1)}, bf16[272,256]{1,0:T(8,128)(2,1)S(1)}, u32[]{:S(2)}, u32[]{:S(2)}) collective-permute-start(bf16[272,256]{1,0:T(8,128)(2,1)S(1)} %get-tuple-element.18.refs_1_), channel_id=1, source_target_pairs={{0,2},{1,3},{2,0},{3,1},{4,6},{5,7},{6,4},{7,5},{8,10},{9,11},{10,... | collective-permute-start | bytes 417800 | tf_op jit(solution)/shard_map/ppermute | solution.py:293
  20.8 3.4 %collective-permute-done.14.q_ref = bf16[272,256]{1,0:T(8,128)(2,1)S(1)} collective-permute-done((bf16[272,256]{1,0:T(8,128)(2,1)S(1)}, bf16[272,256]{1,0:T(8,128)(2,1)S(1)}, u32[]{:S(2)}, u32[]{:S(2)}) %collective-permute-start.14) | collective-permute-done | bytes 139296 | tf_op jit(solution)/shard_map/ppermute | solution.py:293
  24.2 2.8 %collective-permute-start.9 = (bf16[272,256]{1,0:T(8,128)(2,1)S(1)}, bf16[272,256]{1,0:T(8,128)(2,1)S(1)}, u32[]{:S(2)}, u32[]{:S(2)}) collective-permute-start(bf16[272,256]{1,0:T(8,128)(2,1)S(1)} %get-tuple-element.19.refs_2_), channel_id=1, source_target_pairs={{0,4},{1,5},{2,6},{3,7},{4,0},{5,1},{6,2},{7,3},{8,12},{9,13},{10,... | collective-permute-start | bytes 417800 | tf_op jit(solution)/shard_map/ppermute | solution.py:293
  27.0 1.3 %collective-permute-start = (bf16[272,256]{1,0:T(8,128)(2,1)S(1)}, bf16[272,256]{1,0:T(8,128)(2,1)S(1)}, u32[]{:S(2)}, u32[]{:S(2)}) collective-permute-start(bf16[272,256]{1,0:T(8,128)(2,1)S(1)} %get-tuple-element.16.refs_3_), channel_id=1, source_target_pairs={{0,6},{1,7},{2,4},{3,5},{4,2},{5,3},{6,0},{7,1},{8,14},{9,15},{10,... | collective-permute-start | bytes 417800 | tf_op jit(solution)/shard_map/ppermute | solution.py:293
  28.3 2.0 %cache_part.6 = bf16[272,256]{1,0:T(8,128)(2,1)S(1)} custom-call(s32[8]{0:T(128)S(1)} %copy-done.16, s32[8]{0:T(128)S(1)} %copy-done.18, f32[2,4]{1,0:T(2,128)S(1)} %copy-done.14, bf16[272,256]{1,0:T(8,128)(2,1)S(1)} %collective-permute-done.14.q_ref, bf16[1040,256]{1,0:T(8,128)(2,1)S(1)} %pack.1.own_ref, bf16[1040,256]{1,0:T(8,128)(2,1)S(1)} %collective-permute-done.1.other_ref), custom_call_target="tpu_custom_call" | custom-call | flops 268435456 | bytes 1048576 | tf_op jit(solution)/shard_map/cache_part/pallas_call | solution.py:387
  30.3 6.4 %collective-permute-done.9.q_ref = bf16[272,256]{1,0:T(8,128)(2,1)S(1)} collective-permute-done((bf16[272,256]{1,0:T(8,128)(2,1)S(1)}, bf16[272,256]{1,0:T(8,128)(2,1)S(1)}, u32[]{:S(2)}, u32[]{:S(2)}) %collective-permute-start.9) | collective-permute-done | bytes 139296 | tf_op jit(solution)/shard_map/ppermute | solution.py:293
  36.7 2.0 %cache_part.5 = bf16[272,256]{1,0:T(8,128)(2,1)S(1)} custom-call(s32[8]{0:T(128)S(1)} %copy-done.16, s32[8]{0:T(128)S(1)} %copy-done.18, f32[2,4]{1,0:T(2,128)S(1)} %copy-done.14, bf16[272,256]{1,0:T(8,128)(2,1)S(1)} %collective-permute-done.9.q_ref, bf16[1040,256]{1,0:T(8,128)(2,1)S(1)} %pack.1.own_ref, bf16[1040,256]{1,0:T(8,128)(2,1)S(1)} %collective-permute-done.1.other_ref), custom_call_target="tpu_custom_call" | custom-call | flops 268435456 | bytes 1048576 | tf_op jit(solution)/shard_map/cache_part/pallas_call | solution.py:387
  38.7 3.0 %collective-permute-start.10 = (bf16[272,256]{1,0:T(8,128)(2,1)S(1)}, bf16[272,256]{1,0:T(8,128)(2,1)S(1)}, u32[]{:S(2)}, u32[]{:S(2)}) collective-permute-start(bf16[272,256]{1,0:T(8,128)(2,1)S(1)} %cache_part.5), channel_id=1, source_target_pairs={{0,4},{1,5},{2,6},{3,7},{4,0},{5,1},{6,2},{7,3},{8,12},{9,13},{10,... | collective-permute-start | bytes 417800 | tf_op jit(solution)/shard_map/ppermute | solution.py:293
  41.8 4.5 %own_documents.1.own_ref = f32[8,264,128]{2,1,0:T(8,128)S(1)} custom-call(s32[128]{0:T(128)S(1)} %copy-done.24, s32[8]{0:T(128)S(1)} %copy-done.16, f32[2,4]{1,0:T(2,128)S(1)} %copy-done.14, s32[8]{0:T(128)S(1)} %get-tuple-element.15.home_ref, bf16[1024,1024]{1,0:T(8,128)(2,1)S(1)} %copy-done.1, bf16[1024,256]{1,0:T(8,128)(2,1)S(1)} %copy-done.25, ...), custom_call_target="tpu_custom_call" | custom-call | flops 1610612736 | bytes 2097152 | tf_op jit(solution)/shard_map/own_documents/pallas_call | solution.py:372
  46.3 2.0 %cache_part.7.got_ref = bf16[272,256]{1,0:T(8,128)(2,1)S(1)} custom-call(s32[8]{0:T(128)S(1)} %copy-done.16, s32[8]{0:T(128)S(1)} %copy-done.18, f32[2,4]{1,0:T(2,128)S(1)} %copy-done.14, bf16[272,256]{1,0:T(8,128)(2,1)S(1)} %get-tuple-element.17.refs_0_.q_ref, bf16[1040,256]{1,0:T(8,128)(2,1)S(1)} %pack.1.own_ref, ...), custom_call_target="tpu_custom_call" | custom-call | flops 268435456 | bytes 1048576 | tf_op jit(solution)/shard_map/cache_part/pallas_call | solution.py:387
  48.4 2.5 %collective-permute-start.21 = (bf16[256,256]{1,0:T(8,128)(2,1)S(1)}, bf16[256,256]{1,0:T(8,128)(2,1)S(1)}, u32[]{:S(2)}, u32[]{:S(2)}) collective-permute-start(bf16[256,256]{1,0:T(8,128)(2,1)S(1)} %merge.7.refs_0_), channel_id=1, source_target_pairs={{0,24},{8,16},{16,8},{24,0},{1,25},{9,17},{17,9},{25,1},{2,26},{10... | collective-permute-start | bytes 393224 | tf_op jit(solution)/shard_map/ppermute | solution.py:293
  50.9 0.5 collective-permute-start.20
  51.4 0.5 collective-permute-start.19
  52.0 2.0 %cache_part.4 = bf16[272,256]{1,0:T(8,128)(2,1)S(1)} custom-call(s32[8]{0:T(128)S(1)} %copy-done.16, s32[8]{0:T(128)S(1)} %copy-done.18, f32[2,4]{1,0:T(2,128)S(1)} %copy-done.14, bf16[272,256]{1,0:T(8,128)(2,1)S(1)} %collective-permute-done.q_ref, bf16[1040,256]{1,0:T(8,128)(2,1)S(1)} %pack.1.own_ref, bf16[1040,256]{1,0:T(8,128)(2,1)S(1)} %collective-permute-done.1.other_ref), custom_call_target="tpu_custom_call" | custom-call | flops 268435456 | bytes 1048576 | tf_op jit(solution)/shard_map/cache_part/pallas_call | solution.py:387
  54.0 1.5 %collective-permute-start.2 = (bf16[272,256]{1,0:T(8,128)(2,1)S(1)}, bf16[272,256]{1,0:T(8,128)(2,1)S(1)}, u32[]{:S(2)}, u32[]{:S(2)}) collective-permute-start(bf16[272,256]{1,0:T(8,128)(2,1)S(1)} %cache_part.4), channel_id=1, source_target_pairs={{0,6},{1,7},{2,4},{3,5},{4,2},{5,3},{6,0},{7,1},{8,14},{9,15},{10,... | collective-permute-start | bytes 417800 | tf_op jit(solution)/shard_map/ppermute | solution.py:293
  55.6 2.5 %collective-permute-start.13 = (bf16[256,256]{1,0:T(8,128)(2,1)S(1)}, bf16[256,256]{1,0:T(8,128)(2,1)S(1)}, u32[]{:S(2)}, u32[]{:S(2)}) collective-permute-start(bf16[256,256]{1,0:T(8,128)(2,1)S(1)} %merge.5.refs_0_), channel_id=1, source_target_pairs={{0,24},{8,16},{16,8},{24,0},{1,25},{9,17},{17,9},{25,1},{2,26},{10... | collective-permute-start | bytes 393224 | tf_op jit(solution)/shard_map/ppermute | solution.py:293
  58.3 0.5 collective-permute-start.18
  58.8 1.5 %collective-permute-start.17 = (bf16[256,256]{1,0:T(8,128)(2,1)S(1)}, bf16[256,256]{1,0:T(8,128)(2,1)S(1)}, u32[]{:S(2)}, u32[]{:S(2)}) collective-permute-start(bf16[256,256]{1,0:T(8,128)(2,1)S(1)} %merge.6.refs_0_), channel_id=1, source_target_pairs={{0,16},{8,24},{16,0},{24,8},{1,17},{9,25},{17,1},{25,9},{2,18},{10... | collective-permute-start | bytes 393224 | tf_op jit(solution)/shard_map/ppermute | solution.py:293
  60.3 1.5 %collective-permute-start.16 = (bf16[256,256]{1,0:T(8,128)(2,1)S(1)}, bf16[256,256]{1,0:T(8,128)(2,1)S(1)}, u32[]{:S(2)}, u32[]{:S(2)}) collective-permute-start(bf16[256,256]{1,0:T(8,128)(2,1)S(1)} %merge.6.refs_0_), channel_id=1, source_target_pairs={{0,8},{8,0},{16,24},{24,16},{1,9},{9,1},{17,25},{25,17},{2,10},{10... | collective-permute-start | bytes 393224 | tf_op jit(solution)/shard_map/ppermute | solution.py:293
  61.8 0.7 collective-permute-start.12
  62.5 0.4 collective-permute-done.13.refs_3_
  62.9 1.4 %collective-permute-start.11 = (bf16[256,256]{1,0:T(8,128)(2,1)S(1)}, bf16[256,256]{1,0:T(8,128)(2,1)S(1)}, u32[]{:S(2)}, u32[]{:S(2)}) collective-permute-start(bf16[256,256]{1,0:T(8,128)(2,1)S(1)} %merge.5.refs_0_), channel_id=1, source_target_pairs={{0,8},{8,0},{16,24},{24,16},{1,9},{9,1},{17,25},{25,17},{2,10},{10... | collective-permute-start | bytes 393224 | tf_op jit(solution)/shard_map/ppermute | solution.py:293
  64.4 1.3 %collective-permute-done.18.refs_3_ = bf16[256,256]{1,0:T(8,128)(2,1)S(1)} collective-permute-done((bf16[256,256]{1,0:T(8,128)(2,1)S(1)}, bf16[256,256]{1,0:T(8,128)(2,1)S(1)}, u32[]{:S(2)}, u32[]{:S(2)}) %collective-permute-start.18) | collective-permute-done | bytes 131104 | tf_op jit(solution)/shard_map/ppermute | solution.py:293
  65.7 2.6 %collective-permute-start.5 = (bf16[256,256]{1,0:T(8,128)(2,1)S(1)}, bf16[256,256]{1,0:T(8,128)(2,1)S(1)}, u32[]{:S(2)}, u32[]{:S(2)}) collective-permute-start(bf16[256,256]{1,0:T(8,128)(2,1)S(1)} %merge.4.refs_0_), channel_id=1, source_target_pairs={{0,24},{8,16},{16,8},{24,0},{1,25},{9,17},{17,9},{25,1},{2,26},{10... | collective-permute-start | bytes 393224 | tf_op jit(solution)/shard_map/ppermute | solution.py:293
  68.3 0.9 %collective-permute-start.4 = (bf16[256,256]{1,0:T(8,128)(2,1)S(1)}, bf16[256,256]{1,0:T(8,128)(2,1)S(1)}, u32[]{:S(2)}, u32[]{:S(2)}) collective-permute-start(bf16[256,256]{1,0:T(8,128)(2,1)S(1)} %merge.4.refs_0_), channel_id=1, source_target_pairs={{0,16},{8,24},{16,0},{24,8},{1,17},{9,25},{17,1},{25,9},{2,18},{10... | collective-permute-start | bytes 393224 | tf_op jit(solution)/shard_map/ppermute | solution.py:293
  69.2 2.2 %collective-permute-start.3 = (bf16[256,256]{1,0:T(8,128)(2,1)S(1)}, bf16[256,256]{1,0:T(8,128)(2,1)S(1)}, u32[]{:S(2)}, u32[]{:S(2)}) collective-permute-start(bf16[256,256]{1,0:T(8,128)(2,1)S(1)} %merge.4.refs_0_), channel_id=1, source_target_pairs={{0,8},{8,0},{16,24},{24,16},{1,9},{9,1},{17,25},{25,17},{2,10},{10... | collective-permute-start | bytes 393224 | tf_op jit(solution)/shard_map/ppermute | solution.py:293
  71.4 2.4 %output.4 = (f32[1024,256]{1,0:T(8,128)}, f32[8,1,128]{2,1,0:T(1,128)S(1)}) custom-call(s32[8]{0:T(128)S(1)} %get-tuple-element.15.home_ref, bf16[256,256]{1,0:T(8,128)(2,1)S(1)} %merge.7.refs_0_, bf16[256,256]{1,0:T(8,128)(2,1)S(1)} %collective-permute-done.19.refs_1_, bf16[256,256]{1,0:T(8,128)(2,1)S(1)} %collective-permute-done.20.refs_2_, ...), custom_call_target="tpu_custom_call" | custom-call | flops 536870912 | bytes 2097152 | tf_op jit(solution)/shard_map/output/pallas_call | solution.py:423
  73.8 2.4 %output.5 = (f32[1024,256]{1,0:T(8,128)}, f32[8,1,128]{2,1,0:T(1,128)S(1)}) custom-call(s32[8]{0:T(128)S(1)} %get-tuple-element.15.home_ref, bf16[256,256]{1,0:T(8,128)(2,1)S(1)} %merge.6.refs_0_, bf16[256,256]{1,0:T(8,128)(2,1)S(1)} %collective-permute-done.16.refs_1_, ...), custom_call_target="tpu_custom_call", output_to_operand_aliasing={{0}: (13, {}), {1}: (14, {})} | custom-call | flops 536870912 | bytes 2097152 | tf_op jit(solution)/shard_map/output/pallas_call | solution.py:423
  76.3 2.4 %output.6 = (f32[1024,256]{1,0:T(8,128)}, f32[8,1,128]{2,1,0:T(1,128)S(1)}) custom-call(s32[8]{0:T(128)S(1)} %get-tuple-element.15.home_ref, bf16[256,256]{1,0:T(8,128)(2,1)S(1)} %merge.5.refs_0_, bf16[256,256]{1,0:T(8,128)(2,1)S(1)} %collective-permute-done.11.refs_1_, ...), custom_call_target="tpu_custom_call", output_to_operand_aliasing={{0}: (13, {}), {1}: (14, {})} | custom-call | flops 536870912 | bytes 2097152 | tf_op jit(solution)/shard_map/output/pallas_call | solution.py:423
  78.7 2.5 %output.7 = (f32[1024,256]{1,0:T(8,128)}, f32[8,1,128]{2,1,0:T(1,128)S(1)}) custom-call(s32[8]{0:T(128)S(1)} %get-tuple-element.15.home_ref, bf16[256,256]{1,0:T(8,128)(2,1)S(1)} %merge.4.refs_0_, bf16[256,256]{1,0:T(8,128)(2,1)S(1)} %collective-permute-done.3.refs_1_, ...), custom_call_target="tpu_custom_call", output_to_operand_aliasing={{0}: (13, {}), {1}: (14, {})} | custom-call | flops 536870912 | bytes 2097152 | tf_op jit(solution)/shard_map/output/pallas_call | solution.py:423
  81.2 0.6 reshape_squeeze.3
  (67 shorter events, 1.0 us)
Async XLA Ops:
  0.6 27.7 %copy-start.16 = (s32[8]{0:T(128)S(1)}, s32[8]{0:T(128)}, u32[]{:S(2)}) copy-start(s32[8]{0:T(128)} %query_len.11) | copy-start | bytes 100
  0.6 27.7 %copy-start.14 = (f32[2,4]{1,0:T(2,128)S(1)}, f32[2,4]{1,0:T(2,128)}, u32[]{:S(2)}) copy-start(f32[2,4]{1,0:T(2,128)} %bias_ref.9) | copy-start | bytes 100
  0.7 1.0 %copy-start.4 = (bf16[512,256]{1,0:T(8,128)(2,1)S(1)}, bf16[512,256]{1,0:T(8,128)(2,1)}, u32[]{:S(2)}) copy-start(bf16[512,256]{1,0:T(8,128)(2,1)} %k_ref.1) | copy-start | bytes 786436
  1.6 0.9 %copy-start.5 = (bf16[512,256]{1,0:T(8,128)(2,1)S(1)}, bf16[512,256]{1,0:T(8,128)(2,1)}, u32[]{:S(2)}) copy-start(bf16[512,256]{1,0:T(8,128)(2,1)} %v_ref.1) | copy-start | bytes 786436
  2.6 0.7 copy-start.23
  3.2 25.1 %copy-start.18 = (s32[8]{0:T(128)S(1)}, s32[8]{0:T(128)}, u32[]{:S(2)}) copy-start(s32[8]{0:T(128)} %block_perm.9) | copy-start | bytes 100
  3.4 23.6 %collective-permute-start.1 = (bf16[1040,256]{1,0:T(8,128)(2,1)S(1)}, bf16[1040,256]{1,0:T(8,128)(2,1)S(1)}, u32[]{:S(2)}, u32[]{:S(2)}) collective-permute-start(bf16[1040,256]{1,0:T(8,128)(2,1)S(1)} %pack.1.own_ref), channel_id=1, source_target_pairs={{0,1},{1,0},{2,3},{3,2},{4,5},{5,4},{6,7},{7,6},{8,9},{9,8},{10,11... | collective-permute-start | bytes 1597448 | tf_op jit(solution)/shard_map/ppermute | solution.py:293
  3.9 44.5 %collective-permute-start.8 = (bf16[256,1024]{1,0:T(8,128)(2,1)}, bf16[256,1024]{1,0:T(8,128)(2,1)S(1)}, u32[]{:S(2)}, u32[]{:S(2)}) collective-permute-start(bf16[256,1024]{1,0:T(8,128)(2,1)} %refs_4_.7), channel_id=1, source_target_pairs={{0,24},{8,16},{16,8},{24,0},{1,25},{9,17},{17,9},{25,1},{2,26},{10... | collective-permute-start | bytes 1572872 | tf_op jit(solution)/shard_map/ppermute | solution.py:293
  7.4 43.5 %collective-permute-start.7 = (bf16[256,1024]{1,0:T(8,128)(2,1)}, bf16[256,1024]{1,0:T(8,128)(2,1)S(1)}, u32[]{:S(2)}, u32[]{:S(2)}) collective-permute-start(bf16[256,1024]{1,0:T(8,128)(2,1)} %refs_4_.7), channel_id=1, source_target_pairs={{0,16},{8,24},{16,0},{24,8},{1,17},{9,25},{17,1},{25,9},{2,18},{10... | collective-permute-start | bytes 1572872 | tf_op jit(solution)/shard_map/ppermute | solution.py:293
  7.9 43.5 %collective-permute-start.6 = (bf16[256,1024]{1,0:T(8,128)(2,1)}, bf16[256,1024]{1,0:T(8,128)(2,1)S(1)}, u32[]{:S(2)}, u32[]{:S(2)}) collective-permute-start(bf16[256,1024]{1,0:T(8,128)(2,1)} %refs_4_.7), channel_id=1, source_target_pairs={{0,8},{8,0},{16,24},{24,16},{1,9},{9,1},{17,25},{25,17},{2,10},{10... | collective-permute-start | bytes 1572872 | tf_op jit(solution)/shard_map/ppermute | solution.py:293
  8.1 1.6 %copy-start = (bf16[1024,1024]{1,0:T(8,128)(2,1)S(1)}, bf16[1024,1024]{1,0:T(8,128)(2,1)}, u32[]{:S(2)}) copy-start(bf16[1024,1024]{1,0:T(8,128)(2,1)} %refs_8_.7) | copy-start | bytes 6291460
  9.7 1.0 %copy-start.3 = (bf16[1024,256]{1,0:T(8,128)(2,1)S(1)}, bf16[1024,256]{1,0:T(8,128)(2,1)}, u32[]{:S(2)}) copy-start(bf16[1024,256]{1,0:T(8,128)(2,1)} %w_ref.1) | copy-start | bytes 1572868
  10.7 0.7 copy-start.6
  11.4 0.8 %copy-start.8 = (f32[128,128]{1,0:T(8,128)S(1)}, f32[128,128]{1,0:T(8,128)}, u32[]{:S(2)}) copy-start(f32[128,128]{1,0:T(8,128)} %constant.7.clone.sin_ref) | copy-start | bytes 196612
  12.2 0.8 %copy-start.10 = (f32[128,128]{1,0:T(8,128)S(1)}, f32[128,128]{1,0:T(8,128)}, u32[]{:S(2)}) copy-start(f32[128,128]{1,0:T(8,128)} %constant.6.clone.cos_ref) | copy-start | bytes 196612
  13.1 0.7 copy-start.15
  13.7 0.7 copy-start.17
  14.4 0.7 copy-start.19
  15.1 0.7 copy-start.21
  16.4 25.3 %copy-start.1 = (bf16[1024,1024]{1,0:T(8,128)(2,1)S(1)}, bf16[1024,1024]{1,0:T(8,128)(2,1)}, u32[]{:S(2)}) copy-start(bf16[1024,1024]{1,0:T(8,128)(2,1)} %refs_8_.7) | copy-start | bytes 6291460
  16.4 25.3 %copy-start.7 = (s32[1024]{0:T(1024)S(1)}, s32[1024]{0:T(1024)}, u32[]{:S(2)}) copy-start(s32[1024]{0:T(1024)} %param.20) | copy-start | bytes 12292
  16.4 25.3 %copy-start.9 = (f32[128,128]{1,0:T(8,128)S(1)}, f32[128,128]{1,0:T(8,128)}, u32[]{:S(2)}) copy-start(f32[128,128]{1,0:T(8,128)} %constant.7.clone.sin_ref) | copy-start | bytes 196612
  16.4 25.3 %copy-start.11 = (f32[128,128]{1,0:T(8,128)S(1)}, f32[128,128]{1,0:T(8,128)}, u32[]{:S(2)}) copy-start(f32[128,128]{1,0:T(8,128)} %constant.6.clone.cos_ref) | copy-start | bytes 196612
  16.4 25.3 %copy-start.20 = (s32[1024]{0:T(1024)S(1)}, s32[1024]{0:T(1024)}, u32[]{:S(2)}) copy-start(s32[1024]{0:T(1024)} %param.22) | copy-start | bytes 12292
  16.4 25.3 %copy-start.22 = (f32[8,128]{1,0:T(8,128)S(1)}, f32[8,128]{1,0:T(8,128)}, u32[]{:S(2)}) copy-start(f32[8,128]{1,0:T(8,128)} %constant.8.clone.rows_ref) | copy-start | bytes 12292
  16.5 25.3 %copy-start.25 = (bf16[1024,256]{1,0:T(8,128)(2,1)S(1)}, bf16[1024,256]{1,0:T(8,128)(2,1)}, u32[]{:S(2)}) copy-start(bf16[1024,256]{1,0:T(8,128)(2,1)} %wk_ref.1) | copy-start | bytes 1572868
  16.5 25.3 %copy-start.26 = (bf16[1024,256]{1,0:T(8,128)(2,1)S(1)}, bf16[1024,256]{1,0:T(8,128)(2,1)}, u32[]{:S(2)}) copy-start(bf16[1024,256]{1,0:T(8,128)(2,1)} %wv_ref.1) | copy-start | bytes 1572868
  18.7 5.5 %collective-permute-start.14 = (bf16[272,256]{1,0:T(8,128)(2,1)S(1)}, bf16[272,256]{1,0:T(8,128)(2,1)S(1)}, u32[]{:S(2)}, u32[]{:S(2)}) collective-permute-start(bf16[272,256]{1,0:T(8,128)(2,1)S(1)} %get-tuple-element.18.refs_1_), channel_id=1, source_target_pairs={{0,2},{1,3},{2,0},{3,1},{4,6},{5,7},{6,4},{7,5},{8,10},{9,11},{10,... | collective-permute-start | bytes 417800 | tf_op jit(solution)/shard_map/ppermute | solution.py:293
  24.2 12.5 %collective-permute-start.9 = (bf16[272,256]{1,0:T(8,128)(2,1)S(1)}, bf16[272,256]{1,0:T(8,128)(2,1)S(1)}, u32[]{:S(2)}, u32[]{:S(2)}) collective-permute-start(bf16[272,256]{1,0:T(8,128)(2,1)S(1)} %get-tuple-element.19.refs_2_), channel_id=1, source_target_pairs={{0,4},{1,5},{2,6},{3,7},{4,0},{5,1},{6,2},{7,3},{8,12},{9,13},{10,... | collective-permute-start | bytes 417800 | tf_op jit(solution)/shard_map/ppermute | solution.py:293
  27.0 11.7 %collective-permute-start = (bf16[272,256]{1,0:T(8,128)(2,1)S(1)}, bf16[272,256]{1,0:T(8,128)(2,1)S(1)}, u32[]{:S(2)}, u32[]{:S(2)}) collective-permute-start(bf16[272,256]{1,0:T(8,128)(2,1)S(1)} %get-tuple-element.16.refs_3_), channel_id=1, source_target_pairs={{0,6},{1,7},{2,4},{3,5},{4,2},{5,3},{6,0},{7,1},{8,14},{9,15},{10,... | collective-permute-start | bytes 417800 | tf_op jit(solution)/shard_map/ppermute | solution.py:293
  36.7 18.9 %collective-permute-start.15 = (bf16[272,256]{1,0:T(8,128)(2,1)S(1)}, bf16[272,256]{1,0:T(8,128)(2,1)S(1)}, u32[]{:S(2)}, u32[]{:S(2)}) collective-permute-start(bf16[272,256]{1,0:T(8,128)(2,1)S(1)} %cache_part.6), channel_id=1, source_target_pairs={{0,2},{1,3},{2,0},{3,1},{4,6},{5,7},{6,4},{7,5},{8,10},{9,11},{10,... | collective-permute-start | bytes 417800 | tf_op jit(solution)/shard_map/ppermute | solution.py:293
  38.7 15.3 %collective-permute-start.10 = (bf16[272,256]{1,0:T(8,128)(2,1)S(1)}, bf16[272,256]{1,0:T(8,128)(2,1)S(1)}, u32[]{:S(2)}, u32[]{:S(2)}) collective-permute-start(bf16[272,256]{1,0:T(8,128)(2,1)S(1)} %cache_part.5), channel_id=1, source_target_pairs={{0,4},{1,5},{2,6},{3,7},{4,0},{5,1},{6,2},{7,3},{8,12},{9,13},{10,... | collective-permute-start | bytes 417800 | tf_op jit(solution)/shard_map/ppermute | solution.py:293
  48.4 9.9 %collective-permute-start.21 = (bf16[256,256]{1,0:T(8,128)(2,1)S(1)}, bf16[256,256]{1,0:T(8,128)(2,1)S(1)}, u32[]{:S(2)}, u32[]{:S(2)}) collective-permute-start(bf16[256,256]{1,0:T(8,128)(2,1)S(1)} %merge.7.refs_0_), channel_id=1, source_target_pairs={{0,24},{8,16},{16,8},{24,0},{1,25},{9,17},{17,9},{25,1},{2,26},{10... | collective-permute-start | bytes 393224 | tf_op jit(solution)/shard_map/ppermute | solution.py:293
  50.9 7.9 %collective-permute-start.20 = (bf16[256,256]{1,0:T(8,128)(2,1)S(1)}, bf16[256,256]{1,0:T(8,128)(2,1)S(1)}, u32[]{:S(2)}, u32[]{:S(2)}) collective-permute-start(bf16[256,256]{1,0:T(8,128)(2,1)S(1)} %merge.7.refs_0_), channel_id=1, source_target_pairs={{0,16},{8,24},{16,0},{24,8},{1,17},{9,25},{17,1},{25,9},{2,18},{10... | collective-permute-start | bytes 393224 | tf_op jit(solution)/shard_map/ppermute | solution.py:293
  51.4 8.9 %collective-permute-start.19 = (bf16[256,256]{1,0:T(8,128)(2,1)S(1)}, bf16[256,256]{1,0:T(8,128)(2,1)S(1)}, u32[]{:S(2)}, u32[]{:S(2)}) collective-permute-start(bf16[256,256]{1,0:T(8,128)(2,1)S(1)} %merge.7.refs_0_), channel_id=1, source_target_pairs={{0,8},{8,0},{16,24},{24,16},{1,9},{9,1},{17,25},{25,17},{2,10},{10... | collective-permute-start | bytes 393224 | tf_op jit(solution)/shard_map/ppermute | solution.py:293
  53.9 17.5 %copy-start.2 = (bf16[256,1024]{1,0:T(8,128)(2,1)S(1)}, bf16[256,1024]{1,0:T(8,128)(2,1)}, u32[]{:S(2)}) copy-start(bf16[256,1024]{1,0:T(8,128)(2,1)} %refs_4_.7) | copy-start | bytes 1572868
  53.9 17.5 %copy-start.12 = (f32[1024]{0:T(1024)S(1)}, f32[1024]{0:T(1024)}, u32[]{:S(2)}) copy-start(f32[1024]{0:T(1024)} %param.33) | copy-start | bytes 12292
  53.9 17.4 %copy-start.13 = (f32[1024]{0:T(1024)S(1)}, f32[1024]{0:T(1024)}, u32[]{:S(2)}) copy-start(f32[1024]{0:T(1024)} %param.34) | copy-start | bytes 12292
  54.0 7.9 %collective-permute-start.2 = (bf16[272,256]{1,0:T(8,128)(2,1)S(1)}, bf16[272,256]{1,0:T(8,128)(2,1)S(1)}, u32[]{:S(2)}, u32[]{:S(2)}) collective-permute-start(bf16[272,256]{1,0:T(8,128)(2,1)S(1)} %cache_part.4), channel_id=1, source_target_pairs={{0,6},{1,7},{2,4},{3,5},{4,2},{5,3},{6,0},{7,1},{8,14},{9,15},{10,... | collective-permute-start | bytes 417800 | tf_op jit(solution)/shard_map/ppermute | solution.py:293
  55.6 7.3 %collective-permute-start.13 = (bf16[256,256]{1,0:T(8,128)(2,1)S(1)}, bf16[256,256]{1,0:T(8,128)(2,1)S(1)}, u32[]{:S(2)}, u32[]{:S(2)}) collective-permute-start(bf16[256,256]{1,0:T(8,128)(2,1)S(1)} %merge.5.refs_0_), channel_id=1, source_target_pairs={{0,24},{8,16},{16,8},{24,0},{1,25},{9,17},{17,9},{25,1},{2,26},{10... | collective-permute-start | bytes 393224 | tf_op jit(solution)/shard_map/ppermute | solution.py:293
  58.3 7.4 %collective-permute-start.18 = (bf16[256,256]{1,0:T(8,128)(2,1)S(1)}, bf16[256,256]{1,0:T(8,128)(2,1)S(1)}, u32[]{:S(2)}, u32[]{:S(2)}) collective-permute-start(bf16[256,256]{1,0:T(8,128)(2,1)S(1)} %merge.6.refs_0_), channel_id=1, source_target_pairs={{0,24},{8,16},{16,8},{24,0},{1,25},{9,17},{17,9},{25,1},{2,26},{10... | collective-permute-start | bytes 393224 | tf_op jit(solution)/shard_map/ppermute | solution.py:293
  58.8 9.5 %collective-permute-start.17 = (bf16[256,256]{1,0:T(8,128)(2,1)S(1)}, bf16[256,256]{1,0:T(8,128)(2,1)S(1)}, u32[]{:S(2)}, u32[]{:S(2)}) collective-permute-start(bf16[256,256]{1,0:T(8,128)(2,1)S(1)} %merge.6.refs_0_), channel_id=1, source_target_pairs={{0,16},{8,24},{16,0},{24,8},{1,17},{9,25},{17,1},{25,9},{2,18},{10... | collective-permute-start | bytes 393224 | tf_op jit(solution)/shard_map/ppermute | solution.py:293
  60.3 8.9 %collective-permute-start.16 = (bf16[256,256]{1,0:T(8,128)(2,1)S(1)}, bf16[256,256]{1,0:T(8,128)(2,1)S(1)}, u32[]{:S(2)}, u32[]{:S(2)}) collective-permute-start(bf16[256,256]{1,0:T(8,128)(2,1)S(1)} %merge.6.refs_0_), channel_id=1, source_target_pairs={{0,8},{8,0},{16,24},{24,16},{1,9},{9,1},{17,25},{25,17},{2,10},{10... | collective-permute-start | bytes 393224 | tf_op jit(solution)/shard_map/ppermute | solution.py:293
  61.8 14.5 %collective-permute-start.12 = (bf16[256,256]{1,0:T(8,128)(2,1)S(1)}, bf16[256,256]{1,0:T(8,128)(2,1)S(1)}, u32[]{:S(2)}, u32[]{:S(2)}) collective-permute-start(bf16[256,256]{1,0:T(8,128)(2,1)S(1)} %merge.5.refs_0_), channel_id=1, source_target_pairs={{0,16},{8,24},{16,0},{24,8},{1,17},{9,25},{17,1},{25,9},{2,18},{10... | collective-permute-start | bytes 393224 | tf_op jit(solution)/shard_map/ppermute | solution.py:293
  62.9 13.4 %collective-permute-start.11 = (bf16[256,256]{1,0:T(8,128)(2,1)S(1)}, bf16[256,256]{1,0:T(8,128)(2,1)S(1)}, u32[]{:S(2)}, u32[]{:S(2)}) collective-permute-start(bf16[256,256]{1,0:T(8,128)(2,1)S(1)} %merge.5.refs_0_), channel_id=1, source_target_pairs={{0,8},{8,0},{16,24},{24,16},{1,9},{9,1},{17,25},{25,17},{2,10},{10... | collective-permute-start | bytes 393224 | tf_op jit(solution)/shard_map/ppermute | solution.py:293
  65.7 13.0 %collective-permute-start.5 = (bf16[256,256]{1,0:T(8,128)(2,1)S(1)}, bf16[256,256]{1,0:T(8,128)(2,1)S(1)}, u32[]{:S(2)}, u32[]{:S(2)}) collective-permute-start(bf16[256,256]{1,0:T(8,128)(2,1)S(1)} %merge.4.refs_0_), channel_id=1, source_target_pairs={{0,24},{8,16},{16,8},{24,0},{1,25},{9,17},{17,9},{25,1},{2,26},{10... | collective-permute-start | bytes 393224 | tf_op jit(solution)/shard_map/ppermute | solution.py:293
  68.3 10.4 %collective-permute-start.4 = (bf16[256,256]{1,0:T(8,128)(2,1)S(1)}, bf16[256,256]{1,0:T(8,128)(2,1)S(1)}, u32[]{:S(2)}, u32[]{:S(2)}) collective-permute-start(bf16[256,256]{1,0:T(8,128)(2,1)S(1)} %merge.4.refs_0_), channel_id=1, source_target_pairs={{0,16},{8,24},{16,0},{24,8},{1,17},{9,25},{17,1},{25,9},{2,18},{10... | collective-permute-start | bytes 393224 | tf_op jit(solution)/shard_map/ppermute | solution.py:293
  69.2 9.6 %collective-permute-start.3 = (bf16[256,256]{1,0:T(8,128)(2,1)S(1)}, bf16[256,256]{1,0:T(8,128)(2,1)S(1)}, u32[]{:S(2)}, u32[]{:S(2)}) collective-permute-start(bf16[256,256]{1,0:T(8,128)(2,1)S(1)} %merge.4.refs_0_), channel_id=1, source_target_pairs={{0,8},{8,0},{16,24},{24,16},{1,9},{9,1},{17,25},{25,17},{2,10},{10... | collective-permute-start | bytes 393224 | tf_op jit(solution)/shard_map/ppermute | solution.py:293
  (1 other events, 0.7 us)

commit v2 on v1

--- a/solution.py
+++ b/solution.py
@@ -17,6 +17,9 @@
 F32 = jnp.float32
 VMEM = pl.BlockSpec(memory_space=pltpu.VMEM)
 SMEM = pl.BlockSpec(memory_space=pltpu.SMEM)
+HBM = pl.BlockSpec(memory_space=pltpu.HBM)
+ANY = pl.BlockSpec(memory_space=pl.ANY)
+DMA = pltpu.SemaphoreType.DMA
 LIMIT = 32 * 1024 * 1024
 
 
@@ -95,14 +98,31 @@
     return jnp.concatenate(parts, axis=1)
 
 
-def query_kernel(
-    bpq, doc_query, query_len, block_perm, x_ref, w_ref, seg_ref, var_ref, cos_ref, sin_ref,
-    rows_ref, *refs
-):
-    pick_ref, base_ref, y_ref = refs[0], refs[-2], refs[-1]
-    q_refs = refs[1:-2]
+def copies(sources, targets, sems):
+    moves = [
+        pltpu.make_async_copy(source, target, sems.at[i])
+        for i, (source, target) in enumerate(zip(sources, targets))
+    ]
+    for move in moves:
+        move.start()
+    return moves
+
+
+def query_kernel(bpq, chunks, *refs):
+    sources = refs[:8]
+    pick_ref, q_refs = refs[8], refs[9 : 9 + chunks]
+    targets = refs[9 + chunks : 17 + chunks]
+    base_ref, y_ref, sems = refs[17 + chunks :]
+    moves = copies(sources, targets, sems)
+    doc_query, query_len, block_perm, seg_ref, var_ref, table_ref, x_ref, w_ref = targets
     slots, width = seg_ref.shape
+    cos_ref, sin_ref = table_ref.at[0:width], table_ref.at[width : 2 * width]
+    rows_ref = table_ref.at[2 * width :]
+    for move in moves[:6]:
+        move.wait()
     start_tables(doc_query, query_len, seg_ref, rows_ref, base_ref)
+    for move in moves[6:]:
+        move.wait()
     y_ref[...] = dot(x_ref[...], w_ref[...])
     for k, q_ref in enumerate(q_refs):
         for j in range(2):
@@ -118,16 +138,23 @@
             ).astype(BF)
 
 
-def pack_kernel(k_ref, v_ref, var_ref, out_ref):
-    rows, cols = k_ref.shape
-    out_ref[0:rows, :] = k_ref[...]
+def pack_kernel(k_hbm, v_hbm, var_hbm, w_hbm, after, out_ref, w_ref, v_ref, var_ref, sems):
+    del after
+    rows, cols = v_ref.shape
+    moves = copies(
+        [v_hbm, var_hbm, k_hbm, w_hbm], [v_ref, var_ref, out_ref.at[0:rows], w_ref], sems
+    )
+    moves[0].wait()
     for i in range(rows // cols):
         block = v_ref[i * cols : (i + 1) * cols, :].astype(F32)
         out_ref[rows + i * cols : rows + (i + 1) * cols, :] = block.T.astype(BF)
+    moves[1].wait()
     parts = rows // LANES
     var = var_ref[...].astype(F32)
     var = jnp.concatenate([var, jnp.zeros((EXTRA - parts, LANES), F32)], axis=0)
     out_ref[2 * rows :, :] = jnp.concatenate([var, var], axis=1).astype(BF)
+    for move in moves[2:]:
+        move.wait()
 
 
 def by_head(query):
@@ -162,7 +189,10 @@
     return stats
 
 
-def cache_kernel(bpq, query_len, block_perm, bias_ref, q_ref, own_ref, other_ref, out_ref):
+def cache_kernel(
+    bpq, query_len, block_perm, bias_ref, q_ref, own_ref, other_ref, after, out_ref
+):
+    del after
     blk = lax.axis_index("blk")
     width = q_ref.shape[0] // 2 - EXTRA // 2
     cols = q_ref.shape[1]
@@ -192,13 +222,16 @@
 
 
 def own_kernel(
-    doc_query, query_len, bias_ref, home_ref, x_ref, wk_ref, wv_ref, seg_ref, var_ref, cos_ref,
-    sin_ref, rows_ref, *refs
+    doc_query, query_len, bias_ref, home_ref, x_ref, wk_ref, wv_ref, seg_ref, var_ref, table_ref,
+    after, *refs
 ):
+    del after
     out_ref, base_ref, k_ref, v_ref = refs[-4:]
     q_refs = refs[:-4]
     slots, width = seg_ref.shape
     cols = wk_ref.shape[1]
+    cos_ref, sin_ref = table_ref.at[0:width], table_ref.at[width : 2 * width]
+    rows_ref = table_ref.at[2 * width :]
     start_tables(doc_query, query_len, seg_ref, rows_ref, base_ref)
     k_ref[...] = dot(x_ref[...], wk_ref[...])
     v_ref[...] = dot(x_ref[...], wv_ref[...])
@@ -222,56 +255,83 @@
         part_ref[cols:, :] = stats
 
 
-def merge_kernel(first, got_ref, own_ref, out_ref):
-    cols = got_ref.shape[0] - EXTRA
-    heads = cols // DH
-    width = got_ref.shape[1] // 2
-    for j in range(2):
-        at = slice(j * width, (j + 1) * width)
-        stats = got_ref[cols:, at].astype(F32)
-        there = stats[0:heads] + stats[heads : 2 * heads] + stats[2 * heads : 3 * heads]
-        here = own_ref[first + j, cols : cols + heads, :]
-        peak = jnp.maximum(there, here)
-        there, here = jnp.exp(there - peak), jnp.exp(here - peak)
-        inverse = 1.0 / (there + here)
-        there, here = there * inverse, here * inverse
-        parts = []
-        for h in range(heads):
-            row = slice(h * DH, (h + 1) * DH)
-            parts.append(
-                got_ref[row, at].astype(F32) * there[h : h + 1]
-                + own_ref[first + j, row, :] * here[h : h + 1]
+def merge_kernel(firsts, *refs):
+    own_ref, out_ref = refs[-2:]
+    for i, (first, got_ref) in enumerate(zip(firsts, refs)):
+        cols = got_ref.shape[0] - EXTRA
+        heads = cols // DH
+        width = got_ref.shape[1] // 2
+        for j in range(2):
+            at = slice(j * width, (j + 1) * width)
+            stats = got_ref[cols:, at].astype(F32)
+            there = stats[0:heads] + stats[heads : 2 * heads] + stats[2 * heads : 3 * heads]
+            here = own_ref[first + j, cols : cols + heads, :]
+            peak = jnp.maximum(there, here)
+            there, here = jnp.exp(there - peak), jnp.exp(here - peak)
+            inverse = 1.0 / (there + here)
+            there, here = there * inverse, here * inverse
+            parts = []
+            for h in range(heads):
+                row = slice(h * DH, (h + 1) * DH)
+                parts.append(
+                    got_ref[row, at].astype(F32) * there[h : h + 1]
+                    + own_ref[first + j, row, :] * here[h : h + 1]
+                )
+            to = slice((2 * i + j) * width, (2 * i + j + 1) * width)
+            out_ref[to, :] = jnp.concatenate(parts, axis=0).T.astype(BF)
+
+
+def output_kernel(head_count, firsts, last, home_ref, *refs):
+    att_refs, w_refs = refs[:head_count], refs[head_count : 2 * head_count]
+    x_hbm, seg_ref, gain_ref, read_ref = refs[2 * head_count : 2 * head_count + 4]
+    before = refs[2 * head_count + 4 : -7]
+    update_hbm, pooled_ref, x_ref, gr_ref, out_ref, in_sems, out_sems = refs[-7:]
+    tokens, cols = att_refs[0].shape
+    depth = w_refs[0].shape[1]
+    width = tokens // (2 * len(firsts))
+    places = [first + j for first in firsts for j in range(2)]
+    found = [home_ref[place] for place in places]
+    slots = [pl.ds(pl.multiple_of(slot * width, width), width) for slot in found]
+    here = [slice(i * width, (i + 1) * width) for i in range(len(places))]
+    reads = copies([x_hbm.at[at] for at in slots], [x_ref.at[at] for at in here], in_sems)
+    gr_ref[...] = gain_ref[...] * read_ref[...]
+    head = lax.axis_index("head")
+    square = jnp.zeros((tokens, 1), F32)
+    weighted = jnp.zeros((tokens, 1), F32)
+    writes = []
+    for c in range(depth // cols):
+        start = (head + c) % (depth // cols) * cols
+        at = pl.ds(pl.multiple_of(start, cols), cols)
+        total = dot(att_refs[0][...], w_refs[0][:, at])
+        for att_ref, w_ref in zip(att_refs[1:], w_refs[1:]):
+            total = total + dot(att_ref[...], w_ref[:, at])
+        if c == 0:
+            out_ref[...] = total
+            writes = copies(
+                [out_ref.at[row] for row in here], [update_hbm.at[row] for row in slots], out_sems
             )
-        out_ref[at, :] = jnp.concatenate(parts, axis=0).T.astype(BF)
-
-
-def output_kernel(head_count, first, home_ref, *refs):
-    att_refs, w_refs = refs[:head_count], refs[head_count : 2 * head_count]
-    x_ref, seg_ref, gain_ref, read_ref = refs[2 * head_count : 2 * head_count + 4]
-    update_ref, pooled_ref, sum_ref = refs[-3:]
-    step = pl.program_id(0)
-    slot = home_ref[first + step]
-    total = dot(att_refs[0][...], w_refs[0][...])
-    for att_ref, w_ref in zip(att_refs[1:], w_refs[1:]):
-        total = total + dot(att_ref[...], w_ref[...])
-    sum_ref[...] = total
-    cols = update_ref.shape[1]
-    head = lax.axis_index("head")
-    update_ref[...] = sum_ref[:, pl.ds(pl.multiple_of(head * cols, cols), cols)]
-    hidden = x_ref[...].astype(F32) + total
-    square = jnp.sum(hidden * hidden, axis=1, keepdims=True)
-    weighted = jnp.sum(hidden * (gain_ref[...] * read_ref[...]), axis=1, keepdims=True)
-    score = weighted * lax.rsqrt(square / hidden.shape[1] + 1e-06)
-    width = score.shape[0]
-    second = (seg_ref[pl.ds(slot, 1), :] & 1).astype(F32)
-    count_two = jnp.sum(second, axis=1, keepdims=True)
-    count_one = width - count_two
-    token = lax.broadcasted_iota(jnp.int32, score.shape, 0).astype(F32)
-    is_first = token < count_one
-    sum_one = jnp.sum(jnp.where(is_first, score, 0.0), axis=0, keepdims=True)
-    sum_two = jnp.sum(jnp.where(is_first, 0.0, score), axis=0, keepdims=True)
+            for read in reads:
+                read.wait()
+        hidden = x_ref[:, at].astype(F32) + total
+        square = square + jnp.sum(hidden * hidden, axis=1, keepdims=True)
+        weighted = weighted + jnp.sum(hidden * gr_ref[:, at], axis=1, keepdims=True)
+    score = weighted * lax.rsqrt(square / depth + 1e-06)
+    token = lax.broadcasted_iota(jnp.int32, (width, 1), 0).astype(F32)
     lane = lax.broadcasted_iota(jnp.int32, (1, LANES), 1)
-    pooled_ref[0] = jnp.where(lane == 0, sum_one / count_one, sum_two / count_two)
+    pooled = before[1][...] if before else jnp.zeros((1, LANES), F32)
+    for slot, row in zip(found, here):
+        second = (seg_ref[pl.ds(slot, 1), :] & 1).astype(F32)
+        count_two = jnp.sum(second, axis=1, keepdims=True)
+        count_one = width - count_two
+        is_first = token < count_one
+        part = score[row, :]
+        mean_one = jnp.sum(jnp.where(is_first, part, 0.0), axis=0, keepdims=True) / count_one
+        mean_two = jnp.sum(jnp.where(is_first, 0.0, part), axis=0, keepdims=True) / count_two
+        pooled = jnp.where(lane == 2 * slot, mean_one, pooled)
+        pooled = jnp.where(lane == 2 * slot + 1, mean_two, pooled)
+    pooled_ref[...] = pooled[:, : pooled_ref.shape[1]]
+    for write in writes:
+        write.wait()
 
 
 def call(kernel, out, ins, scratch=(), flops=0, bytes_accessed=0, **kwargs):
@@ -286,6 +346,10 @@
         ),
         **kwargs,
     )
+
+
+def in_hbm(*arrays):
+    return [pltpu.with_memory_space_constraint(array, pltpu.HBM) for array in arrays]
 
 
 def partner(value, axis, k):
@@ -328,41 +392,48 @@
     cache_rows = cache_k.shape[0]
     seg = doc_seg.reshape(slots, width)
     var = doc_var.reshape(slots, width)
-    cos, sin, freq_rows = offset_tables(width)
+    table = np.concatenate(offset_tables(width), axis=0)
+    cache_var = cache_var.reshape(cache_rows // LANES, LANES)
     sds = jax.ShapeDtypeStruct
+    i32 = jnp.int32
     chunk_shape = sds((2 * width + EXTRA, cols), BF)
     base = pltpu.VMEM((5, slots, width), F32)
 
-    w_parts = [w_out] + [partner(w_out, "head", r) for r in range(1, head_count)]
-
     pick, *queries = call(
-        functools.partial(query_kernel, bpq),
-        [sds((blocks,), jnp.int32)] + [chunk_shape] * chunks,
-        [SMEM] * 3 + [VMEM] * 7,
-        [base, pltpu.VMEM((rows, cols), F32)],
+        functools.partial(query_kernel, bpq, chunks),
+        [sds((blocks,), i32)] + [chunk_shape] * chunks,
+        [HBM] * 8,
+        [pltpu.SMEM(ref.shape, i32) for ref in (doc_query, query_len, block_perm)]
+        + [
+            pltpu.VMEM(seg.shape, i32), pltpu.VMEM(var.shape, i32),
+            pltpu.VMEM(table.shape, F32), pltpu.VMEM(doc_x.shape, BF),
+            pltpu.VMEM(w_query.shape, BF), base, pltpu.VMEM((rows, cols), F32), DMA((8,)),
+        ],
         flops=2 * rows * depth * cols,
         bytes_accessed=2 * rows * depth,
         out_specs=[SMEM] + [VMEM] * chunks,
         name="query",
-    )(doc_query, query_len, block_perm, doc_x, w_query, seg, var, cos, sin, freq_rows)
+    )(*in_hbm(doc_query, query_len, block_perm, seg, var, jnp.asarray(table), doc_x, w_query))
 
     asked = [queries[0]] + [partner(queries[k], "blk", 2 * k) for k in range(1, chunks)]
 
-    packed = call(
+    packed, w_own = call(
         pack_kernel,
-        sds((2 * cache_rows + EXTRA, cols), BF),
-        [VMEM] * 3,
+        [sds((2 * cache_rows + EXTRA, cols), BF), sds(w_out.shape, BF)],
+        [HBM] * 4 + [ANY],
+        [pltpu.VMEM(cache_v.shape, BF), pltpu.VMEM(cache_var.shape, i32), DMA((4,))],
         bytes_accessed=8 * cache_rows * cols,
-        out_specs=VMEM,
+        out_specs=[VMEM, VMEM],
         name="pack",
-    )(cache_k, cache_v, cache_var.reshape(cache_rows // LANES, LANES))
+    )(*in_hbm(cache_k, cache_v, cache_var, w_out), pick)
     packed_other = partner(packed, "blk", 1)
+    w_parts = [w_own] + [partner(w_own, "head", r) for r in range(1, head_count)]
 
     if bpq == 1:
         home = pick
         home_queries = queries
     else:
-        home = jnp.arange(slots, dtype=jnp.int32)
+        home = jnp.arange(slots, dtype=i32)
         every = jnp.stack([q[: 2 * width] for q in queries]).reshape(blocks, width, cols)
         every = jnp.take(every, jnp.argsort(pick, stable=True)[::bpq], axis=0)
         home_queries = [
@@ -372,90 +443,70 @@
     own = call(
         own_kernel,
         sds((slots, cols + 8, width), F32),
-        [SMEM] * 4 + [VMEM] * (8 + len(home_queries)),
+        [SMEM] * 4 + [VMEM] * 6 + [ANY] + [VMEM] * len(home_queries),
         [base, pltpu.VMEM((rows, cols), F32), pltpu.VMEM((rows, cols), F32)],
         flops=6 * rows * depth * cols,
-        bytes_accessed=2 * rows * depth,
+        bytes_accessed=8 * rows * depth,
         out_specs=VMEM,
         name="own_documents",
     )(
-        doc_query, query_len, var_bias, home, doc_x, w_key, w_value, seg, var, cos, sin,
-        freq_rows, *home_queries,
+        doc_query, query_len, var_bias, home, doc_x, w_key, w_value, seg, var, table, packed,
+        *home_queries,
     )
 
     def from_cache(query):
         return call(
             functools.partial(cache_kernel, bpq),
             chunk_shape,
-            [SMEM] * 3 + [VMEM] * 3,
+            [SMEM] * 3 + [VMEM] * 3 + [ANY],
             flops=16 * width * cache_rows * cols,
             bytes_accessed=8 * cache_rows * cols,
             out_specs=VMEM,
             name="cache_part",
-        )(query_len, block_perm, var_bias, query, packed, packed_other)
+        )(query_len, block_perm, var_bias, query, packed, packed_other, own)
 
     parts = [from_cache(query) for query in asked]
     backs = [parts[0]] + [partner(parts[k], "blk", 2 * k) for k in range(1, chunks)]
 
+    groups = [[k] for k in range(slots // 2)]
     if bpq == 1:
         attended = [
             call(
-                functools.partial(merge_kernel, 2 * k),
-                sds((2 * width, cols), BF),
-                [VMEM] * 2,
+                functools.partial(merge_kernel, [2 * k for k in group]),
+                sds((2 * width * len(group), cols), BF),
+                [VMEM] * (len(group) + 1),
                 bytes_accessed=4 * rows * cols,
                 out_specs=VMEM,
                 name="merge",
-            )(backs[k], own)
-            for k in range(chunks)
+            )(*[backs[k] for k in group], own)
+            for group in groups
         ]
     else:
         attended = spread_merge(backs, own, pick, slots, bpq)
+        attended = [jnp.concatenate([attended[k] for k in group]) for group in groups]
 
     gain, read = norm_gain.reshape(1, depth), readout.reshape(1, depth)
-    update = pooled = None
-    for k in range(slots // 2):
-        atts = [attended[k]] + [partner(attended[k], "head", r) for r in range(1, head_count)]
-        chained = [] if update is None else [update, pooled]
-        arguments = atts + w_parts + [doc_x, seg, gain, read]
-        whole = lambda i, home: (0, 0)
-        at_slot = functools.partial(lambda k, i, home: (home[2 * k + i], 0), k)
-        update, pooled = pl.pallas_call(
-            functools.partial(output_kernel, head_count, 2 * k),
-            out_shape=[sds((rows, cols), F32), sds((slots, 1, LANES), F32)],
-            grid_spec=pltpu.PrefetchScalarGridSpec(
-                num_scalar_prefetch=1,
-                grid=(2,),
-                in_specs=[pl.BlockSpec((width, cols), lambda i, home: (i, 0))] * head_count
-                + [pl.BlockSpec((cols, depth), whole)] * head_count
-                + [
-                    pl.BlockSpec((width, depth), at_slot),
-                    pl.BlockSpec((slots, width), whole),
-                    pl.BlockSpec((1, depth), whole),
-                    pl.BlockSpec((1, depth), whole),
-                ]
-                + [pl.BlockSpec(memory_space=pl.ANY)] * len(chained),
-                out_specs=[
-                    pl.BlockSpec((width, cols), at_slot),
-                    pl.BlockSpec(
-                        (1, 1, LANES),
-                        functools.partial(lambda k, i, home: (home[2 * k + i], 0, 0), k),
-                    ),
-                ],
-                scratch_shapes=[pltpu.VMEM((width, depth), F32)],
-            ),
-            input_output_aliases=(
-                {1 + len(arguments): 0, 2 + len(arguments): 1} if chained else {}
-            ),
-            compiler_params=pltpu.CompilerParams(vmem_limit_bytes=LIMIT),
-            cost_estimate=pl.CostEstimate(
-                flops=4 * width * depth * depth,
-                bytes_accessed=2 * depth * depth,
-                transcendentals=0,
-            ),
+    chained = []
+    for group, own_part in zip(groups, attended):
+        atts = [own_part] + [partner(own_part, "head", r) for r in range(1, head_count)]
+        places = 2 * len(group)
+        last = group is groups[-1]
+        chained = call(
+            functools.partial(output_kernel, head_count, [2 * k for k in group], last),
+            [sds((rows, cols), F32), sds((1, 2 * slots if last else LANES), F32)],
+            [SMEM] + [VMEM] * (2 * head_count) + [HBM] + [VMEM] * 3 + [HBM, VMEM][: len(chained)],
+            [
+                pltpu.VMEM((places * width, depth), BF), pltpu.VMEM((1, depth), F32),
+                pltpu.VMEM((places * width, cols), F32), DMA((places,)), DMA((places,)),
+            ],
+            flops=4 * places * width * depth * depth,
+            bytes_accessed=2 * depth * depth,
+            out_specs=[HBM, VMEM],
+            input_output_aliases={5 + 2 * head_count: 0} if chained else {},
             name="output",
-        )(home, *arguments, *chained)
-    return (update, pooled[:, 0, :2].reshape(2 * slots))
+        )(home, *atts, *w_parts, *in_hbm(doc_x), seg, gain, read, *chained)
+    update, pooled = chained
+    return (update, pooled.reshape(2 * slots))
 
 
 def solution(mesh):

time: 82.3 us -> 68.8 us (0.84)
  local copies, waits for them, and re-layouts: 11.6 us -> 0.06 us
  waiting for transfers between devices: 11.6 us -> 7.39 us
  Pallas kernels: 25 us -> 28.9 us
  starting transfers between devices: 32.7 us -> 31.1 us
    unnamed x54 -> x24, local copies, waits for them, and re-layouts: 11 us -> 0.06 us
    ppermute x22, waiting for transfers between devices: 11.6 us -> 7.39 us  [partner(): return lax.ppermute(value, axis, [(i, i ^ k) for i in range(count)])]
    pallas_call x10, Pallas kernels: 12.7 us -> 16.5 us  [the longest x4 11 us: body(): call(functools.partial(output_kernel, head_count, [2 * k for k in group],...]
    ppermute x22, starting transfers between devices: 32.7 us -> 31.1 us  [partner(): return lax.ppermute(value, axis, [(i, i ^ k) for i in range(count)])]
  transfers between devices with their start and end apart: 22 -> 22, of which waited for: 4 -> 3; matrix products, arithmetic and copies ran while one was open for 0% -> 0% of each run, Pallas kernels for 27% -> 30%
where the time goes in v2:
time: 68.8 us; the launch traced here: 68.6 us
  starting transfers between devices  31.1 us (45%)
  Pallas kernels  28.9 us (42%)
  waiting for transfers between devices  7.39 us (11%)
  between operations  1.16 us (2%)
    ppermute x22, starting transfers between devices, partner(): return lax.ppermute(value, axis, [(i, i ^ k) for i in range(count)])  31.1 us
    pallas_call x4, Pallas kernels, body(): call(functools.partial(output_kernel, head_count, [2 * k for k in group],...  11 us
    pallas_call x4, Pallas kernels, from_cache(): call(functools.partial(cache_kernel, bpq), chunk_shape, [SMEM] * 3 + [VME...  7.9 us
    ppermute x22, waiting for transfers between devices, partner(): return lax.ppermute(value, axis, [(i, i ^ k) for i in range(count)])  7.39 us
    pallas_call x1, Pallas kernels, body(): call(own_kernel, sds((slots, cols + 8, width), F32), [SMEM] * 4 + [VMEM]...  4.49 us
    pallas_call x1, Pallas kernels, body(): call(functools.partial(query_kernel, bpq, chunks), [sds((blocks,), i32)]...  3.65 us
  transfers between devices with their start and end apart: 22, of which 3 were waited for; matrix products, arithmetic and copies ran while one was open for 0% of the time, Pallas kernels for 30%

profile of v2, /device:TPU:0, one launch (start us, length us, event | category | flops | bytes accessed | tf_op | source)
XLA Modules:
  0.0 68.6 jit_solution(17496665097631030867)
XLA Ops:
  0.6 0.0 copy-start.1
  0.7 0.0 copy-start
  0.7 3.7 %query.1 = (s32[8]{0:T(128)S(1)}, bf16[272,256]{1,0:T(8,128)(2,1)S(1)}, bf16[272,256]{1,0:T(8,128)(2,1)S(1)}, bf16[272,256]{1,0:T(8,128)(2,1)S(1)}, bf16[272,256]{1,0:T(8,128)(2,1)S(1)}) custom-call(s32[128]{0:T(128)} %doc_query.1, s32[8]{0:T(128)} %query_len.9, s32[8]{0:T(128)} %block_perm.7, s32[8,128]{1,0:T(8,128)} %bitcast.6, s32[8,128]{1,0:T(8,128)} %bitcast.20, ...), custom_call_target="tpu_custom_call" | custom-call | flops 536870912 | bytes 2097152 | tf_op jit(solution)/shard_map/query/pallas_call | solution.py:402
  4.4 1.3 %pack.1 = (bf16[1040,256]{1,0:T(8,128)(2,1)S(1)}, bf16[256,1024]{1,0:T(8,128)(2,1)S(1)}) custom-call(bf16[512,256]{1,0:T(8,128)(2,1)} %k_hbm.1, bf16[512,256]{1,0:T(8,128)(2,1)} %v_hbm.1, s32[4,128]{1,0:T(4,128)} %bitcast.22, bf16[256,1024]{1,0:T(8,128)(2,1)} %w_hbm.1, s32[8]{0:T(128)S(1)} %get-tuple-element.17.after.home_ref), custom_call_target="tpu_custom_call" | custom-call | bytes 1048576 | tf_op jit(solution)/shard_map/pack/pallas_call | solution.py:420
  5.7 0.5 collective-permute-start.1
  6.2 3.5 %collective-permute-start.8 = (bf16[256,1024]{1,0:T(8,128)(2,1)S(1)}, bf16[256,1024]{1,0:T(8,128)(2,1)S(1)}, u32[]{:S(2)}, u32[]{:S(2)}) collective-permute-start(bf16[256,1024]{1,0:T(8,128)(2,1)S(1)} %get-tuple-element.23.refs_4_), channel_id=1, source_target_pairs={{0,24},{8,16},{16,8},{24,0},{1,25},{9,17},{17,9},{25,1},{2,26},{10... | collective-permute-start | bytes 1572872 | tf_op jit(solution)/shard_map/ppermute | solution.py:357
  9.7 0.5 collective-permute-start.7
  10.2 0.1 collective-permute-start.6
  10.3 3.0 %collective-permute-start.9 = (bf16[272,256]{1,0:T(8,128)(2,1)S(1)}, bf16[272,256]{1,0:T(8,128)(2,1)S(1)}, u32[]{:S(2)}, u32[]{:S(2)}) collective-permute-start(bf16[272,256]{1,0:T(8,128)(2,1)S(1)} %get-tuple-element.22.refs_2_), channel_id=1, source_target_pairs={{0,4},{1,5},{2,6},{3,7},{4,0},{5,1},{6,2},{7,3},{8,12},{9,13},{10,... | collective-permute-start | bytes 417800 | tf_op jit(solution)/shard_map/ppermute | solution.py:357
  13.3 6.4 %collective-permute-done.9.q_ref = bf16[272,256]{1,0:T(8,128)(2,1)S(1)} collective-permute-done((bf16[272,256]{1,0:T(8,128)(2,1)S(1)}, bf16[272,256]{1,0:T(8,128)(2,1)S(1)}, u32[]{:S(2)}, u32[]{:S(2)}) %collective-permute-start.9) | collective-permute-done | bytes 139296 | tf_op jit(solution)/shard_map/ppermute | solution.py:357
  19.7 3.5 %collective-permute-start = (bf16[272,256]{1,0:T(8,128)(2,1)S(1)}, bf16[272,256]{1,0:T(8,128)(2,1)S(1)}, u32[]{:S(2)}, u32[]{:S(2)}) collective-permute-start(bf16[272,256]{1,0:T(8,128)(2,1)S(1)} %get-tuple-element.18.refs_3_), channel_id=1, source_target_pairs={{0,6},{1,7},{2,4},{3,5},{4,2},{5,3},{6,0},{7,1},{8,14},{9,15},{10,... | collective-permute-start | bytes 417800 | tf_op jit(solution)/shard_map/ppermute | solution.py:357
  23.4 0.0 copy-start.7
  23.4 4.5 %own_documents.1.after.refs_1_ = f32[8,264,128]{2,1,0:T(8,128)S(1)} custom-call(s32[128]{0:T(128)S(1)} %copy-done.9, s32[8]{0:T(128)S(1)} %copy-done.6, f32[2,4]{1,0:T(2,128)S(1)} %copy-done.5, s32[8]{0:T(128)S(1)} %get-tuple-element.17.after.home_ref, bf16[1024,1024]{1,0:T(8,128)(2,1)S(1)} %copy-done, bf16[1024,256]{1,0:T(8,128)(2,1)S(1)} %copy-done.10, ...), custom_call_target="tpu_custom_call" | custom-call | flops 1610612736 | bytes 8388608 | tf_op jit(solution)/shard_map/own_documents/pallas_call | solution.py:443
  27.9 2.0 %cache_part.5 = bf16[272,256]{1,0:T(8,128)(2,1)S(1)} custom-call(s32[8]{0:T(128)S(1)} %copy-done.6, s32[8]{0:T(128)S(1)} %copy-done.7, f32[2,4]{1,0:T(2,128)S(1)} %copy-done.5, bf16[272,256]{1,0:T(8,128)(2,1)S(1)} %collective-permute-done.9.q_ref, bf16[1040,256]{1,0:T(8,128)(2,1)S(1)} %get-tuple-element.19.after.own_ref, ...), custom_call_target="tpu_custom_call" | custom-call | flops 268435456 | bytes 1048576 | tf_op jit(solution)/shard_map/cache_part/pallas_call | solution.py:458
  29.9 0.3 collective-permute-done.14.q_ref
  30.2 0.6 collective-permute-start.10
  30.8 2.0 %cache_part.6 = bf16[272,256]{1,0:T(8,128)(2,1)S(1)} custom-call(s32[8]{0:T(128)S(1)} %copy-done.6, s32[8]{0:T(128)S(1)} %copy-done.7, f32[2,4]{1,0:T(2,128)S(1)} %copy-done.5, bf16[272,256]{1,0:T(8,128)(2,1)S(1)} %collective-permute-done.14.q_ref, bf16[1040,256]{1,0:T(8,128)(2,1)S(1)} %get-tuple-element.19.after.own_ref, ...), custom_call_target="tpu_custom_call" | custom-call | flops 268435456 | bytes 1048576 | tf_op jit(solution)/shard_map/cache_part/pallas_call | solution.py:458
  32.8 0.0 collective-permute-done.q_ref
  32.8 1.7 %collective-permute-start.15 = (bf16[272,256]{1,0:T(8,128)(2,1)S(1)}, bf16[272,256]{1,0:T(8,128)(2,1)S(1)}, u32[]{:S(2)}, u32[]{:S(2)}) collective-permute-start(bf16[272,256]{1,0:T(8,128)(2,1)S(1)} %cache_part.6), channel_id=1, source_target_pairs={{0,2},{1,3},{2,0},{3,1},{4,6},{5,7},{6,4},{7,5},{8,10},{9,11},{10,... | collective-permute-start | bytes 417800 | tf_op jit(solution)/shard_map/ppermute | solution.py:357
  34.5 2.0 %cache_part.7.refs_0_ = bf16[272,256]{1,0:T(8,128)(2,1)S(1)} custom-call(s32[8]{0:T(128)S(1)} %copy-done.6, s32[8]{0:T(128)S(1)} %copy-done.7, f32[2,4]{1,0:T(2,128)S(1)} %copy-done.5, bf16[272,256]{1,0:T(8,128)(2,1)S(1)} %get-tuple-element.20.refs_0_.q_ref, bf16[1040,256]{1,0:T(8,128)(2,1)S(1)} %get-tuple-element.19.after.own_ref, ...), custom_call_target="tpu_custom_call" | custom-call | flops 268435456 | bytes 1048576 | tf_op jit(solution)/shard_map/cache_part/pallas_call | solution.py:458
  36.5 0.1 merge.7.refs_0_
  36.6 0.0 copy-start.3
  36.6 0.0 copy-start.4
  36.7 2.5 %collective-permute-start.21 = (bf16[256,256]{1,0:T(8,128)(2,1)S(1)}, bf16[256,256]{1,0:T(8,128)(2,1)S(1)}, u32[]{:S(2)}, u32[]{:S(2)}) collective-permute-start(bf16[256,256]{1,0:T(8,128)(2,1)S(1)} %merge.7.refs_0_), channel_id=1, source_target_pairs={{0,24},{8,16},{16,8},{24,0},{1,25},{9,17},{17,9},{25,1},{2,26},{10... | collective-permute-start | bytes 393224 | tf_op jit(solution)/shard_map/ppermute | solution.py:357
  39.2 0.0 collective-permute-done.7.refs_6_
  39.2 0.5 collective-permute-start.20
  39.7 0.5 collective-permute-start.19
  40.2 2.0 %cache_part.4 = bf16[272,256]{1,0:T(8,128)(2,1)S(1)} custom-call(s32[8]{0:T(128)S(1)} %copy-done.6, s32[8]{0:T(128)S(1)} %copy-done.7, f32[2,4]{1,0:T(2,128)S(1)} %copy-done.5, bf16[272,256]{1,0:T(8,128)(2,1)S(1)} %collective-permute-done.q_ref, bf16[1040,256]{1,0:T(8,128)(2,1)S(1)} %get-tuple-element.19.after.own_ref, ...), custom_call_target="tpu_custom_call" | custom-call | flops 268435456 | bytes 1048576 | tf_op jit(solution)/shard_map/cache_part/pallas_call | solution.py:458
  42.2 0.0 collective-permute-done.10.refs_0_
  42.2 2.2 %collective-permute-start.2 = (bf16[272,256]{1,0:T(8,128)(2,1)S(1)}, bf16[272,256]{1,0:T(8,128)(2,1)S(1)}, u32[]{:S(2)}, u32[]{:S(2)}) collective-permute-start(bf16[272,256]{1,0:T(8,128)(2,1)S(1)} %cache_part.4), channel_id=1, source_target_pairs={{0,6},{1,7},{2,4},{3,5},{4,2},{5,3},{6,0},{7,1},{8,14},{9,15},{10,... | collective-permute-start | bytes 417800 | tf_op jit(solution)/shard_map/ppermute | solution.py:357
  44.5 0.1 merge.5.refs_0_
  44.6 0.0 collective-permute-done.15.refs_0_
  44.6 2.5 %collective-permute-start.13 = (bf16[256,256]{1,0:T(8,128)(2,1)S(1)}, bf16[256,256]{1,0:T(8,128)(2,1)S(1)}, u32[]{:S(2)}, u32[]{:S(2)}) collective-permute-start(bf16[256,256]{1,0:T(8,128)(2,1)S(1)} %merge.5.refs_0_), channel_id=1, source_target_pairs={{0,24},{8,16},{16,8},{24,0},{1,25},{9,17},{17,9},{25,1},{2,26},{10... | collective-permute-start | bytes 393224 | tf_op jit(solution)/shard_map/ppermute | solution.py:357
  47.1 0.1 merge.6.refs_0_
  47.3 0.5 collective-permute-start.18
  47.8 1.5 %collective-permute-start.17 = (bf16[256,256]{1,0:T(8,128)(2,1)S(1)}, bf16[256,256]{1,0:T(8,128)(2,1)S(1)}, u32[]{:S(2)}, u32[]{:S(2)}) collective-permute-start(bf16[256,256]{1,0:T(8,128)(2,1)S(1)} %merge.6.refs_0_), channel_id=1, source_target_pairs={{0,16},{8,24},{16,0},{24,8},{1,17},{9,25},{17,1},{25,9},{2,18},{10... | collective-permute-start | bytes 393224 | tf_op jit(solution)/shard_map/ppermute | solution.py:357
  49.3 1.5 %collective-permute-start.16 = (bf16[256,256]{1,0:T(8,128)(2,1)S(1)}, bf16[256,256]{1,0:T(8,128)(2,1)S(1)}, u32[]{:S(2)}, u32[]{:S(2)}) collective-permute-start(bf16[256,256]{1,0:T(8,128)(2,1)S(1)} %merge.6.refs_0_), channel_id=1, source_target_pairs={{0,8},{8,0},{16,24},{24,16},{1,9},{9,1},{17,25},{25,17},{2,10},{10... | collective-permute-start | bytes 393224 | tf_op jit(solution)/shard_map/ppermute | solution.py:357
  50.8 0.5 collective-permute-start.12
  51.3 0.6 collective-permute-done.13.refs_3_
  51.9 1.5 %collective-permute-start.11 = (bf16[256,256]{1,0:T(8,128)(2,1)S(1)}, bf16[256,256]{1,0:T(8,128)(2,1)S(1)}, u32[]{:S(2)}, u32[]{:S(2)}) collective-permute-start(bf16[256,256]{1,0:T(8,128)(2,1)S(1)} %merge.5.refs_0_), channel_id=1, source_target_pairs={{0,8},{8,0},{16,24},{24,16},{1,9},{9,1},{17,25},{25,17},{2,10},{10... | collective-permute-start | bytes 393224 | tf_op jit(solution)/shard_map/ppermute | solution.py:357
  53.4 2.7 %output.4 = (f32[1024,256]{1,0:T(8,128)}, f32[1,128]{1,0:T(1,128)S(1)}) custom-call(s32[8]{0:T(128)S(1)} %get-tuple-element.17.after.home_ref, bf16[256,256]{1,0:T(8,128)(2,1)S(1)} %merge.7.refs_0_, bf16[256,256]{1,0:T(8,128)(2,1)S(1)} %collective-permute-done.19.refs_1_, bf16[256,256]{1,0:T(8,128)(2,1)S(1)} %collective-permute-done.20.refs_2_, ...), custom_call_target="tpu_custom_call" | custom-call | flops 1073741824 | bytes 2097152 | tf_op jit(solution)/shard_map/output/pallas_call | solution.py:494
  56.1 0.1 merge.4.refs_0_
  56.3 1.5 %collective-permute-start.5 = (bf16[256,256]{1,0:T(8,128)(2,1)S(1)}, bf16[256,256]{1,0:T(8,128)(2,1)S(1)}, u32[]{:S(2)}, u32[]{:S(2)}) collective-permute-start(bf16[256,256]{1,0:T(8,128)(2,1)S(1)} %merge.4.refs_0_), channel_id=1, source_target_pairs={{0,24},{8,16},{16,8},{24,0},{1,25},{9,17},{17,9},{25,1},{2,26},{10... | collective-permute-start | bytes 393224 | tf_op jit(solution)/shard_map/ppermute | solution.py:357
  57.8 0.5 collective-permute-start.4
  58.3 1.7 %collective-permute-start.3 = (bf16[256,256]{1,0:T(8,128)(2,1)S(1)}, bf16[256,256]{1,0:T(8,128)(2,1)S(1)}, u32[]{:S(2)}, u32[]{:S(2)}) collective-permute-start(bf16[256,256]{1,0:T(8,128)(2,1)S(1)} %merge.4.refs_0_), channel_id=1, source_target_pairs={{0,8},{8,0},{16,24},{24,16},{1,9},{9,1},{17,25},{25,17},{2,10},{10... | collective-permute-start | bytes 393224 | tf_op jit(solution)/shard_map/ppermute | solution.py:357
  60.0 2.6 %output.5 = (f32[1024,256]{1,0:T(8,128)}, f32[1,128]{1,0:T(1,128)S(1)}) custom-call(s32[8]{0:T(128)S(1)} %get-tuple-element.17.after.home_ref, bf16[256,256]{1,0:T(8,128)(2,1)S(1)} %merge.6.refs_0_, bf16[256,256]{1,0:T(8,128)(2,1)S(1)} %collective-permute-done.16.refs_1_, ...), custom_call_target="tpu_custom_call", output_to_operand_aliasing={{0}: (13, {})} | custom-call | flops 1073741824 | bytes 2097152 | tf_op jit(solution)/shard_map/output/pallas_call | solution.py:494
  62.6 2.6 %output.6 = (f32[1024,256]{1,0:T(8,128)}, f32[1,128]{1,0:T(1,128)S(1)}) custom-call(s32[8]{0:T(128)S(1)} %get-tuple-element.17.after.home_ref, bf16[256,256]{1,0:T(8,128)(2,1)S(1)} %merge.5.refs_0_, bf16[256,256]{1,0:T(8,128)(2,1)S(1)} %collective-permute-done.11.refs_1_, ...), custom_call_target="tpu_custom_call", output_to_operand_aliasing={{0}: (13, {})} | custom-call | flops 1073741824 | bytes 2097152 | tf_op jit(solution)/shard_map/output/pallas_call | solution.py:494
  65.3 3.1 %output.7 = (f32[1024,256]{1,0:T(8,128)}, f32[1,16]{1,0:T(1,128)}) custom-call(s32[8]{0:T(128)S(1)} %get-tuple-element.17.after.home_ref, bf16[256,256]{1,0:T(8,128)(2,1)S(1)} %merge.4.refs_0_, bf16[256,256]{1,0:T(8,128)(2,1)S(1)} %collective-permute-done.3.refs_1_, ...), custom_call_target="tpu_custom_call", output_to_operand_aliasing={{0}: (13, {})} | custom-call | flops 1073741824 | bytes 2097152 | tf_op jit(solution)/shard_map/output/pallas_call | solution.py:494
  (35 shorter events, 0.1 us)
Async XLA Ops:
  0.6 22.7 %copy-start.1 = (f32[264,128]{1,0:T(8,128)S(1)}, f32[264,128]{1,0:T(8,128)}, u32[]{:S(2)}) copy-start(f32[264,128]{1,0:T(8,128)} %constant.2.clone.refs_5_.table_ref) | copy-start | bytes 405508
  0.6 22.7 %copy-start.6 = (s32[8]{0:T(128)S(1)}, s32[8]{0:T(128)}, u32[]{:S(2)}) copy-start(s32[8]{0:T(128)} %query_len.9) | copy-start | bytes 100
  0.7 22.7 %copy-start = (bf16[1024,1024]{1,0:T(8,128)(2,1)S(1)}, bf16[1024,1024]{1,0:T(8,128)(2,1)}, u32[]{:S(2)}) copy-start(bf16[1024,1024]{1,0:T(8,128)(2,1)} %refs_8_.7) | copy-start | bytes 6291460
  0.7 22.7 %copy-start.9 = (s32[128]{0:T(128)S(1)}, s32[128]{0:T(128)}, u32[]{:S(2)}) copy-start(s32[128]{0:T(128)} %doc_query.1) | copy-start | bytes 1540
  0.7 22.7 %copy-start.8 = (s32[1024]{0:T(1024)S(1)}, s32[1024]{0:T(1024)}, u32[]{:S(2)}) copy-start(s32[1024]{0:T(1024)} %param.20) | copy-start | bytes 12292
  0.7 22.7 %copy-start.2 = (s32[1024]{0:T(1024)S(1)}, s32[1024]{0:T(1024)}, u32[]{:S(2)}) copy-start(s32[1024]{0:T(1024)} %param.18) | copy-start | bytes 12292
  0.7 22.7 %copy-start.5 = (f32[2,4]{1,0:T(2,128)S(1)}, f32[2,4]{1,0:T(2,128)}, u32[]{:S(2)}) copy-start(f32[2,4]{1,0:T(2,128)} %bias_ref.9) | copy-start | bytes 100
  0.7 22.7 %copy-start.11 = (bf16[1024,256]{1,0:T(8,128)(2,1)S(1)}, bf16[1024,256]{1,0:T(8,128)(2,1)}, u32[]{:S(2)}) copy-start(bf16[1024,256]{1,0:T(8,128)(2,1)} %wv_ref.1) | copy-start | bytes 1572868
  0.7 22.7 %copy-start.10 = (bf16[1024,256]{1,0:T(8,128)(2,1)S(1)}, bf16[1024,256]{1,0:T(8,128)(2,1)}, u32[]{:S(2)}) copy-start(bf16[1024,256]{1,0:T(8,128)(2,1)} %wk_ref.1) | copy-start | bytes 1572868
  5.7 17.6 %collective-permute-start.1 = (bf16[1040,256]{1,0:T(8,128)(2,1)S(1)}, bf16[1040,256]{1,0:T(8,128)(2,1)S(1)}, u32[]{:S(2)}, u32[]{:S(2)}) collective-permute-start(bf16[1040,256]{1,0:T(8,128)(2,1)S(1)} %get-tuple-element.19.after.own_ref), channel_id=1, source_target_pairs={{0,1},{1,0},{2,3},{3,2},{4,5},{5,4},{6,7},{7,6},{8,9},{9,8},{10,11... | collective-permute-start | bytes 1597448 | tf_op jit(solution)/shard_map/ppermute | solution.py:357
  6.2 30.5 %collective-permute-start.8 = (bf16[256,1024]{1,0:T(8,128)(2,1)S(1)}, bf16[256,1024]{1,0:T(8,128)(2,1)S(1)}, u32[]{:S(2)}, u32[]{:S(2)}) collective-permute-start(bf16[256,1024]{1,0:T(8,128)(2,1)S(1)} %get-tuple-element.23.refs_4_), channel_id=1, source_target_pairs={{0,24},{8,16},{16,8},{24,0},{1,25},{9,17},{17,9},{25,1},{2,26},{10... | collective-permute-start | bytes 1572872 | tf_op jit(solution)/shard_map/ppermute | solution.py:357
  9.7 29.5 %collective-permute-start.7 = (bf16[256,1024]{1,0:T(8,128)(2,1)S(1)}, bf16[256,1024]{1,0:T(8,128)(2,1)S(1)}, u32[]{:S(2)}, u32[]{:S(2)}) collective-permute-start(bf16[256,1024]{1,0:T(8,128)(2,1)S(1)} %get-tuple-element.23.refs_4_), channel_id=1, source_target_pairs={{0,16},{8,24},{16,0},{24,8},{1,17},{9,25},{17,1},{25,9},{2,18},{10... | collective-permute-start | bytes 1572872 | tf_op jit(solution)/shard_map/ppermute | solution.py:357
  10.2 29.5 %collective-permute-start.6 = (bf16[256,1024]{1,0:T(8,128)(2,1)S(1)}, bf16[256,1024]{1,0:T(8,128)(2,1)S(1)}, u32[]{:S(2)}, u32[]{:S(2)}) collective-permute-start(bf16[256,1024]{1,0:T(8,128)(2,1)S(1)} %get-tuple-element.23.refs_4_), channel_id=1, source_target_pairs={{0,8},{8,0},{16,24},{24,16},{1,9},{9,1},{17,25},{25,17},{2,10},{10... | collective-permute-start | bytes 1572872 | tf_op jit(solution)/shard_map/ppermute | solution.py:357
  10.3 9.4 %collective-permute-start.9 = (bf16[272,256]{1,0:T(8,128)(2,1)S(1)}, bf16[272,256]{1,0:T(8,128)(2,1)S(1)}, u32[]{:S(2)}, u32[]{:S(2)}) collective-permute-start(bf16[272,256]{1,0:T(8,128)(2,1)S(1)} %get-tuple-element.22.refs_2_), channel_id=1, source_target_pairs={{0,4},{1,5},{2,6},{3,7},{4,0},{5,1},{6,2},{7,3},{8,12},{9,13},{10,... | collective-permute-start | bytes 417800 | tf_op jit(solution)/shard_map/ppermute | solution.py:357
  19.7 13.0 %collective-permute-start = (bf16[272,256]{1,0:T(8,128)(2,1)S(1)}, bf16[272,256]{1,0:T(8,128)(2,1)S(1)}, u32[]{:S(2)}, u32[]{:S(2)}) collective-permute-start(bf16[272,256]{1,0:T(8,128)(2,1)S(1)} %get-tuple-element.18.refs_3_), channel_id=1, source_target_pairs={{0,6},{1,7},{2,4},{3,5},{4,2},{5,3},{6,0},{7,1},{8,14},{9,15},{10,... | collective-permute-start | bytes 417800 | tf_op jit(solution)/shard_map/ppermute | solution.py:357
  23.3 6.9 %collective-permute-start.14 = (bf16[272,256]{1,0:T(8,128)(2,1)S(1)}, bf16[272,256]{1,0:T(8,128)(2,1)S(1)}, u32[]{:S(2)}, u32[]{:S(2)}) collective-permute-start(bf16[272,256]{1,0:T(8,128)(2,1)S(1)} %get-tuple-element.21.refs_1_), channel_id=1, source_target_pairs={{0,2},{1,3},{2,0},{3,1},{4,6},{5,7},{6,4},{7,5},{8,10},{9,11},{10,... | collective-permute-start | bytes 417800 | tf_op jit(solution)/shard_map/ppermute | solution.py:357
  23.4 4.5 %copy-start.7 = (s32[8]{0:T(128)S(1)}, s32[8]{0:T(128)}, u32[]{:S(2)}) copy-start(s32[8]{0:T(128)} %block_perm.7) | copy-start | bytes 100
  30.2 12.0 %collective-permute-start.10 = (bf16[272,256]{1,0:T(8,128)(2,1)S(1)}, bf16[272,256]{1,0:T(8,128)(2,1)S(1)}, u32[]{:S(2)}, u32[]{:S(2)}) collective-permute-start(bf16[272,256]{1,0:T(8,128)(2,1)S(1)} %cache_part.5), channel_id=1, source_target_pairs={{0,4},{1,5},{2,6},{3,7},{4,0},{5,1},{6,2},{7,3},{8,12},{9,13},{10,... | collective-permute-start | bytes 417800 | tf_op jit(solution)/shard_map/ppermute | solution.py:357
  32.8 11.8 %collective-permute-start.15 = (bf16[272,256]{1,0:T(8,128)(2,1)S(1)}, bf16[272,256]{1,0:T(8,128)(2,1)S(1)}, u32[]{:S(2)}, u32[]{:S(2)}) collective-permute-start(bf16[272,256]{1,0:T(8,128)(2,1)S(1)} %cache_part.6), channel_id=1, source_target_pairs={{0,2},{1,3},{2,0},{3,1},{4,6},{5,7},{6,4},{7,5},{8,10},{9,11},{10,... | collective-permute-start | bytes 417800 | tf_op jit(solution)/shard_map/ppermute | solution.py:357
  36.6 16.8 %copy-start.3 = (f32[1024]{0:T(1024)S(1)}, f32[1024]{0:T(1024)}, u32[]{:S(2)}) copy-start(f32[1024]{0:T(1024)} %param.31) | copy-start | bytes 12292
  36.6 16.8 %copy-start.4 = (f32[1024]{0:T(1024)S(1)}, f32[1024]{0:T(1024)}, u32[]{:S(2)}) copy-start(f32[1024]{0:T(1024)} %param.32) | copy-start | bytes 12292
  36.7 10.6 %collective-permute-start.21 = (bf16[256,256]{1,0:T(8,128)(2,1)S(1)}, bf16[256,256]{1,0:T(8,128)(2,1)S(1)}, u32[]{:S(2)}, u32[]{:S(2)}) collective-permute-start(bf16[256,256]{1,0:T(8,128)(2,1)S(1)} %merge.7.refs_0_), channel_id=1, source_target_pairs={{0,24},{8,16},{16,8},{24,0},{1,25},{9,17},{17,9},{25,1},{2,26},{10... | collective-permute-start | bytes 393224 | tf_op jit(solution)/shard_map/ppermute | solution.py:357
  39.2 8.6 %collective-permute-start.20 = (bf16[256,256]{1,0:T(8,128)(2,1)S(1)}, bf16[256,256]{1,0:T(8,128)(2,1)S(1)}, u32[]{:S(2)}, u32[]{:S(2)}) collective-permute-start(bf16[256,256]{1,0:T(8,128)(2,1)S(1)} %merge.7.refs_0_), channel_id=1, source_target_pairs={{0,16},{8,24},{16,0},{24,8},{1,17},{9,25},{17,1},{25,9},{2,18},{10... | collective-permute-start | bytes 393224 | tf_op jit(solution)/shard_map/ppermute | solution.py:357
  39.7 9.6 %collective-permute-start.19 = (bf16[256,256]{1,0:T(8,128)(2,1)S(1)}, bf16[256,256]{1,0:T(8,128)(2,1)S(1)}, u32[]{:S(2)}, u32[]{:S(2)}) collective-permute-start(bf16[256,256]{1,0:T(8,128)(2,1)S(1)} %merge.7.refs_0_), channel_id=1, source_target_pairs={{0,8},{8,0},{16,24},{24,16},{1,9},{9,1},{17,25},{25,17},{2,10},{10... | collective-permute-start | bytes 393224 | tf_op jit(solution)/shard_map/ppermute | solution.py:357
  42.2 8.6 %collective-permute-start.2 = (bf16[272,256]{1,0:T(8,128)(2,1)S(1)}, bf16[272,256]{1,0:T(8,128)(2,1)S(1)}, u32[]{:S(2)}, u32[]{:S(2)}) collective-permute-start(bf16[272,256]{1,0:T(8,128)(2,1)S(1)} %cache_part.4), channel_id=1, source_target_pairs={{0,6},{1,7},{2,4},{3,5},{4,2},{5,3},{6,0},{7,1},{8,14},{9,15},{10,... | collective-permute-start | bytes 417800 | tf_op jit(solution)/shard_map/ppermute | solution.py:357
  44.6 7.3 %collective-permute-start.13 = (bf16[256,256]{1,0:T(8,128)(2,1)S(1)}, bf16[256,256]{1,0:T(8,128)(2,1)S(1)}, u32[]{:S(2)}, u32[]{:S(2)}) collective-permute-start(bf16[256,256]{1,0:T(8,128)(2,1)S(1)} %merge.5.refs_0_), channel_id=1, source_target_pairs={{0,24},{8,16},{16,8},{24,0},{1,25},{9,17},{17,9},{25,1},{2,26},{10... | collective-permute-start | bytes 393224 | tf_op jit(solution)/shard_map/ppermute | solution.py:357
  47.3 9.0 %collective-permute-start.18 = (bf16[256,256]{1,0:T(8,128)(2,1)S(1)}, bf16[256,256]{1,0:T(8,128)(2,1)S(1)}, u32[]{:S(2)}, u32[]{:S(2)}) collective-permute-start(bf16[256,256]{1,0:T(8,128)(2,1)S(1)} %merge.6.refs_0_), channel_id=1, source_target_pairs={{0,24},{8,16},{16,8},{24,0},{1,25},{9,17},{17,9},{25,1},{2,26},{10... | collective-permute-start | bytes 393224 | tf_op jit(solution)/shard_map/ppermute | solution.py:357
  47.8 10.0 %collective-permute-start.17 = (bf16[256,256]{1,0:T(8,128)(2,1)S(1)}, bf16[256,256]{1,0:T(8,128)(2,1)S(1)}, u32[]{:S(2)}, u32[]{:S(2)}) collective-permute-start(bf16[256,256]{1,0:T(8,128)(2,1)S(1)} %merge.6.refs_0_), channel_id=1, source_target_pairs={{0,16},{8,24},{16,0},{24,8},{1,17},{9,25},{17,1},{25,9},{2,18},{10... | collective-permute-start | bytes 393224 | tf_op jit(solution)/shard_map/ppermute | solution.py:357
  49.3 9.0 %collective-permute-start.16 = (bf16[256,256]{1,0:T(8,128)(2,1)S(1)}, bf16[256,256]{1,0:T(8,128)(2,1)S(1)}, u32[]{:S(2)}, u32[]{:S(2)}) collective-permute-start(bf16[256,256]{1,0:T(8,128)(2,1)S(1)} %merge.6.refs_0_), channel_id=1, source_target_pairs={{0,8},{8,0},{16,24},{24,16},{1,9},{9,1},{17,25},{25,17},{2,10},{10... | collective-permute-start | bytes 393224 | tf_op jit(solution)/shard_map/ppermute | solution.py:357
  50.8 11.8 %collective-permute-start.12 = (bf16[256,256]{1,0:T(8,128)(2,1)S(1)}, bf16[256,256]{1,0:T(8,128)(2,1)S(1)}, u32[]{:S(2)}, u32[]{:S(2)}) collective-permute-start(bf16[256,256]{1,0:T(8,128)(2,1)S(1)} %merge.5.refs_0_), channel_id=1, source_target_pairs={{0,16},{8,24},{16,0},{24,8},{1,17},{9,25},{17,1},{25,9},{2,18},{10... | collective-permute-start | bytes 393224 | tf_op jit(solution)/shard_map/ppermute | solution.py:357
  51.9 10.7 %collective-permute-start.11 = (bf16[256,256]{1,0:T(8,128)(2,1)S(1)}, bf16[256,256]{1,0:T(8,128)(2,1)S(1)}, u32[]{:S(2)}, u32[]{:S(2)}) collective-permute-start(bf16[256,256]{1,0:T(8,128)(2,1)S(1)} %merge.5.refs_0_), channel_id=1, source_target_pairs={{0,8},{8,0},{16,24},{24,16},{1,9},{9,1},{17,25},{25,17},{2,10},{10... | collective-permute-start | bytes 393224 | tf_op jit(solution)/shard_map/ppermute | solution.py:357
  56.3 9.0 %collective-permute-start.5 = (bf16[256,256]{1,0:T(8,128)(2,1)S(1)}, bf16[256,256]{1,0:T(8,128)(2,1)S(1)}, u32[]{:S(2)}, u32[]{:S(2)}) collective-permute-start(bf16[256,256]{1,0:T(8,128)(2,1)S(1)} %merge.4.refs_0_), channel_id=1, source_target_pairs={{0,24},{8,16},{16,8},{24,0},{1,25},{9,17},{17,9},{25,1},{2,26},{10... | collective-permute-start | bytes 393224 | tf_op jit(solution)/shard_map/ppermute | solution.py:357
  57.8 7.5 %collective-permute-start.4 = (bf16[256,256]{1,0:T(8,128)(2,1)S(1)}, bf16[256,256]{1,0:T(8,128)(2,1)S(1)}, u32[]{:S(2)}, u32[]{:S(2)}) collective-permute-start(bf16[256,256]{1,0:T(8,128)(2,1)S(1)} %merge.4.refs_0_), channel_id=1, source_target_pairs={{0,16},{8,24},{16,0},{24,8},{1,17},{9,25},{17,1},{25,9},{2,18},{10... | collective-permute-start | bytes 393224 | tf_op jit(solution)/shard_map/ppermute | solution.py:357
  58.3 7.0 %collective-permute-start.3 = (bf16[256,256]{1,0:T(8,128)(2,1)S(1)}, bf16[256,256]{1,0:T(8,128)(2,1)S(1)}, u32[]{:S(2)}, u32[]{:S(2)}) collective-permute-start(bf16[256,256]{1,0:T(8,128)(2,1)S(1)} %merge.4.refs_0_), channel_id=1, source_target_pairs={{0,8},{8,0},{16,24},{24,16},{1,9},{9,1},{17,25},{25,17},{2,10},{10... | collective-permute-start | bytes 393224 | tf_op jit(solution)/shard_map/ppermute | solution.py:357

commit v3 on v2

--- a/solution.py
+++ b/solution.py
@@ -20,6 +20,7 @@
 HBM = pl.BlockSpec(memory_space=pltpu.HBM)
 ANY = pl.BlockSpec(memory_space=pl.ANY)
 DMA = pltpu.SemaphoreType.DMA
+GROUPS = [[0, 1], [2], [3]]
 LIMIT = 32 * 1024 * 1024
 
 
@@ -109,21 +110,38 @@
 
 
 def query_kernel(bpq, chunks, *refs):
-    sources = refs[:8]
-    pick_ref, q_refs = refs[8], refs[9 : 9 + chunks]
-    targets = refs[9 + chunks : 17 + chunks]
-    base_ref, y_ref, sems = refs[17 + chunks :]
-    moves = copies(sources, targets, sems)
-    doc_query, query_len, block_perm, seg_ref, var_ref, table_ref, x_ref, w_ref = targets
+    sources, refs = refs[:11], refs[11:]
+    pick_ref, base_ref, usable_ref, packed_ref = refs[:4]
+    q_refs, refs = refs[4 : 4 + chunks], refs[4 + chunks :]
+    targets, (y_ref, sems) = list(refs[:10]), refs[10:]
+    rows, cols = sources[10].shape
+    moves = copies(sources, targets + [packed_ref.at[0:rows]], sems)
+    doc_query, query_len, block_perm, seg_ref, var_ref, table_ref, key_var_ref = targets[:7]
+    x_ref, w_ref, v_ref = targets[7:]
     slots, width = seg_ref.shape
     cos_ref, sin_ref = table_ref.at[0:width], table_ref.at[width : 2 * width]
     rows_ref = table_ref.at[2 * width :]
-    for move in moves[:6]:
+    for move in moves[:7]:
         move.wait()
     start_tables(doc_query, query_len, seg_ref, rows_ref, base_ref)
-    for move in moves[6:]:
+    row = lax.broadcasted_iota(jnp.int32, usable_ref.shape, 0)
+    usable = jnp.zeros(usable_ref.shape, jnp.int32)
+    for j in range(2):
+        block = block_perm[lax.axis_index("blk") ^ j]
+        here = query_len[block // bpq] - block % bpq * rows
+        usable = jnp.where(row == j, here, usable)
+    usable_ref[...] = usable
+    parts = rows // LANES
+    key_var = key_var_ref[...].astype(F32)
+    key_var = jnp.concatenate([key_var, jnp.zeros((EXTRA - parts, LANES), F32)], axis=0)
+    packed_ref[2 * rows :, :] = jnp.concatenate([key_var, key_var], axis=1).astype(BF)
+    for move in moves[7:9]:
         move.wait()
     y_ref[...] = dot(x_ref[...], w_ref[...])
+    moves[9].wait()
+    for i in range(rows // cols):
+        block = v_ref[i * cols : (i + 1) * cols, :].astype(F32)
+        packed_ref[rows + i * cols : rows + (i + 1) * cols, :] = block.T.astype(BF)
     for k, q_ref in enumerate(q_refs):
         for j in range(2):
             slot = slot_of(2 * k + j, doc_query, block_perm, slots, bpq)
@@ -136,25 +154,7 @@
             q_ref[2 * width :, j * width : (j + 1) * width] = jnp.broadcast_to(
                 var, (EXTRA, width)
             ).astype(BF)
-
-
-def pack_kernel(k_hbm, v_hbm, var_hbm, w_hbm, after, out_ref, w_ref, v_ref, var_ref, sems):
-    del after
-    rows, cols = v_ref.shape
-    moves = copies(
-        [v_hbm, var_hbm, k_hbm, w_hbm], [v_ref, var_ref, out_ref.at[0:rows], w_ref], sems
-    )
-    moves[0].wait()
-    for i in range(rows // cols):
-        block = v_ref[i * cols : (i + 1) * cols, :].astype(F32)
-        out_ref[rows + i * cols : rows + (i + 1) * cols, :] = block.T.astype(BF)
-    moves[1].wait()
-    parts = rows // LANES
-    var = var_ref[...].astype(F32)
-    var = jnp.concatenate([var, jnp.zeros((EXTRA - parts, LANES), F32)], axis=0)
-    out_ref[2 * rows :, :] = jnp.concatenate([var, var], axis=1).astype(BF)
-    for move in moves[2:]:
-        move.wait()
+    moves[10].wait()
 
 
 def by_head(query):
@@ -165,16 +165,23 @@
     )
 
 
+def fold(value, op):
+    while value.shape[0] > 8:
+        half = value.shape[0] // 2
+        value = op(value[:half], value[half:])
+    return value
+
+
 def attend(scores, same, allowed, bias_ref, values, out_ref, at):
     width = same.shape[1]
     stats = []
     for h in range(scores.shape[1] // width):
         part = scores[:, h * width : (h + 1) * width]
-        part = part + jnp.where(same, bias_ref[0, h], bias_ref[1, h])
+        part = part + jnp.where(same, bias_ref[0:1, h : h + 1], bias_ref[1:2, h : h + 1])
         part = jnp.where(allowed, part, NEVER)
-        peak = jnp.max(part, axis=0, keepdims=True)
+        peak = jnp.max(fold(part, jnp.maximum), axis=0, keepdims=True)
         weight = jnp.exp(part - peak)
-        total = jnp.sum(weight, axis=0, keepdims=True)
+        total = jnp.sum(fold(weight, jnp.add), axis=0, keepdims=True)
         weight = weight.astype(BF)
         mixed = None
         key = 0
@@ -189,17 +196,12 @@
     return stats
 
 
-def cache_kernel(
-    bpq, query_len, block_perm, bias_ref, q_ref, own_ref, other_ref, after, out_ref
-):
-    del after
-    blk = lax.axis_index("blk")
+def cache_kernel(usable_ref, bias_ref, q_ref, own_ref, other_ref, *refs):
+    out_ref = refs[-1]
     width = q_ref.shape[0] // 2 - EXTRA // 2
     cols = q_ref.shape[1]
     rows = (own_ref.shape[0] - EXTRA) // 2
     for j, ref in enumerate((own_ref, other_ref)):
-        block = block_perm[blk ^ j]
-        usable = query_len[block // bpq] - block % bpq * rows
         var = ref[2 * rows :, 0:LANES].astype(F32)
         var = jnp.concatenate([var, jnp.zeros((LANES - EXTRA, LANES), F32)], axis=0).T
         key_var = jnp.concatenate(
@@ -208,7 +210,7 @@
         )
         tok_var = q_ref[2 * width :, j * width : (j + 1) * width].astype(F32)[0:1, :]
         same = key_var == tok_var
-        allowed = lax.broadcasted_iota(jnp.int32, (rows, width), 0) < usable
+        allowed = lax.broadcasted_iota(jnp.int32, (rows, width), 0) < usable_ref[j : j + 1, :]
         scores = dot_t(ref[0:rows, :], by_head(q_ref[j * width : (j + 1) * width, :]))
         values = [ref[rows + i * cols : rows + (i + 1) * cols, :] for i in range(rows // cols)]
         at = slice(j * width, (j + 1) * width)
@@ -222,23 +224,26 @@
 
 
 def own_kernel(
-    doc_query, query_len, bias_ref, home_ref, x_ref, wk_ref, wv_ref, seg_ref, var_ref, table_ref,
-    after, *refs
+    home_any, bias_ref, x_ref, wk_ref, wv_ref, var_ref, table_ref, base_ref, after,
+    *refs
 ):
     del after
-    out_ref, base_ref, k_ref, v_ref = refs[-4:]
-    q_refs = refs[:-4]
-    slots, width = seg_ref.shape
+    out_ref, x_home_ref, k_ref, v_ref, home_ref, sem = refs[-6:]
+    q_refs = refs[:-6]
+    slots, width = var_ref.shape
     cols = wk_ref.shape[1]
+    home_move = pltpu.make_async_copy(home_any, home_ref, sem)
+    home_move.start()
     cos_ref, sin_ref = table_ref.at[0:width], table_ref.at[width : 2 * width]
     rows_ref = table_ref.at[2 * width :]
-    start_tables(doc_query, query_len, seg_ref, rows_ref, base_ref)
     k_ref[...] = dot(x_ref[...], wk_ref[...])
     v_ref[...] = dot(x_ref[...], wv_ref[...])
+    home_move.wait()
     for n in range(slots):
         slot = home_ref[n]
         cos, sin = slot_tables(slot, base_ref, cos_ref, sin_ref, rows_ref)
         at = pl.ds(pl.multiple_of(slot * width, width), width)
+        x_home_ref[n * width : (n + 1) * width, :] = x_ref[at, :]
         key = turn(k_ref[at, :], cos, sin).astype(BF)
         value = v_ref[at, :].T.astype(BF)
         query = q_refs[n // 2][n % 2 * width : (n % 2 + 1) * width, :]
@@ -256,7 +261,8 @@
 
 
 def merge_kernel(firsts, *refs):
-    own_ref, out_ref = refs[-2:]
+    own_ref, after, out_ref = refs[-3:]
+    del after
     for i, (first, got_ref) in enumerate(zip(firsts, refs)):
         cols = got_ref.shape[0] - EXTRA
         heads = cols // DH
@@ -281,24 +287,22 @@
             out_ref[to, :] = jnp.concatenate(parts, axis=0).T.astype(BF)
 
 
-def output_kernel(head_count, firsts, last, home_ref, *refs):
-    att_refs, w_refs = refs[:head_count], refs[head_count : 2 * head_count]
-    x_hbm, seg_ref, gain_ref, read_ref = refs[2 * head_count : 2 * head_count + 4]
-    before = refs[2 * head_count + 4 : -7]
-    update_hbm, pooled_ref, x_ref, gr_ref, out_ref, in_sems, out_sems = refs[-7:]
+def output_kernel(firsts, home_any, *refs):
+    att_refs, w_refs = refs[:4], refs[4:8]
+    x_ref, base_ref, gain_ref, read_ref = refs[8:12]
+    before = refs[12:-6]
+    update_hbm, pooled_ref, gr_ref, out_ref, home_ref, sems = refs[-6:]
     tokens, cols = att_refs[0].shape
     depth = w_refs[0].shape[1]
     width = tokens // (2 * len(firsts))
     places = [first + j for first in firsts for j in range(2)]
-    found = [home_ref[place] for place in places]
-    slots = [pl.ds(pl.multiple_of(slot * width, width), width) for slot in found]
     here = [slice(i * width, (i + 1) * width) for i in range(len(places))]
-    reads = copies([x_hbm.at[at] for at in slots], [x_ref.at[at] for at in here], in_sems)
+    home_move = pltpu.make_async_copy(home_any, home_ref, sems.at[len(places)])
+    home_move.start()
     gr_ref[...] = gain_ref[...] * read_ref[...]
     head = lax.axis_index("head")
-    square = jnp.zeros((tokens, 1), F32)
-    weighted = jnp.zeros((tokens, 1), F32)
-    writes = []
+    square = jnp.zeros((tokens, LANES), F32)
+    weighted = jnp.zeros((tokens, LANES), F32)
     for c in range(depth // cols):
         start = (head + c) % (depth // cols) * cols
         at = pl.ds(pl.multiple_of(start, cols), cols)
@@ -307,34 +311,38 @@
             total = total + dot(att_ref[...], w_ref[:, at])
         if c == 0:
             out_ref[...] = total
+            home_move.wait()
+            found = [home_ref[place] for place in places]
+            slots = [pl.ds(pl.multiple_of(slot * width, width), width) for slot in found]
             writes = copies(
-                [out_ref.at[row] for row in here], [update_hbm.at[row] for row in slots], out_sems
+                [out_ref.at[row] for row in here], [update_hbm.at[row] for row in slots], sems
             )
-            for read in reads:
-                read.wait()
-        hidden = x_ref[:, at].astype(F32) + total
-        square = square + jnp.sum(hidden * hidden, axis=1, keepdims=True)
-        weighted = weighted + jnp.sum(hidden * gr_ref[:, at], axis=1, keepdims=True)
+        hidden = x_ref[places[0] * width : (places[-1] + 1) * width, at].astype(F32) + total
+        scaled = hidden * gr_ref[:, at]
+        hidden = hidden * hidden
+        for lane in range(0, cols, LANES):
+            square = square + hidden[:, lane : lane + LANES]
+            weighted = weighted + scaled[:, lane : lane + LANES]
+    square = jnp.sum(square, axis=1, keepdims=True)
+    weighted = jnp.sum(weighted, axis=1, keepdims=True)
     score = weighted * lax.rsqrt(square / depth + 1e-06)
     token = lax.broadcasted_iota(jnp.int32, (width, 1), 0).astype(F32)
     lane = lax.broadcasted_iota(jnp.int32, (1, LANES), 1)
     pooled = before[1][...] if before else jnp.zeros((1, LANES), F32)
     for slot, row in zip(found, here):
-        second = (seg_ref[pl.ds(slot, 1), :] & 1).astype(F32)
-        count_two = jnp.sum(second, axis=1, keepdims=True)
-        count_one = width - count_two
+        count_one = base_ref[4, pl.ds(slot, 1), 0:1]
         is_first = token < count_one
         part = score[row, :]
-        mean_one = jnp.sum(jnp.where(is_first, part, 0.0), axis=0, keepdims=True) / count_one
-        mean_two = jnp.sum(jnp.where(is_first, 0.0, part), axis=0, keepdims=True) / count_two
-        pooled = jnp.where(lane == 2 * slot, mean_one, pooled)
-        pooled = jnp.where(lane == 2 * slot + 1, mean_two, pooled)
+        sum_one = jnp.sum(jnp.where(is_first, part, 0.0), axis=0, keepdims=True)
+        sum_two = jnp.sum(jnp.where(is_first, 0.0, part), axis=0, keepdims=True)
+        pooled = jnp.where(lane == 2 * slot, sum_one / count_one, pooled)
+        pooled = jnp.where(lane == 2 * slot + 1, sum_two / (width - count_one), pooled)
     pooled_ref[...] = pooled[:, : pooled_ref.shape[1]]
     for write in writes:
         write.wait()
 
 
-def call(kernel, out, ins, scratch=(), flops=0, bytes_accessed=0, **kwargs):
+def call(kernel, out, ins, scratch=(), work=1, **kwargs):
     return pl.pallas_call(
         kernel,
         out_shape=out,
@@ -342,19 +350,28 @@
         scratch_shapes=list(scratch),
         compiler_params=pltpu.CompilerParams(vmem_limit_bytes=LIMIT),
         cost_estimate=pl.CostEstimate(
-            flops=flops, bytes_accessed=bytes_accessed, transcendentals=0
+            flops=int(work * 1e9), bytes_accessed=0, transcendentals=0
         ),
         **kwargs,
     )
 
 
 def in_hbm(*arrays):
-    return [pltpu.with_memory_space_constraint(array, pltpu.HBM) for array in arrays]
+    return [pltpu.with_memory_space_constraint(jnp.asarray(a), pltpu.HBM) for a in arrays]
 
 
 def partner(value, axis, k):
     count = lax.axis_size(axis)
     return lax.ppermute(value, axis, [(i, i ^ k) for i in range(count)])
+
+
+def hop(value, even, odd):
+    heads, blocks = lax.axis_size("head"), lax.axis_size("blk")
+    pairs = []
+    for h in range(heads):
+        for b in range(blocks):
+            pairs.append((h * blocks + b, (h ^ (odd if b % 2 else even)) * blocks + b))
+    return lax.ppermute(value, ("head", "blk"), pairs)
 
 
 def spread_merge(backs, own, pick, slots, bpq):
@@ -384,7 +401,6 @@
     rows, depth = doc_x.shape
     cols = w_query.shape[1]
     blocks = lax.axis_size("blk")
-    head_count = lax.axis_size("head")
     bpq = blocks // QUERIES
     slots = QUERIES
     width = rows // slots
@@ -397,37 +413,37 @@
     sds = jax.ShapeDtypeStruct
     i32 = jnp.int32
     chunk_shape = sds((2 * width + EXTRA, cols), BF)
-    base = pltpu.VMEM((5, slots, width), F32)
-
-    pick, *queries = call(
+    base_shape = sds((5, slots, width), F32)
+
+    w_first = hop(w_out, 1, 2)
+    w_second = partner(w_first, "blk", 1)
+    w_third = hop(w_first, 2, 1)
+
+    pick, base, usable, packed, *queries = call(
         functools.partial(query_kernel, bpq, chunks),
-        [sds((blocks,), i32)] + [chunk_shape] * chunks,
-        [HBM] * 8,
+        [
+            sds((blocks,), i32), base_shape, sds((8, width), i32),
+            sds((2 * cache_rows + EXTRA, cols), BF),
+        ]
+        + [chunk_shape] * chunks,
+        [HBM] * 11,
         [pltpu.SMEM(ref.shape, i32) for ref in (doc_query, query_len, block_perm)]
-        + [
-            pltpu.VMEM(seg.shape, i32), pltpu.VMEM(var.shape, i32),
-            pltpu.VMEM(table.shape, F32), pltpu.VMEM(doc_x.shape, BF),
-            pltpu.VMEM(w_query.shape, BF), base, pltpu.VMEM((rows, cols), F32), DMA((8,)),
-        ],
-        flops=2 * rows * depth * cols,
-        bytes_accessed=2 * rows * depth,
-        out_specs=[SMEM] + [VMEM] * chunks,
+        + [pltpu.VMEM(ref.shape, i32) for ref in (seg, var)]
+        + [pltpu.VMEM(table.shape, F32), pltpu.VMEM(cache_var.shape, i32)]
+        + [pltpu.VMEM(ref.shape, BF) for ref in (doc_x, w_query, cache_v)]
+        + [pltpu.VMEM((rows, cols), F32), DMA((11,))],
+        out_specs=[SMEM] + [VMEM] * (chunks + 3),
+        work=3.5,
         name="query",
-    )(*in_hbm(doc_query, query_len, block_perm, seg, var, jnp.asarray(table), doc_x, w_query))
+    )(
+        *in_hbm(
+            doc_query, query_len, block_perm, seg, var, table, cache_var, doc_x, w_query,
+            cache_v, cache_k,
+        )
+    )
 
     asked = [queries[0]] + [partner(queries[k], "blk", 2 * k) for k in range(1, chunks)]
-
-    packed, w_own = call(
-        pack_kernel,
-        [sds((2 * cache_rows + EXTRA, cols), BF), sds(w_out.shape, BF)],
-        [HBM] * 4 + [ANY],
-        [pltpu.VMEM(cache_v.shape, BF), pltpu.VMEM(cache_var.shape, i32), DMA((4,))],
-        bytes_accessed=8 * cache_rows * cols,
-        out_specs=[VMEM, VMEM],
-        name="pack",
-    )(*in_hbm(cache_k, cache_v, cache_var, w_out), pick)
     packed_other = partner(packed, "blk", 1)
-    w_parts = [w_own] + [partner(w_own, "head", r) for r in range(1, head_count)]
 
     if bpq == 1:
         home = pick
@@ -440,45 +456,46 @@
             every[2 * k : 2 * k + 2].reshape(2 * width, cols) for k in range(slots // 2)
         ]
 
-    own = call(
+    own, x_home = call(
         own_kernel,
-        sds((slots, cols + 8, width), F32),
-        [SMEM] * 4 + [VMEM] * 6 + [ANY] + [VMEM] * len(home_queries),
-        [base, pltpu.VMEM((rows, cols), F32), pltpu.VMEM((rows, cols), F32)],
-        flops=6 * rows * depth * cols,
-        bytes_accessed=8 * rows * depth,
-        out_specs=VMEM,
+        [sds((slots, cols + 8, width), F32), sds((rows, depth), BF)],
+        [ANY] + [VMEM] * 7 + [ANY] + [VMEM] * len(home_queries),
+        [
+            pltpu.VMEM((rows, cols), F32), pltpu.VMEM((rows, cols), F32),
+            pltpu.SMEM(home.shape, i32), DMA,
+        ],
+        out_specs=[VMEM] * 2,
+        work=4.0,
         name="own_documents",
-    )(
-        doc_query, query_len, var_bias, home, doc_x, w_key, w_value, seg, var, table, packed,
-        *home_queries,
-    )
-
-    def from_cache(query):
-        return call(
-            functools.partial(cache_kernel, bpq),
+    )(home, var_bias, doc_x, w_key, w_value, var, table, base, packed_other, *home_queries)
+
+    parts = []
+    for k, query in enumerate(asked):
+        after = [parts[-1] if parts else own]
+        if k == chunks - 1:
+            after += [w_second, w_third]
+        part = call(
+            cache_kernel,
             chunk_shape,
-            [SMEM] * 3 + [VMEM] * 3 + [ANY],
-            flops=16 * width * cache_rows * cols,
-            bytes_accessed=8 * cache_rows * cols,
+            [VMEM] * 5 + [ANY] * len(after),
             out_specs=VMEM,
+            work=1.5,
             name="cache_part",
-        )(query_len, block_perm, var_bias, query, packed, packed_other, own)
-
-    parts = [from_cache(query) for query in asked]
+        )(usable, var_bias, query, packed, packed_other, *after)
+        parts.append(part)
     backs = [parts[0]] + [partner(parts[k], "blk", 2 * k) for k in range(1, chunks)]
 
-    groups = [[k] for k in range(slots // 2)]
+    groups = GROUPS
     if bpq == 1:
         attended = [
             call(
                 functools.partial(merge_kernel, [2 * k for k in group]),
                 sds((2 * width * len(group), cols), BF),
-                [VMEM] * (len(group) + 1),
-                bytes_accessed=4 * rows * cols,
+                [VMEM] * (len(group) + 1) + [ANY],
                 out_specs=VMEM,
-                name="merge",
-            )(*[backs[k] for k in group], own)
+                work=0.2,
+            name="merge",
+            )(*[backs[k] for k in group], own, parts[-1])
             for group in groups
         ]
     else:
@@ -488,23 +505,23 @@
     gain, read = norm_gain.reshape(1, depth), readout.reshape(1, depth)
     chained = []
     for group, own_part in zip(groups, attended):
-        atts = [own_part] + [partner(own_part, "head", r) for r in range(1, head_count)]
+        near = hop(own_part, 1, 2)
+        atts = [own_part, near, hop(own_part, 2, 1), hop(near, 2, 1)]
         places = 2 * len(group)
         last = group is groups[-1]
         chained = call(
-            functools.partial(output_kernel, head_count, [2 * k for k in group], last),
+            functools.partial(output_kernel, [2 * k for k in group]),
             [sds((rows, cols), F32), sds((1, 2 * slots if last else LANES), F32)],
-            [SMEM] + [VMEM] * (2 * head_count) + [HBM] + [VMEM] * 3 + [HBM, VMEM][: len(chained)],
+            [ANY] + [VMEM] * 12 + [HBM, VMEM][: len(chained)],
             [
-                pltpu.VMEM((places * width, depth), BF), pltpu.VMEM((1, depth), F32),
-                pltpu.VMEM((places * width, cols), F32), DMA((places,)), DMA((places,)),
+                pltpu.VMEM((1, depth), F32), pltpu.VMEM((places * width, cols), F32),
+                pltpu.SMEM(home.shape, i32), DMA((places + 1,)),
             ],
-            flops=4 * places * width * depth * depth,
-            bytes_accessed=2 * depth * depth,
             out_specs=[HBM, VMEM],
-            input_output_aliases={5 + 2 * head_count: 0} if chained else {},
+            input_output_aliases={13: 0} if chained else {},
+            work=2.5,
             name="output",
-        )(home, *atts, *w_parts, *in_hbm(doc_x), seg, gain, read, *chained)
+        )(home, *atts, w_out, w_first, w_second, w_third, x_home, base, gain, read, *chained)
     update, pooled = chained
     return (update, pooled.reshape(2 * slots))
 

time: 68.8 us -> 63.4 us (0.922)
  waiting for transfers between devices: 7.39 us -> 14.2 us
  Pallas kernels: 28.9 us -> 22.9 us
  starting transfers between devices: 31.1 us -> 25.2 us
    ppermute x22 -> x8, starting transfers between devices: 31.1 us -> 10.5 us  [partner(): return lax.ppermute(value, axis, [(i, i ^ k) for i in range(count)])]
    ppermute x0 -> x11, starting transfers between devices: none -> 14.7 us  [hop(): return lax.ppermute(value, ('head', 'blk'), pairs)]
    ppermute x0 -> x11, waiting for transfers between devices: none -> 6.73 us  [hop(): return lax.ppermute(value, ('head', 'blk'), pairs)]
    pallas_call x11 -> x9, Pallas kernels: 28.3 us -> 22.4 us  [the longest x3 8.32 us: body(): call(functools.partial(output_kernel, [2 * k for k in group]), [sds((rows...]
    ppermute x22 -> x8, waiting for transfers between devices: 7.39 us -> 7.43 us  [partner(): return lax.ppermute(value, axis, [(i, i ^ k) for i in range(count)])]
  transfers between devices with their start and end apart: 22 -> 19, of which waited for: 3 -> 6; matrix products, arithmetic and copies ran while one was open for 0% -> 0% of each run, Pallas kernels for 30% -> 25%
where the time goes in v3:
time: 63.4 us; the launch traced here: 63.3 us
  starting transfers between devices  25.2 us (40%)
  Pallas kernels  22.9 us (36%)
  waiting for transfers between devices  14.2 us (22%)
  between operations  1.07 us (2%)
    ppermute x11, starting transfers between devices, hop(): return lax.ppermute(value, ('head', 'blk'), pairs)  14.7 us
    ppermute x8, starting transfers between devices, partner(): return lax.ppermute(value, axis, [(i, i ^ k) for i in range(count)])  10.5 us
    pallas_call x3, Pallas kernels, body(): call(functools.partial(output_kernel, [2 * k for k in group]), [sds((rows...  8.32 us
    ppermute x8, waiting for transfers between devices, partner(): return lax.ppermute(value, axis, [(i, i ^ k) for i in range(count)])  7.43 us
    ppermute x11, waiting for transfers between devices, hop(): return lax.ppermute(value, ('head', 'blk'), pairs)  6.73 us
    pallas_call x4, Pallas kernels, body(): call(cache_kernel, chunk_shape, [VMEM] * 5 + [ANY] * len(after), out_spec...  6.04 us
    pallas_call x1, Pallas kernels, body(): call(functools.partial(query_kernel, bpq, chunks), [sds((blocks,), i32),...  4.1 us
    pallas_call x1, Pallas kernels, body(): call(own_kernel, [sds((slots, cols + 8, width), F32), sds((rows, depth),...  3.94 us
  transfers between devices with their start and end apart: 19, of which 6 were waited for; matrix products, arithmetic and copies ran while one was open for 0% of the time, Pallas kernels for 25%

profile of v3, /device:TPU:0, one launch (start us, length us, event | category | flops | bytes accessed | tf_op | source)
XLA Modules:
  0.0 63.3 jit_solution(8966393695047343066)
XLA Ops:
  0.7 0.0 copy-start.8
  0.7 4.1 %query.1 = (s32[8]{0:T(128)S(1)}, f32[5,8,128]{2,1,0:T(8,128)S(1)}, s32[8,128]{1,0:T(8,128)S(1)}, bf16[1040,256]{1,0:T(8,128)(2,1)S(1)}, bf16[272,256]{1,0:T(8,1...) custom-call(s32[128]{0:T(128)} %refs_0_.1, s32[8]{0:T(128)} %refs_1_.1, ...), custom_call_target="tpu_custom_call" | custom-call | flops 3500000000 | tf_op jit(solution)/shard_map/query/pallas_call | solution.py:422
  4.8 0.5 collective-permute-start.1
  5.3 2.6 %collective-permute-start.4 = (bf16[256,1024]{1,0:T(8,128)(2,1)S(1)}, bf16[256,1024]{1,0:T(8,128)(2,1)S(1)}, u32[]{:S(2)}, u32[]{:S(2)}) collective-permute-start(bf16[256,1024]{1,0:T(8,128)(2,1)S(1)} %copy-done.3), channel_id=1, source_target_pairs={{0,8},{1,17},{2,10},{3,19},{4,12},{5,21},{6,14},{7,23},{8,0},{9,25... | collective-permute-start | bytes 1572872 | tf_op jit(solution)/shard_map/ppermute | solution.py:374
  7.9 3.6 %collective-permute-start = (bf16[272,256]{1,0:T(8,128)(2,1)S(1)}, bf16[272,256]{1,0:T(8,128)(2,1)S(1)}, u32[]{:S(2)}, u32[]{:S(2)}) collective-permute-start(bf16[272,256]{1,0:T(8,128)(2,1)S(1)} %get-tuple-element.20.refs_3_), channel_id=1, source_target_pairs={{0,6},{1,7},{2,4},{3,5},{4,2},{5,3},{6,0},{7,1},{8,14},{9,15},{10,... | collective-permute-start | bytes 417800 | tf_op jit(solution)/shard_map/ppermute | solution.py:365
  11.5 0.0 collective-permute-start.2
  11.5 0.8 %collective-permute-start.3 = (bf16[272,256]{1,0:T(8,128)(2,1)S(1)}, bf16[272,256]{1,0:T(8,128)(2,1)S(1)}, u32[]{:S(2)}, u32[]{:S(2)}) collective-permute-start(bf16[272,256]{1,0:T(8,128)(2,1)S(1)} %get-tuple-element.23.refs_1_), channel_id=1, source_target_pairs={{0,2},{1,3},{2,0},{3,1},{4,6},{5,7},{6,4},{7,5},{8,10},{9,11},{10,... | collective-permute-start | bytes 417800 | tf_op jit(solution)/shard_map/ppermute | solution.py:365
  12.3 2.8 %collective-permute-done.4.refs_5_ = bf16[256,1024]{1,0:T(8,128)(2,1)S(1)} collective-permute-done((bf16[256,1024]{1,0:T(8,128)(2,1)S(1)}, bf16[256,1024]{1,0:T(8,128)(2,1)S(1)}, u32[]{:S(2)}, u32[]{:S(2)}) %collective-permute-start.4) | collective-permute-done | bytes 524320 | tf_op jit(solution)/shard_map/ppermute | solution.py:374
  15.1 2.0 %collective-permute-start.6 = (bf16[256,1024]{1,0:T(8,128)(2,1)S(1)}, bf16[256,1024]{1,0:T(8,128)(2,1)S(1)}, u32[]{:S(2)}, u32[]{:S(2)}) collective-permute-start(bf16[256,1024]{1,0:T(8,128)(2,1)S(1)} %collective-permute-done.4.refs_5_), channel_id=1, source_target_pairs={{0,16},{1,9},{2,18},{3,11},{4,20},{5,13},{6,22},{7,15},{8,24},{9,1... | collective-permute-start | bytes 1572872 | tf_op jit(solution)/shard_map/ppermute | solution.py:374
  17.1 0.0 collective-permute-done.1.after.other_ref
  17.2 3.9 %own_documents.1 = (f32[8,264,128]{2,1,0:T(8,128)S(1)}, bf16[1024,1024]{1,0:T(8,128)(2,1)S(1)}) custom-call(s32[8]{0:T(128)S(1)} %get-tuple-element.18.home_any, f32[2,4]{1,0:T(2,128)S(1)} %copy-done.7, bf16[1024,1024]{1,0:T(8,128)(2,1)S(1)} %copy-done, bf16[1024,256]{1,0:T(8,128)(2,1)S(1)} %copy-done.1, bf16[1024,256]{1,0:T(8,128)(2,1)S(1)} %copy-done.2, ...), custom_call_target="tpu_custom_call" | custom-call | flops 4000000000 | tf_op jit(solution)/shard_map/own_documents/pallas_call | solution.py:459
  21.1 1.5 %cache_part.4.refs_0_ = bf16[272,256]{1,0:T(8,128)(2,1)S(1)} custom-call(s32[8,128]{1,0:T(8,128)S(1)} %get-tuple-element.19.usable_ref, f32[2,4]{1,0:T(2,128)S(1)} %copy-done.7, bf16[272,256]{1,0:T(8,128)(2,1)S(1)} %get-tuple-element.24.refs_0_.q_ref, bf16[1040,256]{1,0:T(8,128)(2,1)S(1)} %get-tuple-element.21.own_ref, ...), custom_call_target="tpu_custom_call" | custom-call | flops 1500000000 | tf_op jit(solution)/shard_map/cache_part/pallas_call | solution.py:477
  22.6 0.0 collective-permute-done.3.q_ref
  22.7 1.5 %cache_part.5.refs_0_ = bf16[272,256]{1,0:T(8,128)(2,1)S(1)} custom-call(s32[8,128]{1,0:T(8,128)S(1)} %get-tuple-element.19.usable_ref, f32[2,4]{1,0:T(2,128)S(1)} %copy-done.7, bf16[272,256]{1,0:T(8,128)(2,1)S(1)} %collective-permute-done.3.q_ref, bf16[1040,256]{1,0:T(8,128)(2,1)S(1)} %get-tuple-element.21.own_ref, ...), custom_call_target="tpu_custom_call" | custom-call | flops 1500000000 | tf_op jit(solution)/shard_map/cache_part/pallas_call | solution.py:477
  24.2 1.6 %collective-permute-start.15 = (bf16[272,256]{1,0:T(8,128)(2,1)S(1)}, bf16[272,256]{1,0:T(8,128)(2,1)S(1)}, u32[]{:S(2)}, u32[]{:S(2)}) collective-permute-start(bf16[272,256]{1,0:T(8,128)(2,1)S(1)} %cache_part.5.refs_0_), channel_id=1, source_target_pairs={{0,2},{1,3},{2,0},{3,1},{4,6},{5,7},{6,4},{7,5},{8,10},{9,11},{10,... | collective-permute-start | bytes 417800 | tf_op jit(solution)/shard_map/ppermute | solution.py:365
  25.8 0.0 collective-permute-done.2.q_ref
  25.8 1.5 %cache_part.6.refs_0_ = bf16[272,256]{1,0:T(8,128)(2,1)S(1)} custom-call(s32[8,128]{1,0:T(8,128)S(1)} %get-tuple-element.19.usable_ref, f32[2,4]{1,0:T(2,128)S(1)} %copy-done.7, bf16[272,256]{1,0:T(8,128)(2,1)S(1)} %collective-permute-done.2.q_ref, bf16[1040,256]{1,0:T(8,128)(2,1)S(1)} %get-tuple-element.21.own_ref, ...), custom_call_target="tpu_custom_call" | custom-call | flops 1500000000 | tf_op jit(solution)/shard_map/cache_part/pallas_call | solution.py:477
  27.3 0.0 collective-permute-done.q_ref
  27.3 0.0 collective-permute-done.6.refs_2_.refs_7_
  27.3 1.5 %cache_part.7.refs_2_.refs_3_ = bf16[272,256]{1,0:T(8,128)(2,1)S(1)} custom-call(s32[8,128]{1,0:T(8,128)S(1)} %get-tuple-element.19.usable_ref, f32[2,4]{1,0:T(2,128)S(1)} %copy-done.7, bf16[272,256]{1,0:T(8,128)(2,1)S(1)} %collective-permute-done.q_ref, bf16[1040,256]{1,0:T(8,128)(2,1)S(1)} %get-tuple-element.21.own_ref, ...), custom_call_target="tpu_custom_call" | custom-call | flops 1500000000 | tf_op jit(solution)/shard_map/cache_part/pallas_call | solution.py:477
  28.9 0.0 copy-start.5
  28.9 0.0 copy-start.6
  28.9 1.4 %collective-permute-done.15.refs_1_ = bf16[272,256]{1,0:T(8,128)(2,1)S(1)} collective-permute-done((bf16[272,256]{1,0:T(8,128)(2,1)S(1)}, bf16[272,256]{1,0:T(8,128)(2,1)S(1)}, u32[]{:S(2)}, u32[]{:S(2)}) %collective-permute-start.15) | collective-permute-done | bytes 139296 | tf_op jit(solution)/shard_map/ppermute | solution.py:365
  30.3 0.2 merge.5.refs_0_
  30.5 1.6 %collective-permute-start.16 = (bf16[512,256]{1,0:T(8,128)(2,1)S(1)}, bf16[512,256]{1,0:T(8,128)(2,1)S(1)}, u32[]{:S(2)}, u32[]{:S(2)}) collective-permute-start(bf16[512,256]{1,0:T(8,128)(2,1)S(1)} %merge.5.refs_0_), channel_id=1, source_target_pairs={{0,8},{1,17},{2,10},{3,19},{4,12},{5,21},{6,14},{7,23},{8,0},{9,25... | collective-permute-start | bytes 786440 | tf_op jit(solution)/shard_map/ppermute | solution.py:374
  32.1 2.6 %collective-permute-start.11 = (bf16[272,256]{1,0:T(8,128)(2,1)S(1)}, bf16[272,256]{1,0:T(8,128)(2,1)S(1)}, u32[]{:S(2)}, u32[]{:S(2)}) collective-permute-start(bf16[272,256]{1,0:T(8,128)(2,1)S(1)} %cache_part.6.refs_0_), channel_id=1, source_target_pairs={{0,4},{1,5},{2,6},{3,7},{4,0},{5,1},{6,2},{7,3},{8,12},{9,13},{10,... | collective-permute-start | bytes 417800 | tf_op jit(solution)/shard_map/ppermute | solution.py:365
  34.6 1.3 %collective-permute-start.7 = (bf16[272,256]{1,0:T(8,128)(2,1)S(1)}, bf16[272,256]{1,0:T(8,128)(2,1)S(1)}, u32[]{:S(2)}, u32[]{:S(2)}) collective-permute-start(bf16[272,256]{1,0:T(8,128)(2,1)S(1)} %cache_part.7.refs_2_.refs_3_), channel_id=1, source_target_pairs={{0,6},{1,7},{2,4},{3,5},{4,2},{5,3},{6,0},{7,1},{8,14},{9,15},{10,... | collective-permute-start | bytes 417800 | tf_op jit(solution)/shard_map/ppermute | solution.py:365
  36.0 0.5 collective-permute-start.17
  36.5 0.9 %collective-permute-done.16.refs_1_ = bf16[512,256]{1,0:T(8,128)(2,1)S(1)} collective-permute-done((bf16[512,256]{1,0:T(8,128)(2,1)S(1)}, bf16[512,256]{1,0:T(8,128)(2,1)S(1)}, u32[]{:S(2)}, u32[]{:S(2)}) %collective-permute-start.16) | collective-permute-done | bytes 262176 | tf_op jit(solution)/shard_map/ppermute | solution.py:374
  37.4 0.6 collective-permute-start.18
  38.0 6.0 %collective-permute-done.11.refs_0_ = bf16[272,256]{1,0:T(8,128)(2,1)S(1)} collective-permute-done((bf16[272,256]{1,0:T(8,128)(2,1)S(1)}, bf16[272,256]{1,0:T(8,128)(2,1)S(1)}, u32[]{:S(2)}, u32[]{:S(2)}) %collective-permute-start.11) | collective-permute-done | bytes 139296 | tf_op jit(solution)/shard_map/ppermute | solution.py:365
  44.0 0.1 merge.4.refs_0_
  44.2 1.6 %collective-permute-start.12 = (bf16[256,256]{1,0:T(8,128)(2,1)S(1)}, bf16[256,256]{1,0:T(8,128)(2,1)S(1)}, u32[]{:S(2)}, u32[]{:S(2)}) collective-permute-start(bf16[256,256]{1,0:T(8,128)(2,1)S(1)} %merge.4.refs_0_), channel_id=1, source_target_pairs={{0,8},{1,17},{2,10},{3,19},{4,12},{5,21},{6,14},{7,23},{8,0},{9,25... | collective-permute-start | bytes 393224 | tf_op jit(solution)/shard_map/ppermute | solution.py:374
  45.8 0.0 collective-permute-done.7.refs_0_
  45.8 0.1 merge.3.refs_0_
  46.0 0.5 collective-permute-start.8
  46.5 1.6 %collective-permute-start.13 = (bf16[256,256]{1,0:T(8,128)(2,1)S(1)}, bf16[256,256]{1,0:T(8,128)(2,1)S(1)}, u32[]{:S(2)}, u32[]{:S(2)}) collective-permute-start(bf16[256,256]{1,0:T(8,128)(2,1)S(1)} %merge.4.refs_0_), channel_id=1, source_target_pairs={{0,16},{1,9},{2,18},{3,11},{4,20},{5,13},{6,22},{7,15},{8,24},{9,1... | collective-permute-start | bytes 393224 | tf_op jit(solution)/shard_map/ppermute | solution.py:374
  48.1 2.2 %collective-permute-done.12.refs_1_ = bf16[256,256]{1,0:T(8,128)(2,1)S(1)} collective-permute-done((bf16[256,256]{1,0:T(8,128)(2,1)S(1)}, bf16[256,256]{1,0:T(8,128)(2,1)S(1)}, u32[]{:S(2)}, u32[]{:S(2)}) %collective-permute-start.12) | collective-permute-done | bytes 131104 | tf_op jit(solution)/shard_map/ppermute | solution.py:374
  50.3 1.7 %collective-permute-start.14 = (bf16[256,256]{1,0:T(8,128)(2,1)S(1)}, bf16[256,256]{1,0:T(8,128)(2,1)S(1)}, u32[]{:S(2)}, u32[]{:S(2)}) collective-permute-start(bf16[256,256]{1,0:T(8,128)(2,1)S(1)} %collective-permute-done.12.refs_1_), channel_id=1, source_target_pairs={{0,16},{1,9},{2,18},{3,11},{4,20},{5,13},{6,22},{7,15},{8,24},{9,1... | collective-permute-start | bytes 393224 | tf_op jit(solution)/shard_map/ppermute | solution.py:374
  52.0 0.4 collective-permute-start.9
  52.3 0.8 %collective-permute-done.8.refs_1_ = bf16[256,256]{1,0:T(8,128)(2,1)S(1)} collective-permute-done((bf16[256,256]{1,0:T(8,128)(2,1)S(1)}, bf16[256,256]{1,0:T(8,128)(2,1)S(1)}, u32[]{:S(2)}, u32[]{:S(2)}) %collective-permute-start.8) | collective-permute-done | bytes 131104 | tf_op jit(solution)/shard_map/ppermute | solution.py:374
  53.1 1.7 %collective-permute-start.10 = (bf16[256,256]{1,0:T(8,128)(2,1)S(1)}, bf16[256,256]{1,0:T(8,128)(2,1)S(1)}, u32[]{:S(2)}, u32[]{:S(2)}) collective-permute-start(bf16[256,256]{1,0:T(8,128)(2,1)S(1)} %collective-permute-done.8.refs_1_), channel_id=1, source_target_pairs={{0,16},{1,9},{2,18},{3,11},{4,20},{5,13},{6,22},{7,15},{8,24},{9,1... | collective-permute-start | bytes 393224 | tf_op jit(solution)/shard_map/ppermute | solution.py:374
  54.8 0.0 collective-permute-done.18.refs_3_
  54.8 3.5 %output.3 = (f32[1024,256]{1,0:T(8,128)}, f32[1,128]{1,0:T(1,128)S(1)}) custom-call(s32[8]{0:T(128)S(1)} %get-tuple-element.18.home_any, bf16[512,256]{1,0:T(8,128)(2,1)S(1)} %merge.5.refs_0_, bf16[512,256]{1,0:T(8,128)(2,1)S(1)} %collective-permute-done.16.refs_1_, bf16[512,256]{1,0:T(8,128)(2,1)S(1)} %collective-permute-done.17.refs_2_, ...), custom_call_target="tpu_custom_call" | custom-call | flops 2500000000 | tf_op jit(solution)/shard_map/output/pallas_call | solution.py:512
  58.3 0.0 collective-permute-done.13.refs_2_
  58.3 0.0 collective-permute-done.14.refs_3_
  58.3 2.1 %output.4 = (f32[1024,256]{1,0:T(8,128)}, f32[1,128]{1,0:T(1,128)S(1)}) custom-call(s32[8]{0:T(128)S(1)} %get-tuple-element.18.home_any, bf16[256,256]{1,0:T(8,128)(2,1)S(1)} %merge.4.refs_0_, bf16[256,256]{1,0:T(8,128)(2,1)S(1)} %collective-permute-done.12.refs_1_, ...), custom_call_target="tpu_custom_call", output_to_operand_aliasing={{0}: (13, {})} | custom-call | flops 2500000000 | tf_op jit(solution)/shard_map/output/pallas_call | solution.py:512
  60.5 2.7 %output.5 = (f32[1024,256]{1,0:T(8,128)}, f32[1,16]{1,0:T(1,128)}) custom-call(s32[8]{0:T(128)S(1)} %get-tuple-element.18.home_any, bf16[256,256]{1,0:T(8,128)(2,1)S(1)} %merge.3.refs_0_, bf16[256,256]{1,0:T(8,128)(2,1)S(1)} %collective-permute-done.8.refs_1_, bf16[256,256]{1,0:T(8,128)(2,1)S(1)} %collective-permute-done.9.refs_2_, ...), custom_call_target="tpu_custom_call", output_to_operand_aliasing={{0}: (13, {})} | custom-call | flops 2500000000 | tf_op jit(solution)/shard_map/output/pallas_call | solution.py:512
  (20 shorter events, 0.0 us)
Async XLA Ops:
  0.6 4.7 %copy-start.3 = (bf16[256,1024]{1,0:T(8,128)(2,1)S(1)}, bf16[256,1024]{1,0:T(8,128)(2,1)}, u32[]{:S(2)}) copy-start(bf16[256,1024]{1,0:T(8,128)(2,1)} %refs_4_.5) | copy-start | bytes 1572868
  0.6 16.5 %copy-start = (bf16[1024,1024]{1,0:T(8,128)(2,1)S(1)}, bf16[1024,1024]{1,0:T(8,128)(2,1)}, u32[]{:S(2)}) copy-start(bf16[1024,1024]{1,0:T(8,128)(2,1)} %x_ref.1) | copy-start | bytes 6291460
  0.7 16.5 %copy-start.1 = (bf16[1024,256]{1,0:T(8,128)(2,1)S(1)}, bf16[1024,256]{1,0:T(8,128)(2,1)}, u32[]{:S(2)}) copy-start(bf16[1024,256]{1,0:T(8,128)(2,1)} %wk_ref.1) | copy-start | bytes 1572868
  0.7 16.5 %copy-start.2 = (bf16[1024,256]{1,0:T(8,128)(2,1)S(1)}, bf16[1024,256]{1,0:T(8,128)(2,1)}, u32[]{:S(2)}) copy-start(bf16[1024,256]{1,0:T(8,128)(2,1)} %wv_ref.1) | copy-start | bytes 1572868
  0.7 16.5 %copy-start.4 = (s32[1024]{0:T(1024)S(1)}, s32[1024]{0:T(1024)}, u32[]{:S(2)}) copy-start(s32[1024]{0:T(1024)} %param.20) | copy-start | bytes 12292
  0.7 16.5 %copy-start.7 = (f32[2,4]{1,0:T(2,128)S(1)}, f32[2,4]{1,0:T(2,128)}, u32[]{:S(2)}) copy-start(f32[2,4]{1,0:T(2,128)} %bias_ref.9) | copy-start | bytes 100
  0.7 16.5 %copy-start.8 = (f32[264,128]{1,0:T(8,128)S(1)}, f32[264,128]{1,0:T(8,128)}, u32[]{:S(2)}) copy-start(f32[264,128]{1,0:T(8,128)} %constant.2.clone.refs_5_.table_ref) | copy-start | bytes 405508
  4.8 12.3 %collective-permute-start.1 = (bf16[1040,256]{1,0:T(8,128)(2,1)S(1)}, bf16[1040,256]{1,0:T(8,128)(2,1)S(1)}, u32[]{:S(2)}, u32[]{:S(2)}) collective-permute-start(bf16[1040,256]{1,0:T(8,128)(2,1)S(1)} %get-tuple-element.21.own_ref), channel_id=1, source_target_pairs={{0,1},{1,0},{2,3},{3,2},{4,5},{5,4},{6,7},{7,6},{8,9},{9,8},{10,11... | collective-permute-start | bytes 1597448 | tf_op jit(solution)/shard_map/ppermute | solution.py:365
  5.3 9.7 %collective-permute-start.4 = (bf16[256,1024]{1,0:T(8,128)(2,1)S(1)}, bf16[256,1024]{1,0:T(8,128)(2,1)S(1)}, u32[]{:S(2)}, u32[]{:S(2)}) collective-permute-start(bf16[256,1024]{1,0:T(8,128)(2,1)S(1)} %copy-done.3), channel_id=1, source_target_pairs={{0,8},{1,17},{2,10},{3,19},{4,12},{5,21},{6,14},{7,23},{8,0},{9,25... | collective-permute-start | bytes 1572872 | tf_op jit(solution)/shard_map/ppermute | solution.py:374
  7.9 19.4 %collective-permute-start = (bf16[272,256]{1,0:T(8,128)(2,1)S(1)}, bf16[272,256]{1,0:T(8,128)(2,1)S(1)}, u32[]{:S(2)}, u32[]{:S(2)}) collective-permute-start(bf16[272,256]{1,0:T(8,128)(2,1)S(1)} %get-tuple-element.20.refs_3_), channel_id=1, source_target_pairs={{0,6},{1,7},{2,4},{3,5},{4,2},{5,3},{6,0},{7,1},{8,14},{9,15},{10,... | collective-permute-start | bytes 417800 | tf_op jit(solution)/shard_map/ppermute | solution.py:365
  11.5 14.3 %collective-permute-start.2 = (bf16[272,256]{1,0:T(8,128)(2,1)S(1)}, bf16[272,256]{1,0:T(8,128)(2,1)S(1)}, u32[]{:S(2)}, u32[]{:S(2)}) collective-permute-start(bf16[272,256]{1,0:T(8,128)(2,1)S(1)} %get-tuple-element.22.refs_2_), channel_id=1, source_target_pairs={{0,4},{1,5},{2,6},{3,7},{4,0},{5,1},{6,2},{7,3},{8,12},{9,13},{10,... | collective-permute-start | bytes 417800 | tf_op jit(solution)/shard_map/ppermute | solution.py:365
  11.5 11.1 %collective-permute-start.3 = (bf16[272,256]{1,0:T(8,128)(2,1)S(1)}, bf16[272,256]{1,0:T(8,128)(2,1)S(1)}, u32[]{:S(2)}, u32[]{:S(2)}) collective-permute-start(bf16[272,256]{1,0:T(8,128)(2,1)S(1)} %get-tuple-element.23.refs_1_), channel_id=1, source_target_pairs={{0,2},{1,3},{2,0},{3,1},{4,6},{5,7},{6,4},{7,5},{8,10},{9,11},{10,... | collective-permute-start | bytes 417800 | tf_op jit(solution)/shard_map/ppermute | solution.py:365
  15.1 12.3 %collective-permute-start.6 = (bf16[256,1024]{1,0:T(8,128)(2,1)S(1)}, bf16[256,1024]{1,0:T(8,128)(2,1)S(1)}, u32[]{:S(2)}, u32[]{:S(2)}) collective-permute-start(bf16[256,1024]{1,0:T(8,128)(2,1)S(1)} %collective-permute-done.4.refs_5_), channel_id=1, source_target_pairs={{0,16},{1,9},{2,18},{3,11},{4,20},{5,13},{6,22},{7,15},{8,24},{9,1... | collective-permute-start | bytes 1572872 | tf_op jit(solution)/shard_map/ppermute | solution.py:374
  17.1 10.2 %collective-permute-start.5 = (bf16[256,1024]{1,0:T(8,128)(2,1)S(1)}, bf16[256,1024]{1,0:T(8,128)(2,1)S(1)}, u32[]{:S(2)}, u32[]{:S(2)}) collective-permute-start(bf16[256,1024]{1,0:T(8,128)(2,1)S(1)} %collective-permute-done.4.refs_5_), channel_id=1, source_target_pairs={{0,1},{1,0},{2,3},{3,2},{4,5},{5,4},{6,7},{7,6},{8,9},{9,8},{10,11... | collective-permute-start | bytes 1572872 | tf_op jit(solution)/shard_map/ppermute | solution.py:365
  24.2 6.1 %collective-permute-start.15 = (bf16[272,256]{1,0:T(8,128)(2,1)S(1)}, bf16[272,256]{1,0:T(8,128)(2,1)S(1)}, u32[]{:S(2)}, u32[]{:S(2)}) collective-permute-start(bf16[272,256]{1,0:T(8,128)(2,1)S(1)} %cache_part.5.refs_0_), channel_id=1, source_target_pairs={{0,2},{1,3},{2,0},{3,1},{4,6},{5,7},{6,4},{7,5},{8,10},{9,11},{10,... | collective-permute-start | bytes 417800 | tf_op jit(solution)/shard_map/ppermute | solution.py:365
  28.9 25.9 %copy-start.5 = (f32[1024]{0:T(1024)S(1)}, f32[1024]{0:T(1024)}, u32[]{:S(2)}) copy-start(f32[1024]{0:T(1024)} %param.31) | copy-start | bytes 12292
  28.9 25.9 %copy-start.6 = (f32[1024]{0:T(1024)S(1)}, f32[1024]{0:T(1024)}, u32[]{:S(2)}) copy-start(f32[1024]{0:T(1024)} %param.32) | copy-start | bytes 12292
  30.5 7.0 %collective-permute-start.16 = (bf16[512,256]{1,0:T(8,128)(2,1)S(1)}, bf16[512,256]{1,0:T(8,128)(2,1)S(1)}, u32[]{:S(2)}, u32[]{:S(2)}) collective-permute-start(bf16[512,256]{1,0:T(8,128)(2,1)S(1)} %merge.5.refs_0_), channel_id=1, source_target_pairs={{0,8},{1,17},{2,10},{3,19},{4,12},{5,21},{6,14},{7,23},{8,0},{9,25... | collective-permute-start | bytes 786440 | tf_op jit(solution)/shard_map/ppermute | solution.py:374
  32.1 12.0 %collective-permute-start.11 = (bf16[272,256]{1,0:T(8,128)(2,1)S(1)}, bf16[272,256]{1,0:T(8,128)(2,1)S(1)}, u32[]{:S(2)}, u32[]{:S(2)}) collective-permute-start(bf16[272,256]{1,0:T(8,128)(2,1)S(1)} %cache_part.6.refs_0_), channel_id=1, source_target_pairs={{0,4},{1,5},{2,6},{3,7},{4,0},{5,1},{6,2},{7,3},{8,12},{9,13},{10,... | collective-permute-start | bytes 417800 | tf_op jit(solution)/shard_map/ppermute | solution.py:365
  34.6 11.2 %collective-permute-start.7 = (bf16[272,256]{1,0:T(8,128)(2,1)S(1)}, bf16[272,256]{1,0:T(8,128)(2,1)S(1)}, u32[]{:S(2)}, u32[]{:S(2)}) collective-permute-start(bf16[272,256]{1,0:T(8,128)(2,1)S(1)} %cache_part.7.refs_2_.refs_3_), channel_id=1, source_target_pairs={{0,6},{1,7},{2,4},{3,5},{4,2},{5,3},{6,0},{7,1},{8,14},{9,15},{10,... | collective-permute-start | bytes 417800 | tf_op jit(solution)/shard_map/ppermute | solution.py:365
  36.0 16.0 %collective-permute-start.17 = (bf16[512,256]{1,0:T(8,128)(2,1)S(1)}, bf16[512,256]{1,0:T(8,128)(2,1)S(1)}, u32[]{:S(2)}, u32[]{:S(2)}) collective-permute-start(bf16[512,256]{1,0:T(8,128)(2,1)S(1)} %merge.5.refs_0_), channel_id=1, source_target_pairs={{0,16},{1,9},{2,18},{3,11},{4,20},{5,13},{6,22},{7,15},{8,24},{9,1... | collective-permute-start | bytes 786440 | tf_op jit(solution)/shard_map/ppermute | solution.py:374
  37.4 17.3 %collective-permute-start.18 = (bf16[512,256]{1,0:T(8,128)(2,1)S(1)}, bf16[512,256]{1,0:T(8,128)(2,1)S(1)}, u32[]{:S(2)}, u32[]{:S(2)}) collective-permute-start(bf16[512,256]{1,0:T(8,128)(2,1)S(1)} %collective-permute-done.16.refs_1_), channel_id=1, source_target_pairs={{0,16},{1,9},{2,18},{3,11},{4,20},{5,13},{6,22},{7,15},{8,24},{9,1... | collective-permute-start | bytes 786440 | tf_op jit(solution)/shard_map/ppermute | solution.py:374
  44.2 6.1 %collective-permute-start.12 = (bf16[256,256]{1,0:T(8,128)(2,1)S(1)}, bf16[256,256]{1,0:T(8,128)(2,1)S(1)}, u32[]{:S(2)}, u32[]{:S(2)}) collective-permute-start(bf16[256,256]{1,0:T(8,128)(2,1)S(1)} %merge.4.refs_0_), channel_id=1, source_target_pairs={{0,8},{1,17},{2,10},{3,19},{4,12},{5,21},{6,14},{7,23},{8,0},{9,25... | collective-permute-start | bytes 393224 | tf_op jit(solution)/shard_map/ppermute | solution.py:374
  46.0 7.1 %collective-permute-start.8 = (bf16[256,256]{1,0:T(8,128)(2,1)S(1)}, bf16[256,256]{1,0:T(8,128)(2,1)S(1)}, u32[]{:S(2)}, u32[]{:S(2)}) collective-permute-start(bf16[256,256]{1,0:T(8,128)(2,1)S(1)} %merge.3.refs_0_), channel_id=1, source_target_pairs={{0,8},{1,17},{2,10},{3,19},{4,12},{5,21},{6,14},{7,23},{8,0},{9,25... | collective-permute-start | bytes 393224 | tf_op jit(solution)/shard_map/ppermute | solution.py:374
  46.5 11.8 %collective-permute-start.13 = (bf16[256,256]{1,0:T(8,128)(2,1)S(1)}, bf16[256,256]{1,0:T(8,128)(2,1)S(1)}, u32[]{:S(2)}, u32[]{:S(2)}) collective-permute-start(bf16[256,256]{1,0:T(8,128)(2,1)S(1)} %merge.4.refs_0_), channel_id=1, source_target_pairs={{0,16},{1,9},{2,18},{3,11},{4,20},{5,13},{6,22},{7,15},{8,24},{9,1... | collective-permute-start | bytes 393224 | tf_op jit(solution)/shard_map/ppermute | solution.py:374
  50.3 8.0 %collective-permute-start.14 = (bf16[256,256]{1,0:T(8,128)(2,1)S(1)}, bf16[256,256]{1,0:T(8,128)(2,1)S(1)}, u32[]{:S(2)}, u32[]{:S(2)}) collective-permute-start(bf16[256,256]{1,0:T(8,128)(2,1)S(1)} %collective-permute-done.12.refs_1_), channel_id=1, source_target_pairs={{0,16},{1,9},{2,18},{3,11},{4,20},{5,13},{6,22},{7,15},{8,24},{9,1... | collective-permute-start | bytes 393224 | tf_op jit(solution)/shard_map/ppermute | solution.py:374
  52.0 8.5 %collective-permute-start.9 = (bf16[256,256]{1,0:T(8,128)(2,1)S(1)}, bf16[256,256]{1,0:T(8,128)(2,1)S(1)}, u32[]{:S(2)}, u32[]{:S(2)}) collective-permute-start(bf16[256,256]{1,0:T(8,128)(2,1)S(1)} %merge.3.refs_0_), channel_id=1, source_target_pairs={{0,16},{1,9},{2,18},{3,11},{4,20},{5,13},{6,22},{7,15},{8,24},{9,1... | collective-permute-start | bytes 393224 | tf_op jit(solution)/shard_map/ppermute | solution.py:374
  53.1 7.3 %collective-permute-start.10 = (bf16[256,256]{1,0:T(8,128)(2,1)S(1)}, bf16[256,256]{1,0:T(8,128)(2,1)S(1)}, u32[]{:S(2)}, u32[]{:S(2)}) collective-permute-start(bf16[256,256]{1,0:T(8,128)(2,1)S(1)} %collective-permute-done.8.refs_1_), channel_id=1, source_target_pairs={{0,16},{1,9},{2,18},{3,11},{4,20},{5,13},{6,22},{7,15},{8,24},{9,1... | collective-permute-start | bytes 393224 | tf_op jit(solution)/shard_map/ppermute | solution.py:374

commit v4 on v3

--- a/solution.py
+++ b/solution.py
@@ -20,7 +20,7 @@
 HBM = pl.BlockSpec(memory_space=pltpu.HBM)
 ANY = pl.BlockSpec(memory_space=pl.ANY)
 DMA = pltpu.SemaphoreType.DMA
-GROUPS = [[0, 1], [2], [3]]
+GROUPS = [[0, 1], [2, 3]]
 LIMIT = 32 * 1024 * 1024
 
 
@@ -109,7 +109,8 @@
     return moves
 
 
-def query_kernel(bpq, chunks, *refs):
+def query_kernel(bpq, order, *refs):
+    chunks = len(order)
     sources, refs = refs[:11], refs[11:]
     pick_ref, base_ref, usable_ref, packed_ref = refs[:4]
     q_refs, refs = refs[4 : 4 + chunks], refs[4 + chunks :]
@@ -144,7 +145,7 @@
         packed_ref[rows + i * cols : rows + (i + 1) * cols, :] = block.T.astype(BF)
     for k, q_ref in enumerate(q_refs):
         for j in range(2):
-            slot = slot_of(2 * k + j, doc_query, block_perm, slots, bpq)
+            slot = slot_of(2 * order[k] + j, doc_query, block_perm, slots, bpq)
             pick_ref[2 * k + j] = slot
             cos, sin = slot_tables(slot, base_ref, cos_ref, sin_ref, rows_ref)
             at = pl.ds(pl.multiple_of(slot * width, width), width)
@@ -224,12 +225,12 @@
 
 
 def own_kernel(
-    home_any, bias_ref, x_ref, wk_ref, wv_ref, var_ref, table_ref, base_ref, after,
+    home_any, bias_ref, x_ref, wk_ref, wv_ref, var_ref, table_ref, base_ref,
     *refs
 ):
-    del after
-    out_ref, x_home_ref, k_ref, v_ref, home_ref, sem = refs[-6:]
-    q_refs = refs[:-6]
+    w_ref, out_ref, x_home_ref, w_copy_ref, k_ref, v_ref, home_ref, sem = refs[-8:]
+    q_refs = refs[:-8]
+    w_copy_ref[...] = w_ref[...]
     slots, width = var_ref.shape
     cols = wk_ref.shape[1]
     home_move = pltpu.make_async_copy(home_any, home_ref, sem)
@@ -260,9 +261,8 @@
         part_ref[cols:, :] = stats
 
 
-def merge_kernel(firsts, *refs):
-    own_ref, after, out_ref = refs[-3:]
-    del after
+def merge_kernel(firsts, own_ref, *refs):
+    out_ref = refs[-1]
     for i, (first, got_ref) in enumerate(zip(firsts, refs)):
         cols = got_ref.shape[0] - EXTRA
         heads = cols // DH
@@ -405,6 +405,7 @@
     slots = QUERIES
     width = rows // slots
     chunks = blocks // 2
+    order = [0, 2, 3, 1] + list(range(4, chunks))
     cache_rows = cache_k.shape[0]
     seg = doc_seg.reshape(slots, width)
     var = doc_var.reshape(slots, width)
@@ -416,11 +417,9 @@
     base_shape = sds((5, slots, width), F32)
 
     w_first = hop(w_out, 1, 2)
-    w_second = partner(w_first, "blk", 1)
-    w_third = hop(w_first, 2, 1)
 
     pick, base, usable, packed, *queries = call(
-        functools.partial(query_kernel, bpq, chunks),
+        functools.partial(query_kernel, bpq, order),
         [
             sds((blocks,), i32), base_shape, sds((8, width), i32),
             sds((2 * cache_rows + EXTRA, cols), BF),
@@ -442,7 +441,7 @@
         )
     )
 
-    asked = [queries[0]] + [partner(queries[k], "blk", 2 * k) for k in range(1, chunks)]
+    asked = [queries[0]] + [partner(queries[k], "blk", 2 * order[k]) for k in range(1, chunks)]
     packed_other = partner(packed, "blk", 1)
 
     if bpq == 1:
@@ -456,24 +455,24 @@
             every[2 * k : 2 * k + 2].reshape(2 * width, cols) for k in range(slots // 2)
         ]
 
-    own, x_home = call(
+    own, x_home, w_copy = call(
         own_kernel,
-        [sds((slots, cols + 8, width), F32), sds((rows, depth), BF)],
-        [ANY] + [VMEM] * 7 + [ANY] + [VMEM] * len(home_queries),
+        [sds((slots, cols + 8, width), F32), sds((rows, depth), BF), sds(w_out.shape, BF)],
+        [ANY] + [VMEM] * (8 + len(home_queries)),
         [
             pltpu.VMEM((rows, cols), F32), pltpu.VMEM((rows, cols), F32),
             pltpu.SMEM(home.shape, i32), DMA,
         ],
-        out_specs=[VMEM] * 2,
+        out_specs=[VMEM] * 3,
         work=4.0,
         name="own_documents",
-    )(home, var_bias, doc_x, w_key, w_value, var, table, base, packed_other, *home_queries)
-
+    )(home, var_bias, doc_x, w_key, w_value, var, table, base, *home_queries, w_first)
+
+    w_second = partner(w_copy, "blk", 1)
+    w_third = hop(w_copy, 2, 1)
     parts = []
     for k, query in enumerate(asked):
         after = [parts[-1] if parts else own]
-        if k == chunks - 1:
-            after += [w_second, w_third]
         part = call(
             cache_kernel,
             chunk_shape,
@@ -483,21 +482,23 @@
             name="cache_part",
         )(usable, var_bias, query, packed, packed_other, *after)
         parts.append(part)
-    backs = [parts[0]] + [partner(parts[k], "blk", 2 * k) for k in range(1, chunks)]
+    backs = [parts[0]] + [partner(parts[k], "blk", 2 * order[k]) for k in range(1, chunks)]
 
     groups = GROUPS
     if bpq == 1:
-        attended = [
-            call(
-                functools.partial(merge_kernel, [2 * k for k in group]),
-                sds((2 * width * len(group), cols), BF),
-                [VMEM] * (len(group) + 1) + [ANY],
-                out_specs=VMEM,
-                work=0.2,
-            name="merge",
-            )(*[backs[k] for k in group], own, parts[-1])
-            for group in groups
-        ]
+        attended = []
+        for group in groups:
+            after = attended[-1:] or [parts[-1], w_second, w_third]
+            attended.append(
+                call(
+                    functools.partial(merge_kernel, [2 * k for k in group]),
+                    sds((2 * width * len(group), cols), BF),
+                    [VMEM] * (len(group) + 1) + [ANY] * len(after),
+                    out_specs=VMEM,
+                    work=20 if attended else 0.2,
+                    name="merge",
+                )(own, *[backs[k] for k in group], *after)
+            )
     else:
         attended = spread_merge(backs, own, pick, slots, bpq)
         attended = [jnp.concatenate([attended[k] for k in group]) for group in groups]

time: 63.4 us -> 58 us (0.915); the launches traced: 63.3 us -> 57.2 us
  starting transfers between devices: 25.2 us -> 20.2 us
  Pallas kernels: 22.9 us -> 21.4 us
    ppermute x11 -> x8, starting transfers between devices: 14.7 us -> 10.8 us  [hop(): return lax.ppermute(value, ('head', 'blk'), pairs)]
    pallas_call x3 -> x2, Pallas kernels: 8.32 us -> 6.88 us  [body(): call(functools.partial(output_kernel, [2 * k for k in group]), [sds((rows...]
    ppermute x8, starting transfers between devices: 10.5 us -> 9.43 us  [partner(): return lax.ppermute(value, axis, [(i, i ^ k) for i in range(count)])]
    ppermute x8, waiting for transfers between devices: 7.43 us -> 8.07 us  [partner(): return lax.ppermute(value, axis, [(i, i ^ k) for i in range(count)])]
    ppermute x11 -> x8, waiting for transfers between devices: 6.73 us -> 6.7 us  [hop(): return lax.ppermute(value, ('head', 'blk'), pairs)]
  transfers between devices with their start and end apart: 19 -> 16, of which waited for: 6 -> 6; matrix products, arithmetic and copies ran while one was open for 0% -> 0% of each run, Pallas kernels for 25% -> 31%
where the time goes in v4:
time: 58 us; the launch traced here: 57.2 us
  Pallas kernels  21.4 us (37%)
  starting transfers between devices  20.2 us (35%)
  waiting for transfers between devices  14.8 us (26%)
  between operations  0.83 us (1%)
    ppermute x8, starting transfers between devices, hop(): return lax.ppermute(value, ('head', 'blk'), pairs)  10.8 us
    ppermute x8, starting transfers between devices, partner(): return lax.ppermute(value, axis, [(i, i ^ k) for i in range(count)])  9.43 us
    ppermute x8, waiting for transfers between devices, partner(): return lax.ppermute(value, axis, [(i, i ^ k) for i in range(count)])  8.07 us
    pallas_call x2, Pallas kernels, body(): call(functools.partial(output_kernel, [2 * k for k in group]), [sds((rows...  6.88 us
    ppermute x8, waiting for transfers between devices, hop(): return lax.ppermute(value, ('head', 'blk'), pairs)  6.7 us
    pallas_call x4, Pallas kernels, body(): call(cache_kernel, chunk_shape, [VMEM] * 5 + [ANY] * len(after), out_spec...  6.05 us
    pallas_call x1, Pallas kernels, body(): call(functools.partial(query_kernel, bpq, order), [sds((blocks,), i32), b...  4.11 us
    pallas_call x1, Pallas kernels, body(): call(own_kernel, [sds((slots, cols + 8, width), F32), sds((rows, depth),...  3.94 us
  transfers between devices with their start and end apart: 16, of which 6 were waited for; matrix products, arithmetic and copies ran while one was open for 0% of the time, Pallas kernels for 31%

profile of v4, /device:TPU:0, one launch (start us, length us, event | category | flops | bytes accessed | tf_op | source)
XLA Modules:
  0.0 57.2 jit_solution(9545943064902211011)
XLA Ops:
  0.6 3.0 %collective-permute-start = (bf16[256,1024]{1,0:T(8,128)(2,1)}, bf16[256,1024]{1,0:T(8,128)(2,1)S(1)}, u32[]{:S(2)}, u32[]{:S(2)}) collective-permute-start(bf16[256,1024]{1,0:T(8,128)(2,1)} %refs_4_.3), channel_id=1, source_target_pairs={{0,8},{1,17},{2,10},{3,19},{4,12},{5,21},{6,14},{7,23},{8,0},{9,25... | collective-permute-start | bytes 1572872 | tf_op jit(solution)/shard_map/ppermute | solution.py:374
  3.6 0.0 copy-start.7
  3.7 0.0 copy-start.8
  3.7 4.1 %query.1 = (s32[8]{0:T(128)S(1)}, f32[5,8,128]{2,1,0:T(8,128)S(1)}, s32[8,128]{1,0:T(8,128)S(1)}, bf16[1040,256]{1,0:T(8,128)(2,1)S(1)}, bf16[272,256]{1,0:T(8,1...) custom-call(s32[128]{0:T(128)} %refs_0_.1, s32[8]{0:T(128)} %refs_1_.1, ...), custom_call_target="tpu_custom_call" | custom-call | flops 3500000000 | tf_op jit(solution)/shard_map/query/pallas_call | solution.py:421
  7.8 0.1 collective-permute-start.2
  7.9 2.7 %collective-permute-start.3 = (bf16[272,256]{1,0:T(8,128)(2,1)S(1)}, bf16[272,256]{1,0:T(8,128)(2,1)S(1)}, u32[]{:S(2)}, u32[]{:S(2)}) collective-permute-start(bf16[272,256]{1,0:T(8,128)(2,1)S(1)} %get-tuple-element.20.refs_1_), channel_id=1, source_target_pairs={{0,4},{1,5},{2,6},{3,7},{4,0},{5,1},{6,2},{7,3},{8,12},{9,13},{10,... | collective-permute-start | bytes 417800 | tf_op jit(solution)/shard_map/ppermute | solution.py:365
  10.5 1.3 %collective-permute-start.1 = (bf16[272,256]{1,0:T(8,128)(2,1)S(1)}, bf16[272,256]{1,0:T(8,128)(2,1)S(1)}, u32[]{:S(2)}, u32[]{:S(2)}) collective-permute-start(bf16[272,256]{1,0:T(8,128)(2,1)S(1)} %get-tuple-element.21.refs_2_), channel_id=1, source_target_pairs={{0,6},{1,7},{2,4},{3,5},{4,2},{5,3},{6,0},{7,1},{8,14},{9,15},{10,... | collective-permute-start | bytes 417800 | tf_op jit(solution)/shard_map/ppermute | solution.py:365
  11.9 0.2 collective-permute-start.5
  12.1 0.0 collective-permute-done.refs_4_.refs_5_
  12.2 3.9 %own_documents.1 = (f32[8,264,128]{2,1,0:T(8,128)S(1)}, bf16[1024,1024]{1,0:T(8,128)(2,1)S(1)}, bf16[256,1024]{1,0:T(8,128)(2,1)S(1)}) custom-call(s32[8]{0:T(128)S(1)} %get-tuple-element.17.home_any, f32[2,4]{1,0:T(2,128)S(1)} %copy-done.7, bf16[1024,1024]{1,0:T(8,128)(2,1)S(1)} %copy-done, bf16[1024,256]{1,0:T(8,128)(2,1)S(1)} %copy-done.1, ...), custom_call_target="tpu_custom_call" | custom-call | flops 4000000000 | tf_op jit(solution)/shard_map/own_documents/pallas_call | solution.py:458
  16.1 1.6 %collective-permute-start.9 = (bf16[256,1024]{1,0:T(8,128)(2,1)S(1)}, bf16[256,1024]{1,0:T(8,128)(2,1)S(1)}, u32[]{:S(2)}, u32[]{:S(2)}) collective-permute-start(bf16[256,1024]{1,0:T(8,128)(2,1)S(1)} %get-tuple-element.26), channel_id=1, source_target_pairs={{0,16},{1,9},{2,18},{3,11},{4,20},{5,13},{6,22},{7,15},{8,24},{9,1... | collective-permute-start | bytes 1572872 | tf_op jit(solution)/shard_map/ppermute | solution.py:374
  17.7 0.0 collective-permute-done.2.other_ref
  17.7 0.0 collective-permute-start.8
  17.7 1.5 %cache_part.4.refs_0_ = bf16[272,256]{1,0:T(8,128)(2,1)S(1)} custom-call(s32[8,128]{1,0:T(8,128)S(1)} %get-tuple-element.24.usable_ref, f32[2,4]{1,0:T(2,128)S(1)} %copy-done.7, bf16[272,256]{1,0:T(8,128)(2,1)S(1)} %get-tuple-element.19.refs_0_.q_ref, bf16[1040,256]{1,0:T(8,128)(2,1)S(1)} %get-tuple-element.25.own_ref, ...), custom_call_target="tpu_custom_call" | custom-call | flops 1500000000 | tf_op jit(solution)/shard_map/cache_part/pallas_call | solution.py:476
  19.2 2.1 %collective-permute-done.3.q_ref = bf16[272,256]{1,0:T(8,128)(2,1)S(1)} collective-permute-done((bf16[272,256]{1,0:T(8,128)(2,1)S(1)}, bf16[272,256]{1,0:T(8,128)(2,1)S(1)}, u32[]{:S(2)}, u32[]{:S(2)}) %collective-permute-start.3) | collective-permute-done | bytes 139296 | tf_op jit(solution)/shard_map/ppermute | solution.py:365
  21.3 1.5 %cache_part.5.refs_0_ = bf16[272,256]{1,0:T(8,128)(2,1)S(1)} custom-call(s32[8,128]{1,0:T(8,128)S(1)} %get-tuple-element.24.usable_ref, f32[2,4]{1,0:T(2,128)S(1)} %copy-done.7, bf16[272,256]{1,0:T(8,128)(2,1)S(1)} %collective-permute-done.3.q_ref, bf16[1040,256]{1,0:T(8,128)(2,1)S(1)} %get-tuple-element.25.own_ref, ...), custom_call_target="tpu_custom_call" | custom-call | flops 1500000000 | tf_op jit(solution)/shard_map/cache_part/pallas_call | solution.py:476
  22.8 0.8 %collective-permute-start.7 = (bf16[272,256]{1,0:T(8,128)(2,1)S(1)}, bf16[272,256]{1,0:T(8,128)(2,1)S(1)}, u32[]{:S(2)}, u32[]{:S(2)}) collective-permute-start(bf16[272,256]{1,0:T(8,128)(2,1)S(1)} %cache_part.5.refs_0_), channel_id=1, source_target_pairs={{0,4},{1,5},{2,6},{3,7},{4,0},{5,1},{6,2},{7,3},{8,12},{9,13},{10,... | collective-permute-start | bytes 417800 | tf_op jit(solution)/shard_map/ppermute | solution.py:365
  23.6 0.0 collective-permute-done.1.q_ref
  23.6 1.5 %cache_part.6.refs_0_ = bf16[272,256]{1,0:T(8,128)(2,1)S(1)} custom-call(s32[8,128]{1,0:T(8,128)S(1)} %get-tuple-element.24.usable_ref, f32[2,4]{1,0:T(2,128)S(1)} %copy-done.7, bf16[272,256]{1,0:T(8,128)(2,1)S(1)} %collective-permute-done.1.q_ref, bf16[1040,256]{1,0:T(8,128)(2,1)S(1)} %get-tuple-element.25.own_ref, ...), custom_call_target="tpu_custom_call" | custom-call | flops 1500000000 | tf_op jit(solution)/shard_map/cache_part/pallas_call | solution.py:476
  25.1 0.0 collective-permute-done.5.q_ref
  25.1 1.5 %cache_part.7.refs_2_ = bf16[272,256]{1,0:T(8,128)(2,1)S(1)} custom-call(s32[8,128]{1,0:T(8,128)S(1)} %get-tuple-element.24.usable_ref, f32[2,4]{1,0:T(2,128)S(1)} %copy-done.7, bf16[272,256]{1,0:T(8,128)(2,1)S(1)} %collective-permute-done.5.q_ref, bf16[1040,256]{1,0:T(8,128)(2,1)S(1)} %get-tuple-element.25.own_ref, ...), custom_call_target="tpu_custom_call" | custom-call | flops 1500000000 | tf_op jit(solution)/shard_map/cache_part/pallas_call | solution.py:476
  26.7 3.0 %collective-permute-start.6 = (bf16[272,256]{1,0:T(8,128)(2,1)S(1)}, bf16[272,256]{1,0:T(8,128)(2,1)S(1)}, u32[]{:S(2)}, u32[]{:S(2)}) collective-permute-start(bf16[272,256]{1,0:T(8,128)(2,1)S(1)} %cache_part.7.refs_2_), channel_id=1, source_target_pairs={{0,2},{1,3},{2,0},{3,1},{4,6},{5,7},{6,4},{7,5},{8,10},{9,11},{10,... | collective-permute-start | bytes 417800 | tf_op jit(solution)/shard_map/ppermute | solution.py:365
  29.7 1.3 %collective-permute-start.4 = (bf16[272,256]{1,0:T(8,128)(2,1)S(1)}, bf16[272,256]{1,0:T(8,128)(2,1)S(1)}, u32[]{:S(2)}, u32[]{:S(2)}) collective-permute-start(bf16[272,256]{1,0:T(8,128)(2,1)S(1)} %cache_part.6.refs_0_), channel_id=1, source_target_pairs={{0,6},{1,7},{2,4},{3,5},{4,2},{5,3},{6,0},{7,1},{8,14},{9,15},{10,... | collective-permute-start | bytes 417800 | tf_op jit(solution)/shard_map/ppermute | solution.py:365
  31.0 0.7 %collective-permute-done.7.refs_1_ = bf16[272,256]{1,0:T(8,128)(2,1)S(1)} collective-permute-done((bf16[272,256]{1,0:T(8,128)(2,1)S(1)}, bf16[272,256]{1,0:T(8,128)(2,1)S(1)}, u32[]{:S(2)}, u32[]{:S(2)}) %collective-permute-start.7) | collective-permute-done | bytes 139296 | tf_op jit(solution)/shard_map/ppermute | solution.py:365
  31.7 0.0 collective-permute-done.9.refs_4_.refs_7_
  31.7 0.0 collective-permute-done.8.refs_3_.refs_6_
  31.7 0.2 merge.2.refs_2_.refs_0_
  31.9 0.0 copy-start.3
  31.9 0.0 copy-start.5
  31.9 0.0 copy-start.6
  31.9 0.4 collective-permute-start.13
  32.3 3.0 %collective-permute-done.6.refs_1_ = bf16[272,256]{1,0:T(8,128)(2,1)S(1)} collective-permute-done((bf16[272,256]{1,0:T(8,128)(2,1)S(1)}, bf16[272,256]{1,0:T(8,128)(2,1)S(1)}, u32[]{:S(2)}, u32[]{:S(2)}) %collective-permute-start.6) | collective-permute-done | bytes 139296 | tf_op jit(solution)/shard_map/ppermute | solution.py:365
  35.4 2.2 %collective-permute-done.4.refs_0_ = bf16[272,256]{1,0:T(8,128)(2,1)S(1)} collective-permute-done((bf16[272,256]{1,0:T(8,128)(2,1)S(1)}, bf16[272,256]{1,0:T(8,128)(2,1)S(1)}, u32[]{:S(2)}, u32[]{:S(2)}) %collective-permute-start.4) | collective-permute-done | bytes 139296 | tf_op jit(solution)/shard_map/ppermute | solution.py:365
  37.6 0.2 merge.3.refs_0_
  37.8 0.7 %collective-permute-start.10 = (bf16[512,256]{1,0:T(8,128)(2,1)S(1)}, bf16[512,256]{1,0:T(8,128)(2,1)S(1)}, u32[]{:S(2)}, u32[]{:S(2)}) collective-permute-start(bf16[512,256]{1,0:T(8,128)(2,1)S(1)} %merge.3.refs_0_), channel_id=1, source_target_pairs={{0,8},{1,17},{2,10},{3,19},{4,12},{5,21},{6,14},{7,23},{8,0},{9,25... | collective-permute-start | bytes 786440 | tf_op jit(solution)/shard_map/ppermute | solution.py:374
  38.5 1.5 %collective-permute-start.14 = (bf16[512,256]{1,0:T(8,128)(2,1)S(1)}, bf16[512,256]{1,0:T(8,128)(2,1)S(1)}, u32[]{:S(2)}, u32[]{:S(2)}) collective-permute-start(bf16[512,256]{1,0:T(8,128)(2,1)S(1)} %merge.2.refs_2_.refs_0_), channel_id=1, source_target_pairs={{0,16},{1,9},{2,18},{3,11},{4,20},{5,13},{6,22},{7,15},{8,24},{9,1... | collective-permute-start | bytes 786440 | tf_op jit(solution)/shard_map/ppermute | solution.py:374
  39.9 0.0 collective-permute-done.13.refs_1_
  39.9 0.6 collective-permute-start.15
  40.5 1.5 %collective-permute-start.11 = (bf16[512,256]{1,0:T(8,128)(2,1)S(1)}, bf16[512,256]{1,0:T(8,128)(2,1)S(1)}, u32[]{:S(2)}, u32[]{:S(2)}) collective-permute-start(bf16[512,256]{1,0:T(8,128)(2,1)S(1)} %merge.3.refs_0_), channel_id=1, source_target_pairs={{0,16},{1,9},{2,18},{3,11},{4,20},{5,13},{6,22},{7,15},{8,24},{9,1... | collective-permute-start | bytes 786440 | tf_op jit(solution)/shard_map/ppermute | solution.py:374
  42.0 5.0 %collective-permute-done.10.refs_1_ = bf16[512,256]{1,0:T(8,128)(2,1)S(1)} collective-permute-done((bf16[512,256]{1,0:T(8,128)(2,1)S(1)}, bf16[512,256]{1,0:T(8,128)(2,1)S(1)}, u32[]{:S(2)}, u32[]{:S(2)}) %collective-permute-start.10) | collective-permute-done | bytes 262176 | tf_op jit(solution)/shard_map/ppermute | solution.py:374
  47.0 1.7 %collective-permute-start.12 = (bf16[512,256]{1,0:T(8,128)(2,1)S(1)}, bf16[512,256]{1,0:T(8,128)(2,1)S(1)}, u32[]{:S(2)}, u32[]{:S(2)}) collective-permute-start(bf16[512,256]{1,0:T(8,128)(2,1)S(1)} %collective-permute-done.10.refs_1_), channel_id=1, source_target_pairs={{0,16},{1,9},{2,18},{3,11},{4,20},{5,13},{6,22},{7,15},{8,24},{9,1... | collective-permute-start | bytes 786440 | tf_op jit(solution)/shard_map/ppermute | solution.py:374
  48.6 0.0 collective-permute-done.14.refs_2_
  48.6 0.0 collective-permute-done.15.refs_3_
  48.7 0.0 copy-done.3
  48.7 3.4 %output.2 = (f32[1024,256]{1,0:T(8,128)}, f32[1,128]{1,0:T(1,128)S(1)}) custom-call(s32[8]{0:T(128)S(1)} %get-tuple-element.17.home_any, bf16[512,256]{1,0:T(8,128)(2,1)S(1)} %merge.2.refs_2_.refs_0_, bf16[512,256]{1,0:T(8,128)(2,1)S(1)} %collective-permute-done.13.refs_1_, bf16[512,256]{1,0:T(8,128)(2,1)S(1)} %collective-permute-done.14.refs_2_, ...), custom_call_target="tpu_custom_call" | custom-call | flops 2500000000 | tf_op jit(solution)/shard_map/output/pallas_call | solution.py:513
  52.1 0.0 collective-permute-done.11.refs_2_
  52.1 1.7 %collective-permute-done.12.refs_3_ = bf16[512,256]{1,0:T(8,128)(2,1)S(1)} collective-permute-done((bf16[512,256]{1,0:T(8,128)(2,1)S(1)}, bf16[512,256]{1,0:T(8,128)(2,1)S(1)}, u32[]{:S(2)}, u32[]{:S(2)}) %collective-permute-start.12) | collective-permute-done | bytes 262176 | tf_op jit(solution)/shard_map/ppermute | solution.py:374
  53.7 3.5 %output.3 = (f32[1024,256]{1,0:T(8,128)}, f32[1,16]{1,0:T(1,128)}) custom-call(s32[8]{0:T(128)S(1)} %get-tuple-element.17.home_any, bf16[512,256]{1,0:T(8,128)(2,1)S(1)} %merge.3.refs_0_, bf16[512,256]{1,0:T(8,128)(2,1)S(1)} %collective-permute-done.10.refs_1_, ...), custom_call_target="tpu_custom_call", output_to_operand_aliasing={{0}: (13, {})} | custom-call | flops 2500000000 | tf_op jit(solution)/shard_map/output/pallas_call | solution.py:513
  (12 shorter events, 0.0 us)
Async XLA Ops:
  0.6 11.5 %collective-permute-start = (bf16[256,1024]{1,0:T(8,128)(2,1)}, bf16[256,1024]{1,0:T(8,128)(2,1)S(1)}, u32[]{:S(2)}, u32[]{:S(2)}) collective-permute-start(bf16[256,1024]{1,0:T(8,128)(2,1)} %refs_4_.3), channel_id=1, source_target_pairs={{0,8},{1,17},{2,10},{3,19},{4,12},{5,21},{6,14},{7,23},{8,0},{9,25... | collective-permute-start | bytes 1572872 | tf_op jit(solution)/shard_map/ppermute | solution.py:374
  3.6 8.5 %copy-start = (bf16[1024,1024]{1,0:T(8,128)(2,1)S(1)}, bf16[1024,1024]{1,0:T(8,128)(2,1)}, u32[]{:S(2)}) copy-start(bf16[1024,1024]{1,0:T(8,128)(2,1)} %x_ref.1) | copy-start | bytes 6291460
  3.6 8.5 %copy-start.1 = (bf16[1024,256]{1,0:T(8,128)(2,1)S(1)}, bf16[1024,256]{1,0:T(8,128)(2,1)}, u32[]{:S(2)}) copy-start(bf16[1024,256]{1,0:T(8,128)(2,1)} %wk_ref.1) | copy-start | bytes 1572868
  3.6 8.5 %copy-start.2 = (bf16[1024,256]{1,0:T(8,128)(2,1)S(1)}, bf16[1024,256]{1,0:T(8,128)(2,1)}, u32[]{:S(2)}) copy-start(bf16[1024,256]{1,0:T(8,128)(2,1)} %wv_ref.1) | copy-start | bytes 1572868
  3.6 8.5 %copy-start.4 = (s32[1024]{0:T(1024)S(1)}, s32[1024]{0:T(1024)}, u32[]{:S(2)}) copy-start(s32[1024]{0:T(1024)} %param.20) | copy-start | bytes 12292
  3.6 8.5 %copy-start.7 = (f32[2,4]{1,0:T(2,128)S(1)}, f32[2,4]{1,0:T(2,128)}, u32[]{:S(2)}) copy-start(f32[2,4]{1,0:T(2,128)} %bias_ref.9) | copy-start | bytes 100
  3.7 8.5 %copy-start.8 = (f32[264,128]{1,0:T(8,128)S(1)}, f32[264,128]{1,0:T(8,128)}, u32[]{:S(2)}) copy-start(f32[264,128]{1,0:T(8,128)} %constant.2.clone.refs_5_.table_ref) | copy-start | bytes 405508
  7.8 9.9 %collective-permute-start.2 = (bf16[1040,256]{1,0:T(8,128)(2,1)S(1)}, bf16[1040,256]{1,0:T(8,128)(2,1)S(1)}, u32[]{:S(2)}, u32[]{:S(2)}) collective-permute-start(bf16[1040,256]{1,0:T(8,128)(2,1)S(1)} %get-tuple-element.25.own_ref), channel_id=1, source_target_pairs={{0,1},{1,0},{2,3},{3,2},{4,5},{5,4},{6,7},{7,6},{8,9},{9,8},{10,11... | collective-permute-start | bytes 1597448 | tf_op jit(solution)/shard_map/ppermute | solution.py:365
  7.9 13.5 %collective-permute-start.3 = (bf16[272,256]{1,0:T(8,128)(2,1)S(1)}, bf16[272,256]{1,0:T(8,128)(2,1)S(1)}, u32[]{:S(2)}, u32[]{:S(2)}) collective-permute-start(bf16[272,256]{1,0:T(8,128)(2,1)S(1)} %get-tuple-element.20.refs_1_), channel_id=1, source_target_pairs={{0,4},{1,5},{2,6},{3,7},{4,0},{5,1},{6,2},{7,3},{8,12},{9,13},{10,... | collective-permute-start | bytes 417800 | tf_op jit(solution)/shard_map/ppermute | solution.py:365
  10.5 13.1 %collective-permute-start.1 = (bf16[272,256]{1,0:T(8,128)(2,1)S(1)}, bf16[272,256]{1,0:T(8,128)(2,1)S(1)}, u32[]{:S(2)}, u32[]{:S(2)}) collective-permute-start(bf16[272,256]{1,0:T(8,128)(2,1)S(1)} %get-tuple-element.21.refs_2_), channel_id=1, source_target_pairs={{0,6},{1,7},{2,4},{3,5},{4,2},{5,3},{6,0},{7,1},{8,14},{9,15},{10,... | collective-permute-start | bytes 417800 | tf_op jit(solution)/shard_map/ppermute | solution.py:365
  11.9 13.3 %collective-permute-start.5 = (bf16[272,256]{1,0:T(8,128)(2,1)S(1)}, bf16[272,256]{1,0:T(8,128)(2,1)S(1)}, u32[]{:S(2)}, u32[]{:S(2)}) collective-permute-start(bf16[272,256]{1,0:T(8,128)(2,1)S(1)} %get-tuple-element.22.refs_3_), channel_id=1, source_target_pairs={{0,2},{1,3},{2,0},{3,1},{4,6},{5,7},{6,4},{7,5},{8,10},{9,11},{10,... | collective-permute-start | bytes 417800 | tf_op jit(solution)/shard_map/ppermute | solution.py:365
  16.1 15.6 %collective-permute-start.9 = (bf16[256,1024]{1,0:T(8,128)(2,1)S(1)}, bf16[256,1024]{1,0:T(8,128)(2,1)S(1)}, u32[]{:S(2)}, u32[]{:S(2)}) collective-permute-start(bf16[256,1024]{1,0:T(8,128)(2,1)S(1)} %get-tuple-element.26), channel_id=1, source_target_pairs={{0,16},{1,9},{2,18},{3,11},{4,20},{5,13},{6,22},{7,15},{8,24},{9,1... | collective-permute-start | bytes 1572872 | tf_op jit(solution)/shard_map/ppermute | solution.py:374
  17.7 14.0 %collective-permute-start.8 = (bf16[256,1024]{1,0:T(8,128)(2,1)S(1)}, bf16[256,1024]{1,0:T(8,128)(2,1)S(1)}, u32[]{:S(2)}, u32[]{:S(2)}) collective-permute-start(bf16[256,1024]{1,0:T(8,128)(2,1)S(1)} %get-tuple-element.26), channel_id=1, source_target_pairs={{0,1},{1,0},{2,3},{3,2},{4,5},{5,4},{6,7},{7,6},{8,9},{9,8},{10,11... | collective-permute-start | bytes 1572872 | tf_op jit(solution)/shard_map/ppermute | solution.py:365
  22.8 8.8 %collective-permute-start.7 = (bf16[272,256]{1,0:T(8,128)(2,1)S(1)}, bf16[272,256]{1,0:T(8,128)(2,1)S(1)}, u32[]{:S(2)}, u32[]{:S(2)}) collective-permute-start(bf16[272,256]{1,0:T(8,128)(2,1)S(1)} %cache_part.5.refs_0_), channel_id=1, source_target_pairs={{0,4},{1,5},{2,6},{3,7},{4,0},{5,1},{6,2},{7,3},{8,12},{9,13},{10,... | collective-permute-start | bytes 417800 | tf_op jit(solution)/shard_map/ppermute | solution.py:365
  26.7 8.7 %collective-permute-start.6 = (bf16[272,256]{1,0:T(8,128)(2,1)S(1)}, bf16[272,256]{1,0:T(8,128)(2,1)S(1)}, u32[]{:S(2)}, u32[]{:S(2)}) collective-permute-start(bf16[272,256]{1,0:T(8,128)(2,1)S(1)} %cache_part.7.refs_2_), channel_id=1, source_target_pairs={{0,2},{1,3},{2,0},{3,1},{4,6},{5,7},{6,4},{7,5},{8,10},{9,11},{10,... | collective-permute-start | bytes 417800 | tf_op jit(solution)/shard_map/ppermute | solution.py:365
  29.7 7.9 %collective-permute-start.4 = (bf16[272,256]{1,0:T(8,128)(2,1)S(1)}, bf16[272,256]{1,0:T(8,128)(2,1)S(1)}, u32[]{:S(2)}, u32[]{:S(2)}) collective-permute-start(bf16[272,256]{1,0:T(8,128)(2,1)S(1)} %cache_part.6.refs_0_), channel_id=1, source_target_pairs={{0,6},{1,7},{2,4},{3,5},{4,2},{5,3},{6,0},{7,1},{8,14},{9,15},{10,... | collective-permute-start | bytes 417800 | tf_op jit(solution)/shard_map/ppermute | solution.py:365
  31.9 16.8 %copy-start.3 = (bf16[256,1024]{1,0:T(8,128)(2,1)S(1)}, bf16[256,1024]{1,0:T(8,128)(2,1)}, u32[]{:S(2)}) copy-start(bf16[256,1024]{1,0:T(8,128)(2,1)} %refs_4_.3) | copy-start | bytes 1572868
  31.9 16.8 %copy-start.5 = (f32[1024]{0:T(1024)S(1)}, f32[1024]{0:T(1024)}, u32[]{:S(2)}) copy-start(f32[1024]{0:T(1024)} %param.31) | copy-start | bytes 12292
  31.9 16.8 %copy-start.6 = (f32[1024]{0:T(1024)S(1)}, f32[1024]{0:T(1024)}, u32[]{:S(2)}) copy-start(f32[1024]{0:T(1024)} %param.32) | copy-start | bytes 12292
  31.9 8.0 %collective-permute-start.13 = (bf16[512,256]{1,0:T(8,128)(2,1)S(1)}, bf16[512,256]{1,0:T(8,128)(2,1)S(1)}, u32[]{:S(2)}, u32[]{:S(2)}) collective-permute-start(bf16[512,256]{1,0:T(8,128)(2,1)S(1)} %merge.2.refs_2_.refs_0_), channel_id=1, source_target_pairs={{0,8},{1,17},{2,10},{3,19},{4,12},{5,21},{6,14},{7,23},{8,0},{9,25... | collective-permute-start | bytes 786440 | tf_op jit(solution)/shard_map/ppermute | solution.py:374
  37.8 9.2 %collective-permute-start.10 = (bf16[512,256]{1,0:T(8,128)(2,1)S(1)}, bf16[512,256]{1,0:T(8,128)(2,1)S(1)}, u32[]{:S(2)}, u32[]{:S(2)}) collective-permute-start(bf16[512,256]{1,0:T(8,128)(2,1)S(1)} %merge.3.refs_0_), channel_id=1, source_target_pairs={{0,8},{1,17},{2,10},{3,19},{4,12},{5,21},{6,14},{7,23},{8,0},{9,25... | collective-permute-start | bytes 786440 | tf_op jit(solution)/shard_map/ppermute | solution.py:374
  38.5 10.2 %collective-permute-start.14 = (bf16[512,256]{1,0:T(8,128)(2,1)S(1)}, bf16[512,256]{1,0:T(8,128)(2,1)S(1)}, u32[]{:S(2)}, u32[]{:S(2)}) collective-permute-start(bf16[512,256]{1,0:T(8,128)(2,1)S(1)} %merge.2.refs_2_.refs_0_), channel_id=1, source_target_pairs={{0,16},{1,9},{2,18},{3,11},{4,20},{5,13},{6,22},{7,15},{8,24},{9,1... | collective-permute-start | bytes 786440 | tf_op jit(solution)/shard_map/ppermute | solution.py:374
  39.9 8.7 %collective-permute-start.15 = (bf16[512,256]{1,0:T(8,128)(2,1)S(1)}, bf16[512,256]{1,0:T(8,128)(2,1)S(1)}, u32[]{:S(2)}, u32[]{:S(2)}) collective-permute-start(bf16[512,256]{1,0:T(8,128)(2,1)S(1)} %collective-permute-done.13.refs_1_), channel_id=1, source_target_pairs={{0,16},{1,9},{2,18},{3,11},{4,20},{5,13},{6,22},{7,15},{8,24},{9,1... | collective-permute-start | bytes 786440 | tf_op jit(solution)/shard_map/ppermute | solution.py:374
  40.5 11.6 %collective-permute-start.11 = (bf16[512,256]{1,0:T(8,128)(2,1)S(1)}, bf16[512,256]{1,0:T(8,128)(2,1)S(1)}, u32[]{:S(2)}, u32[]{:S(2)}) collective-permute-start(bf16[512,256]{1,0:T(8,128)(2,1)S(1)} %merge.3.refs_0_), channel_id=1, source_target_pairs={{0,16},{1,9},{2,18},{3,11},{4,20},{5,13},{6,22},{7,15},{8,24},{9,1... | collective-permute-start | bytes 786440 | tf_op jit(solution)/shard_map/ppermute | solution.py:374
  47.0 6.8 %collective-permute-start.12 = (bf16[512,256]{1,0:T(8,128)(2,1)S(1)}, bf16[512,256]{1,0:T(8,128)(2,1)S(1)}, u32[]{:S(2)}, u32[]{:S(2)}) collective-permute-start(bf16[512,256]{1,0:T(8,128)(2,1)S(1)} %collective-permute-done.10.refs_1_), channel_id=1, source_target_pairs={{0,16},{1,9},{2,18},{3,11},{4,20},{5,13},{6,22},{7,15},{8,24},{9,1... | collective-permute-start | bytes 786440 | tf_op jit(solution)/shard_map/ppermute | solution.py:374

commit v5 on v4

--- a/solution.py
+++ b/solution.py
@@ -20,7 +20,6 @@
 HBM = pl.BlockSpec(memory_space=pltpu.HBM)
 ANY = pl.BlockSpec(memory_space=pl.ANY)
 DMA = pltpu.SemaphoreType.DMA
-GROUPS = [[0, 1], [2, 3]]
 LIMIT = 32 * 1024 * 1024
 
 
@@ -228,8 +227,10 @@
     home_any, bias_ref, x_ref, wk_ref, wv_ref, var_ref, table_ref, base_ref,
     *refs
 ):
-    w_ref, out_ref, x_home_ref, w_copy_ref, k_ref, v_ref, home_ref, sem = refs[-8:]
-    q_refs = refs[:-8]
+    w_ref, out_ref, x_part_ref, count_ref, w_copy_ref, k_ref, v_ref, home_ref, sem = refs[-9:]
+    q_refs = refs[:-9]
+    part = x_part_ref.shape[0] // var_ref.shape[0]
+    part_start = lax.axis_index("head") * part
     w_copy_ref[...] = w_ref[...]
     slots, width = var_ref.shape
     cols = wk_ref.shape[1]
@@ -244,7 +245,8 @@
         slot = home_ref[n]
         cos, sin = slot_tables(slot, base_ref, cos_ref, sin_ref, rows_ref)
         at = pl.ds(pl.multiple_of(slot * width, width), width)
-        x_home_ref[n * width : (n + 1) * width, :] = x_ref[at, :]
+        part_at = pl.ds(pl.multiple_of(slot * width + part_start, part), part)
+        x_part_ref[n * part : (n + 1) * part, :] = x_ref[part_at, :]
         key = turn(k_ref[at, :], cos, sin).astype(BF)
         value = v_ref[at, :].T.astype(BF)
         query = q_refs[n // 2][n % 2 * width : (n % 2 + 1) * width, :]
@@ -252,6 +254,7 @@
         var = jnp.broadcast_to(var_ref[pl.ds(slot, 1), :].astype(F32), (width, width))
         same = var.T == var
         count = base_ref[4, pl.ds(slot, 1), :]
+        count_ref[n : n + 1, :] = count
         key_second = lax.broadcasted_iota(jnp.int32, (width, width), 0).astype(F32) >= count
         tok_second = lax.broadcasted_iota(jnp.int32, (width, width), 1).astype(F32) >= count
         allowed = jnp.logical_not(jnp.logical_xor(key_second, tok_second))
@@ -261,63 +264,81 @@
         part_ref[cols:, :] = stats
 
 
-def merge_kernel(firsts, own_ref, *refs):
+def distances():
+    core = lax.axis_index("blk") % 2
+    return [0, 1 + core, 2 - core, 3]
+
+
+def merge(first, got_ref, own_ref, out_ref, start):
+    cols = got_ref.shape[0] - EXTRA
+    heads = cols // DH
+    width = got_ref.shape[1] // 2
+    for j in range(2):
+        at = slice(j * width, (j + 1) * width)
+        stats = got_ref[cols:, at].astype(F32)
+        there = stats[0:heads] + stats[heads : 2 * heads] + stats[2 * heads : 3 * heads]
+        here = own_ref[first + j, cols : cols + heads, :]
+        peak = jnp.maximum(there, here)
+        there, here = jnp.exp(there - peak), jnp.exp(here - peak)
+        inverse = 1.0 / (there + here)
+        there, here = there * inverse, here * inverse
+        parts = []
+        for h in range(heads):
+            row = slice(h * DH, (h + 1) * DH)
+            parts.append(
+                got_ref[row, at].astype(F32) * there[h : h + 1]
+                + own_ref[first + j, row, :] * here[h : h + 1]
+            )
+        to = slice(start + j * width, start + (j + 1) * width)
+        out_ref[to, :] = jnp.concatenate(parts, axis=0).T.astype(BF)
+
+
+def merge_kernel(chunk, own_ref, got_ref, *refs):
     out_ref = refs[-1]
-    for i, (first, got_ref) in enumerate(zip(firsts, refs)):
-        cols = got_ref.shape[0] - EXTRA
-        heads = cols // DH
-        width = got_ref.shape[1] // 2
-        for j in range(2):
-            at = slice(j * width, (j + 1) * width)
-            stats = got_ref[cols:, at].astype(F32)
-            there = stats[0:heads] + stats[heads : 2 * heads] + stats[2 * heads : 3 * heads]
-            here = own_ref[first + j, cols : cols + heads, :]
-            peak = jnp.maximum(there, here)
-            there, here = jnp.exp(there - peak), jnp.exp(here - peak)
-            inverse = 1.0 / (there + here)
-            there, here = there * inverse, here * inverse
-            parts = []
-            for h in range(heads):
-                row = slice(h * DH, (h + 1) * DH)
-                parts.append(
-                    got_ref[row, at].astype(F32) * there[h : h + 1]
-                    + own_ref[first + j, row, :] * here[h : h + 1]
-                )
-            to = slice((2 * i + j) * width, (2 * i + j + 1) * width)
-            out_ref[to, :] = jnp.concatenate(parts, axis=0).T.astype(BF)
-
-
-def output_kernel(firsts, home_any, *refs):
-    att_refs, w_refs = refs[:4], refs[4:8]
-    x_ref, base_ref, gain_ref, read_ref = refs[8:12]
-    before = refs[12:-6]
-    update_hbm, pooled_ref, gr_ref, out_ref, home_ref, sems = refs[-6:]
+    merge(2 * chunk, got_ref, own_ref, out_ref, 0)
+
+
+def last_merge_kernel(chunk, earlier, own_ref, got_ref, *refs):
+    att_refs = [*refs[:earlier], refs[-1]]
+    out_refs = refs[-5:-1]
+    merge(2 * chunk, got_ref, own_ref, refs[-1], 0)
+    slots = 2 * len(att_refs)
+    width = refs[-1].shape[0] // 2
+    part = out_refs[0].shape[0] // slots
+    head = lax.axis_index("head")
+    for distance, out_ref in zip(distances(), out_refs):
+        for n in range(slots):
+            start = pl.multiple_of(n % 2 * width + (head ^ distance) * part, part)
+            out_ref[n * part : (n + 1) * part, :] = att_refs[n // 2][pl.ds(start, part), :]
+
+
+def output_kernel(*refs):
+    att_halves, refs = (refs[0:4], refs[4:8]), refs[8:]
+    w_refs = refs[:4]
+    x_ref, count_ref, gain_ref, read_ref = refs[4:8]
+    mine_ref, sums_ref = refs[8:10]
+    send_refs, gr_ref, att_refs = refs[10:13], refs[13], refs[14:]
+    for first_ref, second_ref, att_ref in zip(*att_halves, att_refs):
+        att_ref[0 : first_ref.shape[0], :] = first_ref[...]
+        att_ref[first_ref.shape[0] :, :] = second_ref[...]
     tokens, cols = att_refs[0].shape
     depth = w_refs[0].shape[1]
-    width = tokens // (2 * len(firsts))
-    places = [first + j for first in firsts for j in range(2)]
-    here = [slice(i * width, (i + 1) * width) for i in range(len(places))]
-    home_move = pltpu.make_async_copy(home_any, home_ref, sems.at[len(places)])
-    home_move.start()
+    slots = count_ref.shape[0]
+    part = tokens // slots
     gr_ref[...] = gain_ref[...] * read_ref[...]
     head = lax.axis_index("head")
     square = jnp.zeros((tokens, LANES), F32)
     weighted = jnp.zeros((tokens, LANES), F32)
-    for c in range(depth // cols):
-        start = (head + c) % (depth // cols) * cols
-        at = pl.ds(pl.multiple_of(start, cols), cols)
+    for c, distance in enumerate(distances()):
+        at = pl.ds(pl.multiple_of((head ^ distance) * cols, cols), cols)
         total = dot(att_refs[0][...], w_refs[0][:, at])
         for att_ref, w_ref in zip(att_refs[1:], w_refs[1:]):
             total = total + dot(att_ref[...], w_ref[:, at])
         if c == 0:
-            out_ref[...] = total
-            home_move.wait()
-            found = [home_ref[place] for place in places]
-            slots = [pl.ds(pl.multiple_of(slot * width, width), width) for slot in found]
-            writes = copies(
-                [out_ref.at[row] for row in here], [update_hbm.at[row] for row in slots], sems
-            )
-        hidden = x_ref[places[0] * width : (places[-1] + 1) * width, at].astype(F32) + total
+            mine_ref[...] = total
+        else:
+            send_refs[c - 1][0:tokens, :] = total.astype(BF)
+        hidden = x_ref[:, at].astype(F32) + total
         scaled = hidden * gr_ref[:, at]
         hidden = hidden * hidden
         for lane in range(0, cols, LANES):
@@ -326,20 +347,64 @@
     square = jnp.sum(square, axis=1, keepdims=True)
     weighted = jnp.sum(weighted, axis=1, keepdims=True)
     score = weighted * lax.rsqrt(square / depth + 1e-06)
-    token = lax.broadcasted_iota(jnp.int32, (width, 1), 0).astype(F32)
+    token = lax.broadcasted_iota(jnp.int32, (part, 1), 0) + head * part
     lane = lax.broadcasted_iota(jnp.int32, (1, LANES), 1)
-    pooled = before[1][...] if before else jnp.zeros((1, LANES), F32)
-    for slot, row in zip(found, here):
-        count_one = base_ref[4, pl.ds(slot, 1), 0:1]
-        is_first = token < count_one
-        part = score[row, :]
-        sum_one = jnp.sum(jnp.where(is_first, part, 0.0), axis=0, keepdims=True)
-        sum_two = jnp.sum(jnp.where(is_first, 0.0, part), axis=0, keepdims=True)
-        pooled = jnp.where(lane == 2 * slot, sum_one / count_one, pooled)
-        pooled = jnp.where(lane == 2 * slot + 1, sum_two / (width - count_one), pooled)
+    sums = jnp.zeros((1, LANES), F32)
+    for n in range(slots):
+        is_first = token.astype(F32) < count_ref[n : n + 1, 0:1]
+        piece = score[n * part : (n + 1) * part, :]
+        sum_one = jnp.sum(jnp.where(is_first, piece, 0.0), axis=0, keepdims=True)
+        sum_two = jnp.sum(jnp.where(is_first, 0.0, piece), axis=0, keepdims=True)
+        sums = jnp.where(lane == 2 * n, sum_one, sums)
+        sums = jnp.where(lane == 2 * n + 1, sum_two, sums)
+    sums_ref[...] = jnp.broadcast_to(sums, sums_ref.shape)
+    high = sums.astype(BF).astype(F32)
+    middle = (sums - high).astype(BF).astype(F32)
+    low = sums - high - middle
+    block = jnp.concatenate([high, middle, low, jnp.zeros((EXTRA - 3, LANES), F32)], axis=0)
+    block = jnp.concatenate([block] * (cols // LANES), axis=1).astype(BF)
+    for send_ref in send_refs:
+        send_ref[tokens:, :] = block
+
+
+def place_kernel(home_any, mine_ref, *refs):
+    got_refs = refs[:3]
+    sums_ref, count_ref, update_hbm, pooled_ref, stage_ref, home_ref, sems = refs[3:]
+    slots = count_ref.shape[0]
+    home_move = pltpu.make_async_copy(home_any, home_ref, sems.at[slots])
+    home_move.start()
+    tokens = mine_ref.shape[0]
+    part = tokens // slots
+    width = stage_ref.shape[0] // slots
+    head = lax.axis_index("head")
+    for n in range(slots):
+        for distance, ref in zip(distances(), (mine_ref, *got_refs)):
+            start = pl.multiple_of(n * width + (head ^ distance) * part, part)
+            stage_ref[pl.ds(start, part), :] = ref[n * part : (n + 1) * part, :].astype(F32)
+    home_move.wait()
+    moves = []
+    for n in range(slots):
+        to = pl.ds(pl.multiple_of(home_ref[n] * width, width), width)
+        move = pltpu.make_async_copy(
+            stage_ref.at[n * width : (n + 1) * width], update_hbm.at[to], sems.at[n]
+        )
+        move.start()
+        moves.append(move)
+    sums = sums_ref[0:1, :]
+    for ref in got_refs:
+        block = ref[tokens:, 0:LANES].astype(F32)
+        sums = sums + (block[0:1] + block[1:2] + block[2:3])
+    lane = lax.broadcasted_iota(jnp.int32, (1, LANES), 1)
+    pooled = jnp.zeros((1, LANES), F32)
+    for n in range(slots):
+        slot, count = home_ref[n], count_ref[n : n + 1, 0:1]
+        pooled = jnp.where(lane == 2 * slot, sums[:, 2 * n : 2 * n + 1] / count, pooled)
+        pooled = jnp.where(
+            lane == 2 * slot + 1, sums[:, 2 * n + 1 : 2 * n + 2] / (width - count), pooled
+        )
     pooled_ref[...] = pooled[:, : pooled_ref.shape[1]]
-    for write in writes:
-        write.wait()
+    for move in moves:
+        move.wait()
 
 
 def call(kernel, out, ins, scratch=(), work=1, **kwargs):
@@ -401,11 +466,12 @@
     rows, depth = doc_x.shape
     cols = w_query.shape[1]
     blocks = lax.axis_size("blk")
+    heads = lax.axis_size("head")
     bpq = blocks // QUERIES
     slots = QUERIES
     width = rows // slots
     chunks = blocks // 2
-    order = [0, 2, 3, 1] + list(range(4, chunks))
+    order = list(range(chunks))
     cache_rows = cache_k.shape[0]
     seg = doc_seg.reshape(slots, width)
     var = doc_var.reshape(slots, width)
@@ -455,15 +521,18 @@
             every[2 * k : 2 * k + 2].reshape(2 * width, cols) for k in range(slots // 2)
         ]
 
-    own, x_home, w_copy = call(
+    own, x_part, count, w_copy = call(
         own_kernel,
-        [sds((slots, cols + 8, width), F32), sds((rows, depth), BF), sds(w_out.shape, BF)],
+        [
+            sds((slots, cols + 8, width), F32), sds((rows // heads, depth), BF),
+            sds((slots, width), F32), sds(w_out.shape, BF),
+        ],
         [ANY] + [VMEM] * (8 + len(home_queries)),
         [
             pltpu.VMEM((rows, cols), F32), pltpu.VMEM((rows, cols), F32),
             pltpu.SMEM(home.shape, i32), DMA,
         ],
-        out_specs=[VMEM] * 3,
+        out_specs=[VMEM] * 4,
         work=4.0,
         name="own_documents",
     )(home, var_bias, doc_x, w_key, w_value, var, table, base, *home_queries, w_first)
@@ -484,46 +553,74 @@
         parts.append(part)
     backs = [parts[0]] + [partner(parts[k], "blk", 2 * order[k]) for k in range(1, chunks)]
 
-    groups = GROUPS
+    def spread(a, b, c):
+        return [hop(a, 1, 2), hop(b, 2, 1), partner(c, "head", 3)]
+
+    part_shape = sds((rows // heads // 2, cols), BF)
+    halves = []
     if bpq == 1:
-        attended = []
-        for group in groups:
-            after = attended[-1:] or [parts[-1], w_second, w_third]
-            attended.append(
-                call(
-                    functools.partial(merge_kernel, [2 * k for k in group]),
-                    sds((2 * width * len(group), cols), BF),
-                    [VMEM] * (len(group) + 1) + [ANY] * len(after),
-                    out_specs=VMEM,
-                    work=20 if attended else 0.2,
-                    name="merge",
-                )(own, *[backs[k] for k in group], *after)
-            )
+        chunk_att = sds((2 * width, cols), BF)
+        after, waiting = [parts[-1], w_second, w_third], []
+        for group in (range(chunks // 2), range(chunks // 2, chunks)):
+            attended = []
+            for k in group[:-1]:
+                attended.append(
+                    call(
+                        functools.partial(merge_kernel, k),
+                        chunk_att,
+                        [VMEM] * 2 + [ANY] * len(after),
+                        out_specs=VMEM,
+                        work=20 if halves else 0.2,
+                        name="merge",
+                    )(own, backs[k], *after)
+                )
+                after = attended[-1:]
+            pieces = call(
+                functools.partial(last_merge_kernel, group[-1], len(attended)),
+                [part_shape] * 4,
+                [VMEM] * (2 + len(attended)) + [ANY] * len(after + waiting),
+                [pltpu.VMEM(chunk_att.shape, BF)],
+                out_specs=[VMEM] * 4,
+                work=20 if halves else 0.2,
+                name="last_merge",
+            )(own, backs[group[-1]], *attended, *after, *waiting)
+            halves.append([pieces[0], *spread(*pieces[1:])])
+            after, waiting = pieces[:1], halves[-1][1:]
     else:
         attended = spread_merge(backs, own, pick, slots, bpq)
-        attended = [jnp.concatenate([attended[k] for k in group]) for group in groups]
+        attended = jnp.concatenate(attended).reshape(slots, width, cols)
+        head, part = lax.axis_index("head"), width // heads
+        pieces = [
+            lax.dynamic_slice_in_dim(attended, (head ^ distance) * part, part, 1)
+            for distance in distances()
+        ]
+        pieces = [piece.reshape(2, *part_shape.shape) for piece in pieces]
+        halves = [[piece[i] for piece in pieces] for i in range(2)]
+        halves = [[piece, *spread(*others)] for piece, *others in halves]
 
     gain, read = norm_gain.reshape(1, depth), readout.reshape(1, depth)
-    chained = []
-    for group, own_part in zip(groups, attended):
-        near = hop(own_part, 1, 2)
-        atts = [own_part, near, hop(own_part, 2, 1), hop(near, 2, 1)]
-        places = 2 * len(group)
-        last = group is groups[-1]
-        chained = call(
-            functools.partial(output_kernel, [2 * k for k in group]),
-            [sds((rows, cols), F32), sds((1, 2 * slots if last else LANES), F32)],
-            [ANY] + [VMEM] * 12 + [HBM, VMEM][: len(chained)],
-            [
-                pltpu.VMEM((1, depth), F32), pltpu.VMEM((places * width, cols), F32),
-                pltpu.SMEM(home.shape, i32), DMA((places + 1,)),
-            ],
-            out_specs=[HBM, VMEM],
-            input_output_aliases={13: 0} if chained else {},
-            work=2.5,
-            name="output",
-        )(home, *atts, w_out, w_first, w_second, w_third, x_home, base, gain, read, *chained)
-    update, pooled = chained
+    send_shape = sds((rows // heads + EXTRA, cols), BF)
+    mine, sums, *sends = call(
+        output_kernel,
+        [sds((rows // heads, cols), F32), sds((8, LANES), F32)] + [send_shape] * 3,
+        [VMEM] * 16,
+        [pltpu.VMEM((1, depth), F32)] + [pltpu.VMEM((rows // heads, cols), BF)] * 4,
+        out_specs=[VMEM] * 5,
+        work=2.0,
+        name="output",
+    )(
+        *halves[0], *halves[1],
+        w_out, w_first, w_second, w_third, x_part, count, gain, read,
+    )
+    update, pooled = call(
+        place_kernel,
+        [sds((rows, cols), F32), sds((1, 2 * slots), F32)],
+        [ANY] + [VMEM] * 6,
+        [pltpu.VMEM((rows, cols), F32), pltpu.SMEM(home.shape, i32), DMA((slots + 1,))],
+        out_specs=[HBM, VMEM],
+        work=1.5,
+        name="place",
+    )(home, mine, *spread(*sends), sums, count)
     return (update, pooled.reshape(2 * slots))
 
 

time: 58 us -> 56.6 us (0.976)
  Pallas kernels: 21.4 us -> 17.7 us
  starting transfers between devices: 20.2 us -> 23.3 us
    pallas_call x5 -> x7, Pallas kernels: 11.2 us -> 7.62 us  [the longest x1 3.92 us: body(): call(own_kernel, [sds((slots, cols + 8, width), F32), sds((rows // heads,...]
    ppermute x8 -> x11, starting transfers between devices: 9.43 us -> 12.6 us  [partner(): return lax.ppermute(value, axis, [(i, i ^ k) for i in range(count)])]
    ppermute x8, waiting for transfers between devices: 6.7 us -> 5.93 us  [hop(): return lax.ppermute(value, ('head', 'blk'), pairs)]
    ppermute x8 -> x11, waiting for transfers between devices: 8.07 us -> 8.47 us  [partner(): return lax.ppermute(value, axis, [(i, i ^ k) for i in range(count)])]
  transfers between devices with their start and end apart: 16 -> 19, of which waited for: 6 -> 7; matrix products, arithmetic and copies ran while one was open for 0% -> 0% of each run, Pallas kernels for 31% -> 26%
where the time goes in v5:
time: 56.6 us; the launch traced here: 56.4 us
  starting transfers between devices  23.3 us (41%)
  Pallas kernels  17.7 us (31%)
  waiting for transfers between devices  14.4 us (25%)
  between operations  0.87 us (2%)
    ppermute x11, starting transfers between devices, partner(): return lax.ppermute(value, axis, [(i, i ^ k) for i in range(count)])  12.6 us
    ppermute x8, starting transfers between devices, hop(): return lax.ppermute(value, ('head', 'blk'), pairs)  10.8 us
    ppermute x11, waiting for transfers between devices, partner(): return lax.ppermute(value, axis, [(i, i ^ k) for i in range(count)])  8.47 us
    pallas_call x4, Pallas kernels, body(): call(cache_kernel, chunk_shape, [VMEM] * 5 + [ANY] * len(after), out_spec...  6.01 us
    ppermute x8, waiting for transfers between devices, hop(): return lax.ppermute(value, ('head', 'blk'), pairs)  5.93 us
    pallas_call x1, Pallas kernels, body(): call(functools.partial(query_kernel, bpq, order), [sds((blocks,), i32), b...  4.11 us
    pallas_call x1, Pallas kernels, body(): call(own_kernel, [sds((slots, cols + 8, width), F32), sds((rows // heads,...  3.92 us
    pallas_call x1, Pallas kernels, body(): call(place_kernel, [sds((rows, cols), F32), sds((1, 2 * slots), F32)], [A...  2.09 us
  transfers between devices with their start and end apart: 19, of which 7 were waited for; matrix products, arithmetic and copies ran while one was open for 0% of the time, Pallas kernels for 26%

profile of v5, /device:TPU:0, one launch (start us, length us, event | category | flops | bytes accessed | tf_op | source)
XLA Modules:
  0.0 56.4 jit_solution(1955510323788215948)
XLA Ops:
  0.6 3.0 %collective-permute-start = (bf16[256,1024]{1,0:T(8,128)(2,1)}, bf16[256,1024]{1,0:T(8,128)(2,1)S(1)}, u32[]{:S(2)}, u32[]{:S(2)}) collective-permute-start(bf16[256,1024]{1,0:T(8,128)(2,1)} %refs_8_.3), channel_id=1, source_target_pairs={{0,8},{1,17},{2,10},{3,19},{4,12},{5,21},{6,14},{7,23},{8,0},{9,25... | collective-permute-start | bytes 1572872 | tf_op jit(solution)/shard_map/ppermute | solution.py:439
  3.7 0.0 copy-start.8
  3.7 4.1 %query.1 = (s32[8]{0:T(128)S(1)}, f32[5,8,128]{2,1,0:T(8,128)S(1)}, s32[8,128]{1,0:T(8,128)S(1)}, bf16[1040,256]{1,0:T(8,128)(2,1)S(1)}, bf16[272,256]{1,0:T(8,1...) custom-call(s32[128]{0:T(128)} %refs_0_.1, s32[8]{0:T(128)} %refs_1_.1, ...), custom_call_target="tpu_custom_call" | custom-call | flops 3500000000 | tf_op jit(solution)/shard_map/query/pallas_call | solution.py:487
  7.8 0.1 collective-permute-start.2
  7.9 1.6 %collective-permute-start.1 = (bf16[272,256]{1,0:T(8,128)(2,1)S(1)}, bf16[272,256]{1,0:T(8,128)(2,1)S(1)}, u32[]{:S(2)}, u32[]{:S(2)}) collective-permute-start(bf16[272,256]{1,0:T(8,128)(2,1)S(1)} %get-tuple-element.32.refs_1_), channel_id=1, source_target_pairs={{0,2},{1,3},{2,0},{3,1},{4,6},{5,7},{6,4},{7,5},{8,10},{9,11},{10,... | collective-permute-start | bytes 417800 | tf_op jit(solution)/shard_map/ppermute | solution.py:430
  9.5 2.6 %collective-permute-start.5 = (bf16[272,256]{1,0:T(8,128)(2,1)S(1)}, bf16[272,256]{1,0:T(8,128)(2,1)S(1)}, u32[]{:S(2)}, u32[]{:S(2)}) collective-permute-start(bf16[272,256]{1,0:T(8,128)(2,1)S(1)} %get-tuple-element.33.refs_2_), channel_id=1, source_target_pairs={{0,4},{1,5},{2,6},{3,7},{4,0},{5,1},{6,2},{7,3},{8,12},{9,13},{10,... | collective-permute-start | bytes 417800 | tf_op jit(solution)/shard_map/ppermute | solution.py:430
  12.1 0.2 collective-permute-start.4
  12.4 3.9 %own_documents.1 = (f32[8,264,128]{2,1,0:T(8,128)S(1)}, bf16[256,1024]{1,0:T(8,128)(2,1)S(1)}, f32[8,128]{1,0:T(8,128)S(1)}, bf16[256,1024]{1,0:T(8,128)(2,1)S(1)}) custom-call(s32[8]{0:T(128)S(1)} %get-tuple-element.29.home_any, f32[2,4]{1,0:T(2,128)S(1)} %copy-done.7, bf16[1024,1024]{1,0:T(8,128)(2,1)S(1)} %copy-done, bf16[1024,256]{1,0:T(8,128)(2,1)S(1)} %copy-done.1, ...), custom_call_target="tpu_custom_call" | custom-call | flops 4000000000 | tf_op jit(solution)/shard_map/own_documents/pallas_call | solution.py:524
  16.3 0.1 collective-permute-start.6
  16.4 1.6 %collective-permute-start.7 = (bf16[256,1024]{1,0:T(8,128)(2,1)S(1)}, bf16[256,1024]{1,0:T(8,128)(2,1)S(1)}, u32[]{:S(2)}, u32[]{:S(2)}) collective-permute-start(bf16[256,1024]{1,0:T(8,128)(2,1)S(1)} %get-tuple-element.38), channel_id=1, source_target_pairs={{0,16},{1,9},{2,18},{3,11},{4,20},{5,13},{6,22},{7,15},{8,24},{9,1... | collective-permute-start | bytes 1572872 | tf_op jit(solution)/shard_map/ppermute | solution.py:439
  18.0 1.5 %cache_part.4.refs_0_.got_ref = bf16[272,256]{1,0:T(8,128)(2,1)S(1)} custom-call(s32[8,128]{1,0:T(8,128)S(1)} %get-tuple-element.36.usable_ref, f32[2,4]{1,0:T(2,128)S(1)} %copy-done.7, bf16[272,256]{1,0:T(8,128)(2,1)S(1)} %get-tuple-element.31.refs_0_.q_ref, bf16[1040,256]{1,0:T(8,128)(2,1)S(1)} %get-tuple-element.37.own_ref, ...), custom_call_target="tpu_custom_call" | custom-call | flops 1500000000 | tf_op jit(solution)/shard_map/cache_part/pallas_call | solution.py:545
  19.5 1.5 %cache_part.5.refs_0_ = bf16[272,256]{1,0:T(8,128)(2,1)S(1)} custom-call(s32[8,128]{1,0:T(8,128)S(1)} %get-tuple-element.36.usable_ref, f32[2,4]{1,0:T(2,128)S(1)} %copy-done.7, bf16[272,256]{1,0:T(8,128)(2,1)S(1)} %collective-permute-done.1.q_ref, bf16[1040,256]{1,0:T(8,128)(2,1)S(1)} %get-tuple-element.37.own_ref, ...), custom_call_target="tpu_custom_call" | custom-call | flops 1500000000 | tf_op jit(solution)/shard_map/cache_part/pallas_call | solution.py:545
  21.0 0.9 %collective-permute-start.3 = (bf16[272,256]{1,0:T(8,128)(2,1)S(1)}, bf16[272,256]{1,0:T(8,128)(2,1)S(1)}, u32[]{:S(2)}, u32[]{:S(2)}) collective-permute-start(bf16[272,256]{1,0:T(8,128)(2,1)S(1)} %cache_part.5.refs_0_), channel_id=1, source_target_pairs={{0,2},{1,3},{2,0},{3,1},{4,6},{5,7},{6,4},{7,5},{8,10},{9,11},{10,... | collective-permute-start | bytes 417800 | tf_op jit(solution)/shard_map/ppermute | solution.py:430
  21.9 1.1 %collective-permute-done.5.q_ref = bf16[272,256]{1,0:T(8,128)(2,1)S(1)} collective-permute-done((bf16[272,256]{1,0:T(8,128)(2,1)S(1)}, bf16[272,256]{1,0:T(8,128)(2,1)S(1)}, u32[]{:S(2)}, u32[]{:S(2)}) %collective-permute-start.5) | collective-permute-done | bytes 139296 | tf_op jit(solution)/shard_map/ppermute | solution.py:430
  22.9 1.5 %cache_part.6.refs_0_ = bf16[272,256]{1,0:T(8,128)(2,1)S(1)} custom-call(s32[8,128]{1,0:T(8,128)S(1)} %get-tuple-element.36.usable_ref, f32[2,4]{1,0:T(2,128)S(1)} %copy-done.7, bf16[272,256]{1,0:T(8,128)(2,1)S(1)} %collective-permute-done.5.q_ref, bf16[1040,256]{1,0:T(8,128)(2,1)S(1)} %get-tuple-element.37.own_ref, ...), custom_call_target="tpu_custom_call" | custom-call | flops 1500000000 | tf_op jit(solution)/shard_map/cache_part/pallas_call | solution.py:545
  24.5 2.4 %collective-permute-start.12 = (bf16[272,256]{1,0:T(8,128)(2,1)S(1)}, bf16[272,256]{1,0:T(8,128)(2,1)S(1)}, u32[]{:S(2)}, u32[]{:S(2)}) collective-permute-start(bf16[272,256]{1,0:T(8,128)(2,1)S(1)} %cache_part.6.refs_0_), channel_id=1, source_target_pairs={{0,4},{1,5},{2,6},{3,7},{4,0},{5,1},{6,2},{7,3},{8,12},{9,13},{10,... | collective-permute-start | bytes 417800 | tf_op jit(solution)/shard_map/ppermute | solution.py:430
  26.8 0.0 collective-permute-done.4.q_ref
  26.8 1.5 %cache_part.7.refs_0_ = bf16[272,256]{1,0:T(8,128)(2,1)S(1)} custom-call(s32[8,128]{1,0:T(8,128)S(1)} %get-tuple-element.36.usable_ref, f32[2,4]{1,0:T(2,128)S(1)} %copy-done.7, bf16[272,256]{1,0:T(8,128)(2,1)S(1)} %collective-permute-done.4.q_ref, bf16[1040,256]{1,0:T(8,128)(2,1)S(1)} %get-tuple-element.37.own_ref, ...), custom_call_target="tpu_custom_call" | custom-call | flops 1500000000 | tf_op jit(solution)/shard_map/cache_part/pallas_call | solution.py:545
  28.3 0.3 collective-permute-start.11
  28.6 0.0 collective-permute-done.6.refs_1_.refs_10_
  28.6 0.0 collective-permute-done.7.refs_2_.refs_11_
  28.6 0.1 merge.2.refs_0_.refs_1_
  28.8 0.1 last_merge.2
  28.9 1.5 %collective-permute-start.10 = (bf16[128,256]{1,0:T(8,128)(2,1)S(1)}, bf16[128,256]{1,0:T(8,128)(2,1)S(1)}, u32[]{:S(2)}, u32[]{:S(2)}) collective-permute-start(bf16[128,256]{1,0:T(8,128)(2,1)S(1)} %get-tuple-element.42), channel_id=1, source_target_pairs={{0,24},{8,16},{16,8},{24,0},{1,25},{9,17},{17,9},{25,1},{2,26},{10... | collective-permute-start | bytes 196616 | tf_op jit(solution)/shard_map/ppermute | solution.py:430
  30.5 1.5 %collective-permute-start.8 = (bf16[128,256]{1,0:T(8,128)(2,1)S(1)}, bf16[128,256]{1,0:T(8,128)(2,1)S(1)}, u32[]{:S(2)}, u32[]{:S(2)}) collective-permute-start(bf16[128,256]{1,0:T(8,128)(2,1)S(1)} %get-tuple-element.40), channel_id=1, source_target_pairs={{0,8},{1,17},{2,10},{3,19},{4,12},{5,21},{6,14},{7,23},{8,0},{9,25... | collective-permute-start | bytes 196616 | tf_op jit(solution)/shard_map/ppermute | solution.py:439
  32.0 0.5 collective-permute-start.9
  32.5 4.5 %collective-permute-done.12.got_ref = bf16[272,256]{1,0:T(8,128)(2,1)S(1)} collective-permute-done((bf16[272,256]{1,0:T(8,128)(2,1)S(1)}, bf16[272,256]{1,0:T(8,128)(2,1)S(1)}, u32[]{:S(2)}, u32[]{:S(2)}) %collective-permute-start.12) | collective-permute-done | bytes 139296 | tf_op jit(solution)/shard_map/ppermute | solution.py:430
  37.0 0.1 merge.3.refs_0_.refs_1_
  37.2 0.0 copy-start.3
  37.2 0.0 copy-start.5
  37.2 0.0 copy-start.6
  37.2 0.0 collective-permute-done.10.refs_4_.refs_3_
  37.2 0.0 collective-permute-done.8.refs_2_.refs_1_
  37.2 0.1 last_merge.3
  37.4 1.0 %collective-permute-start.13 = (bf16[128,256]{1,0:T(8,128)(2,1)S(1)}, bf16[128,256]{1,0:T(8,128)(2,1)S(1)}, u32[]{:S(2)}, u32[]{:S(2)}) collective-permute-start(bf16[128,256]{1,0:T(8,128)(2,1)S(1)} %get-tuple-element.44), channel_id=1, source_target_pairs={{0,8},{1,17},{2,10},{3,19},{4,12},{5,21},{6,14},{7,23},{8,0},{9,25... | collective-permute-start | bytes 196616 | tf_op jit(solution)/shard_map/ppermute | solution.py:439
  38.4 1.8 %collective-permute-start.14 = (bf16[128,256]{1,0:T(8,128)(2,1)S(1)}, bf16[128,256]{1,0:T(8,128)(2,1)S(1)}, u32[]{:S(2)}, u32[]{:S(2)}) collective-permute-start(bf16[128,256]{1,0:T(8,128)(2,1)S(1)} %get-tuple-element.45), channel_id=1, source_target_pairs={{0,16},{1,9},{2,18},{3,11},{4,20},{5,13},{6,22},{7,15},{8,24},{9,1... | collective-permute-start | bytes 196616 | tf_op jit(solution)/shard_map/ppermute | solution.py:439
  40.2 0.7 %collective-permute-start.15 = (bf16[128,256]{1,0:T(8,128)(2,1)S(1)}, bf16[128,256]{1,0:T(8,128)(2,1)S(1)}, u32[]{:S(2)}, u32[]{:S(2)}) collective-permute-start(bf16[128,256]{1,0:T(8,128)(2,1)S(1)} %get-tuple-element.46), channel_id=1, source_target_pairs={{0,24},{8,16},{16,8},{24,0},{1,25},{9,17},{17,9},{25,1},{2,26},{10... | collective-permute-start | bytes 196616 | tf_op jit(solution)/shard_map/ppermute | solution.py:430
  41.0 0.8 %collective-permute-done.13.refs_5_ = bf16[128,256]{1,0:T(8,128)(2,1)S(1)} collective-permute-done((bf16[128,256]{1,0:T(8,128)(2,1)S(1)}, bf16[128,256]{1,0:T(8,128)(2,1)S(1)}, u32[]{:S(2)}, u32[]{:S(2)}) %collective-permute-start.13) | collective-permute-done | bytes 65568 | tf_op jit(solution)/shard_map/ppermute | solution.py:439
  41.7 1.0 %collective-permute-done.14.refs_6_ = bf16[128,256]{1,0:T(8,128)(2,1)S(1)} collective-permute-done((bf16[128,256]{1,0:T(8,128)(2,1)S(1)}, bf16[128,256]{1,0:T(8,128)(2,1)S(1)}, u32[]{:S(2)}, u32[]{:S(2)}) %collective-permute-start.14) | collective-permute-done | bytes 65568 | tf_op jit(solution)/shard_map/ppermute | solution.py:439
  42.7 2.8 %collective-permute-done.15.refs_7_ = bf16[128,256]{1,0:T(8,128)(2,1)S(1)} collective-permute-done((bf16[128,256]{1,0:T(8,128)(2,1)S(1)}, bf16[128,256]{1,0:T(8,128)(2,1)S(1)}, u32[]{:S(2)}, u32[]{:S(2)}) %collective-permute-start.15) | collective-permute-done | bytes 65568 | tf_op jit(solution)/shard_map/ppermute | solution.py:430
  45.5 1.0 %output.1 = (f32[256,256]{1,0:T(8,128)S(1)}, f32[8,128]{1,0:T(8,128)S(1)}, bf16[272,256]{1,0:T(8,128)(2,1)S(1)}, bf16[272,256]{1,0:T(8,128)(2,1)S(1)}, bf16[272,256]{1,0:T(8,128)(2,1)S(1)}) custom-call(bf16[128,256]{1,0:T(8,128)(2,1)S(1)} %get-tuple-element.39.refs_0_, bf16[128,256]{1,0:T(8,128)(2,1)S(1)} %collective-permute-done.8.refs_2_.refs_1_, ...), custom_call_target="tpu_custom_call" | custom-call | flops 2000000000 | tf_op jit(solution)/shard_map/output/pallas_call | solution.py:603
  46.6 1.2 %collective-permute-start.16 = (bf16[272,256]{1,0:T(8,128)(2,1)S(1)}, bf16[272,256]{1,0:T(8,128)(2,1)S(1)}, u32[]{:S(2)}, u32[]{:S(2)}) collective-permute-start(bf16[272,256]{1,0:T(8,128)(2,1)S(1)} %get-tuple-element.50), channel_id=1, source_target_pairs={{0,8},{1,17},{2,10},{3,19},{4,12},{5,21},{6,14},{7,23},{8,0},{9,25... | collective-permute-start | bytes 417800 | tf_op jit(solution)/shard_map/ppermute | solution.py:439
  47.8 0.1 collective-permute-start.17
  47.9 2.2 %collective-permute-start.18 = (bf16[272,256]{1,0:T(8,128)(2,1)S(1)}, bf16[272,256]{1,0:T(8,128)(2,1)S(1)}, u32[]{:S(2)}, u32[]{:S(2)}) collective-permute-start(bf16[272,256]{1,0:T(8,128)(2,1)S(1)} %get-tuple-element.52), channel_id=1, source_target_pairs={{0,24},{8,16},{16,8},{24,0},{1,25},{9,17},{17,9},{25,1},{2,26},{10... | collective-permute-start | bytes 417800 | tf_op jit(solution)/shard_map/ppermute | solution.py:430
  50.1 1.6 %collective-permute-done.16.refs_0_ = bf16[272,256]{1,0:T(8,128)(2,1)S(1)} collective-permute-done((bf16[272,256]{1,0:T(8,128)(2,1)S(1)}, bf16[272,256]{1,0:T(8,128)(2,1)S(1)}, u32[]{:S(2)}, u32[]{:S(2)}) %collective-permute-start.16) | collective-permute-done | bytes 139296 | tf_op jit(solution)/shard_map/ppermute | solution.py:439
  51.7 2.6 %collective-permute-done.17.refs_1_ = bf16[272,256]{1,0:T(8,128)(2,1)S(1)} collective-permute-done((bf16[272,256]{1,0:T(8,128)(2,1)S(1)}, bf16[272,256]{1,0:T(8,128)(2,1)S(1)}, u32[]{:S(2)}, u32[]{:S(2)}) %collective-permute-start.17) | collective-permute-done | bytes 139296 | tf_op jit(solution)/shard_map/ppermute | solution.py:439
  54.3 0.0 collective-permute-done.18.refs_2_
  54.3 2.1 %place.1 = (f32[1024,256]{1,0:T(8,128)}, f32[1,16]{1,0:T(1,128)}) custom-call(s32[8]{0:T(128)S(1)} %get-tuple-element.29.home_any, f32[256,256]{1,0:T(8,128)S(1)} %get-tuple-element.49.mine_ref, bf16[272,256]{1,0:T(8,128)(2,1)S(1)} %collective-permute-done.16.refs_0_, bf16[272,256]{1,0:T(8,128)(2,1)S(1)} %collective-permute-done.17.refs_1_, ...), custom_call_target="tpu_custom_call" | custom-call | flops 1500000000 | tf_op jit(solution)/shard_map/place/pallas_call | solution.py:615
  (20 shorter events, 0.0 us)
Async XLA Ops:
  0.6 11.7 %collective-permute-start = (bf16[256,1024]{1,0:T(8,128)(2,1)}, bf16[256,1024]{1,0:T(8,128)(2,1)S(1)}, u32[]{:S(2)}, u32[]{:S(2)}) collective-permute-start(bf16[256,1024]{1,0:T(8,128)(2,1)} %refs_8_.3), channel_id=1, source_target_pairs={{0,8},{1,17},{2,10},{3,19},{4,12},{5,21},{6,14},{7,23},{8,0},{9,25... | collective-permute-start | bytes 1572872 | tf_op jit(solution)/shard_map/ppermute | solution.py:439
  3.6 8.7 %copy-start = (bf16[1024,1024]{1,0:T(8,128)(2,1)S(1)}, bf16[1024,1024]{1,0:T(8,128)(2,1)}, u32[]{:S(2)}) copy-start(bf16[1024,1024]{1,0:T(8,128)(2,1)} %x_ref.1) | copy-start | bytes 6291460
  3.6 8.7 %copy-start.1 = (bf16[1024,256]{1,0:T(8,128)(2,1)S(1)}, bf16[1024,256]{1,0:T(8,128)(2,1)}, u32[]{:S(2)}) copy-start(bf16[1024,256]{1,0:T(8,128)(2,1)} %wk_ref.1) | copy-start | bytes 1572868
  3.6 8.7 %copy-start.2 = (bf16[1024,256]{1,0:T(8,128)(2,1)S(1)}, bf16[1024,256]{1,0:T(8,128)(2,1)}, u32[]{:S(2)}) copy-start(bf16[1024,256]{1,0:T(8,128)(2,1)} %wv_ref.1) | copy-start | bytes 1572868
  3.6 8.7 %copy-start.4 = (s32[1024]{0:T(1024)S(1)}, s32[1024]{0:T(1024)}, u32[]{:S(2)}) copy-start(s32[1024]{0:T(1024)} %param.20) | copy-start | bytes 12292
  3.6 8.7 %copy-start.7 = (f32[2,4]{1,0:T(2,128)S(1)}, f32[2,4]{1,0:T(2,128)}, u32[]{:S(2)}) copy-start(f32[2,4]{1,0:T(2,128)} %bias_ref.9) | copy-start | bytes 100
  3.7 8.7 %copy-start.8 = (f32[264,128]{1,0:T(8,128)S(1)}, f32[264,128]{1,0:T(8,128)}, u32[]{:S(2)}) copy-start(f32[264,128]{1,0:T(8,128)} %constant.2.clone.refs_5_.table_ref) | copy-start | bytes 405508
  7.8 8.6 %collective-permute-start.2 = (bf16[1040,256]{1,0:T(8,128)(2,1)S(1)}, bf16[1040,256]{1,0:T(8,128)(2,1)S(1)}, u32[]{:S(2)}, u32[]{:S(2)}) collective-permute-start(bf16[1040,256]{1,0:T(8,128)(2,1)S(1)} %get-tuple-element.37.own_ref), channel_id=1, source_target_pairs={{0,1},{1,0},{2,3},{3,2},{4,5},{5,4},{6,7},{7,6},{8,9},{9,8},{10,11... | collective-permute-start | bytes 1597448 | tf_op jit(solution)/shard_map/ppermute | solution.py:430
  7.9 11.6 %collective-permute-start.1 = (bf16[272,256]{1,0:T(8,128)(2,1)S(1)}, bf16[272,256]{1,0:T(8,128)(2,1)S(1)}, u32[]{:S(2)}, u32[]{:S(2)}) collective-permute-start(bf16[272,256]{1,0:T(8,128)(2,1)S(1)} %get-tuple-element.32.refs_1_), channel_id=1, source_target_pairs={{0,2},{1,3},{2,0},{3,1},{4,6},{5,7},{6,4},{7,5},{8,10},{9,11},{10,... | collective-permute-start | bytes 417800 | tf_op jit(solution)/shard_map/ppermute | solution.py:430
  9.5 13.4 %collective-permute-start.5 = (bf16[272,256]{1,0:T(8,128)(2,1)S(1)}, bf16[272,256]{1,0:T(8,128)(2,1)S(1)}, u32[]{:S(2)}, u32[]{:S(2)}) collective-permute-start(bf16[272,256]{1,0:T(8,128)(2,1)S(1)} %get-tuple-element.33.refs_2_), channel_id=1, source_target_pairs={{0,4},{1,5},{2,6},{3,7},{4,0},{5,1},{6,2},{7,3},{8,12},{9,13},{10,... | collective-permute-start | bytes 417800 | tf_op jit(solution)/shard_map/ppermute | solution.py:430
  12.1 14.7 %collective-permute-start.4 = (bf16[272,256]{1,0:T(8,128)(2,1)S(1)}, bf16[272,256]{1,0:T(8,128)(2,1)S(1)}, u32[]{:S(2)}, u32[]{:S(2)}) collective-permute-start(bf16[272,256]{1,0:T(8,128)(2,1)S(1)} %get-tuple-element.34.refs_3_), channel_id=1, source_target_pairs={{0,6},{1,7},{2,4},{3,5},{4,2},{5,3},{6,0},{7,1},{8,14},{9,15},{10,... | collective-permute-start | bytes 417800 | tf_op jit(solution)/shard_map/ppermute | solution.py:430
  16.3 12.3 %collective-permute-start.6 = (bf16[256,1024]{1,0:T(8,128)(2,1)S(1)}, bf16[256,1024]{1,0:T(8,128)(2,1)S(1)}, u32[]{:S(2)}, u32[]{:S(2)}) collective-permute-start(bf16[256,1024]{1,0:T(8,128)(2,1)S(1)} %get-tuple-element.38), channel_id=1, source_target_pairs={{0,1},{1,0},{2,3},{3,2},{4,5},{5,4},{6,7},{7,6},{8,9},{9,8},{10,11... | collective-permute-start | bytes 1572872 | tf_op jit(solution)/shard_map/ppermute | solution.py:430
  16.4 12.2 %collective-permute-start.7 = (bf16[256,1024]{1,0:T(8,128)(2,1)S(1)}, bf16[256,1024]{1,0:T(8,128)(2,1)S(1)}, u32[]{:S(2)}, u32[]{:S(2)}) collective-permute-start(bf16[256,1024]{1,0:T(8,128)(2,1)S(1)} %get-tuple-element.38), channel_id=1, source_target_pairs={{0,16},{1,9},{2,18},{3,11},{4,20},{5,13},{6,22},{7,15},{8,24},{9,1... | collective-permute-start | bytes 1572872 | tf_op jit(solution)/shard_map/ppermute | solution.py:439
  21.0 7.8 %collective-permute-start.3 = (bf16[272,256]{1,0:T(8,128)(2,1)S(1)}, bf16[272,256]{1,0:T(8,128)(2,1)S(1)}, u32[]{:S(2)}, u32[]{:S(2)}) collective-permute-start(bf16[272,256]{1,0:T(8,128)(2,1)S(1)} %cache_part.5.refs_0_), channel_id=1, source_target_pairs={{0,2},{1,3},{2,0},{3,1},{4,6},{5,7},{6,4},{7,5},{8,10},{9,11},{10,... | collective-permute-start | bytes 417800 | tf_op jit(solution)/shard_map/ppermute | solution.py:430
  24.5 12.6 %collective-permute-start.12 = (bf16[272,256]{1,0:T(8,128)(2,1)S(1)}, bf16[272,256]{1,0:T(8,128)(2,1)S(1)}, u32[]{:S(2)}, u32[]{:S(2)}) collective-permute-start(bf16[272,256]{1,0:T(8,128)(2,1)S(1)} %cache_part.6.refs_0_), channel_id=1, source_target_pairs={{0,4},{1,5},{2,6},{3,7},{4,0},{5,1},{6,2},{7,3},{8,12},{9,13},{10,... | collective-permute-start | bytes 417800 | tf_op jit(solution)/shard_map/ppermute | solution.py:430
  28.3 8.9 %collective-permute-start.11 = (bf16[272,256]{1,0:T(8,128)(2,1)S(1)}, bf16[272,256]{1,0:T(8,128)(2,1)S(1)}, u32[]{:S(2)}, u32[]{:S(2)}) collective-permute-start(bf16[272,256]{1,0:T(8,128)(2,1)S(1)} %cache_part.7.refs_0_), channel_id=1, source_target_pairs={{0,6},{1,7},{2,4},{3,5},{4,2},{5,3},{6,0},{7,1},{8,14},{9,15},{10,... | collective-permute-start | bytes 417800 | tf_op jit(solution)/shard_map/ppermute | solution.py:430
  28.9 8.3 %collective-permute-start.10 = (bf16[128,256]{1,0:T(8,128)(2,1)S(1)}, bf16[128,256]{1,0:T(8,128)(2,1)S(1)}, u32[]{:S(2)}, u32[]{:S(2)}) collective-permute-start(bf16[128,256]{1,0:T(8,128)(2,1)S(1)} %get-tuple-element.42), channel_id=1, source_target_pairs={{0,24},{8,16},{16,8},{24,0},{1,25},{9,17},{17,9},{25,1},{2,26},{10... | collective-permute-start | bytes 196616 | tf_op jit(solution)/shard_map/ppermute | solution.py:430
  30.5 6.8 %collective-permute-start.8 = (bf16[128,256]{1,0:T(8,128)(2,1)S(1)}, bf16[128,256]{1,0:T(8,128)(2,1)S(1)}, u32[]{:S(2)}, u32[]{:S(2)}) collective-permute-start(bf16[128,256]{1,0:T(8,128)(2,1)S(1)} %get-tuple-element.40), channel_id=1, source_target_pairs={{0,8},{1,17},{2,10},{3,19},{4,12},{5,21},{6,14},{7,23},{8,0},{9,25... | collective-permute-start | bytes 196616 | tf_op jit(solution)/shard_map/ppermute | solution.py:439
  32.0 5.3 %collective-permute-start.9 = (bf16[128,256]{1,0:T(8,128)(2,1)S(1)}, bf16[128,256]{1,0:T(8,128)(2,1)S(1)}, u32[]{:S(2)}, u32[]{:S(2)}) collective-permute-start(bf16[128,256]{1,0:T(8,128)(2,1)S(1)} %get-tuple-element.41), channel_id=1, source_target_pairs={{0,16},{1,9},{2,18},{3,11},{4,20},{5,13},{6,22},{7,15},{8,24},{9,1... | collective-permute-start | bytes 196616 | tf_op jit(solution)/shard_map/ppermute | solution.py:439
  37.2 8.3 %copy-start.3 = (bf16[256,1024]{1,0:T(8,128)(2,1)S(1)}, bf16[256,1024]{1,0:T(8,128)(2,1)}, u32[]{:S(2)}) copy-start(bf16[256,1024]{1,0:T(8,128)(2,1)} %refs_8_.3) | copy-start | bytes 1572868
  37.2 8.3 %copy-start.5 = (f32[1024]{0:T(1024)S(1)}, f32[1024]{0:T(1024)}, u32[]{:S(2)}) copy-start(f32[1024]{0:T(1024)} %param.31) | copy-start | bytes 12292
  37.2 8.3 %copy-start.6 = (f32[1024]{0:T(1024)S(1)}, f32[1024]{0:T(1024)}, u32[]{:S(2)}) copy-start(f32[1024]{0:T(1024)} %param.32) | copy-start | bytes 12292
  37.4 4.3 %collective-permute-start.13 = (bf16[128,256]{1,0:T(8,128)(2,1)S(1)}, bf16[128,256]{1,0:T(8,128)(2,1)S(1)}, u32[]{:S(2)}, u32[]{:S(2)}) collective-permute-start(bf16[128,256]{1,0:T(8,128)(2,1)S(1)} %get-tuple-element.44), channel_id=1, source_target_pairs={{0,8},{1,17},{2,10},{3,19},{4,12},{5,21},{6,14},{7,23},{8,0},{9,25... | collective-permute-start | bytes 196616 | tf_op jit(solution)/shard_map/ppermute | solution.py:439
  38.4 4.3 %collective-permute-start.14 = (bf16[128,256]{1,0:T(8,128)(2,1)S(1)}, bf16[128,256]{1,0:T(8,128)(2,1)S(1)}, u32[]{:S(2)}, u32[]{:S(2)}) collective-permute-start(bf16[128,256]{1,0:T(8,128)(2,1)S(1)} %get-tuple-element.45), channel_id=1, source_target_pairs={{0,16},{1,9},{2,18},{3,11},{4,20},{5,13},{6,22},{7,15},{8,24},{9,1... | collective-permute-start | bytes 196616 | tf_op jit(solution)/shard_map/ppermute | solution.py:439
  40.2 5.3 %collective-permute-start.15 = (bf16[128,256]{1,0:T(8,128)(2,1)S(1)}, bf16[128,256]{1,0:T(8,128)(2,1)S(1)}, u32[]{:S(2)}, u32[]{:S(2)}) collective-permute-start(bf16[128,256]{1,0:T(8,128)(2,1)S(1)} %get-tuple-element.46), channel_id=1, source_target_pairs={{0,24},{8,16},{16,8},{24,0},{1,25},{9,17},{17,9},{25,1},{2,26},{10... | collective-permute-start | bytes 196616 | tf_op jit(solution)/shard_map/ppermute | solution.py:430
  46.6 5.1 %collective-permute-start.16 = (bf16[272,256]{1,0:T(8,128)(2,1)S(1)}, bf16[272,256]{1,0:T(8,128)(2,1)S(1)}, u32[]{:S(2)}, u32[]{:S(2)}) collective-permute-start(bf16[272,256]{1,0:T(8,128)(2,1)S(1)} %get-tuple-element.50), channel_id=1, source_target_pairs={{0,8},{1,17},{2,10},{3,19},{4,12},{5,21},{6,14},{7,23},{8,0},{9,25... | collective-permute-start | bytes 417800 | tf_op jit(solution)/shard_map/ppermute | solution.py:439
  47.8 6.5 %collective-permute-start.17 = (bf16[272,256]{1,0:T(8,128)(2,1)S(1)}, bf16[272,256]{1,0:T(8,128)(2,1)S(1)}, u32[]{:S(2)}, u32[]{:S(2)}) collective-permute-start(bf16[272,256]{1,0:T(8,128)(2,1)S(1)} %get-tuple-element.51), channel_id=1, source_target_pairs={{0,16},{1,9},{2,18},{3,11},{4,20},{5,13},{6,22},{7,15},{8,24},{9,1... | collective-permute-start | bytes 417800 | tf_op jit(solution)/shard_map/ppermute | solution.py:439
  47.9 6.4 %collective-permute-start.18 = (bf16[272,256]{1,0:T(8,128)(2,1)S(1)}, bf16[272,256]{1,0:T(8,128)(2,1)S(1)}, u32[]{:S(2)}, u32[]{:S(2)}) collective-permute-start(bf16[272,256]{1,0:T(8,128)(2,1)S(1)} %get-tuple-element.52), channel_id=1, source_target_pairs={{0,24},{8,16},{16,8},{24,0},{1,25},{9,17},{17,9},{25,1},{2,26},{10... | collective-permute-start | bytes 417800 | tf_op jit(solution)/shard_map/ppermute | solution.py:430

commit v6 on v5

--- a/solution.py
+++ b/solution.py
@@ -111,18 +111,17 @@
 def query_kernel(bpq, order, *refs):
     chunks = len(order)
     sources, refs = refs[:11], refs[11:]
-    pick_ref, base_ref, usable_ref, packed_ref = refs[:4]
-    q_refs, refs = refs[4 : 4 + chunks], refs[4 + chunks :]
+    pick_ref, base_ref, usable_ref, packed_ref, cos_ref, sin_ref = refs[:6]
+    q_refs, refs = refs[6 : 6 + chunks], refs[6 + chunks :]
     targets, (y_ref, sems) = list(refs[:10]), refs[10:]
-    rows, cols = sources[10].shape
-    moves = copies(sources, targets + [packed_ref.at[0:rows]], sems)
-    doc_query, query_len, block_perm, seg_ref, var_ref, table_ref, key_var_ref = targets[:7]
-    x_ref, w_ref, v_ref = targets[7:]
+    rows, cols = sources[8].shape
+    moves = copies(sources, targets[:8] + [packed_ref.at[0:rows]] + targets[8:], sems)
+    doc_query, query_len, block_perm, seg_ref, var_ref, table_ref, key_var_ref, v_ref = targets[:8]
+    w_ref, x_ref = targets[8:]
     slots, width = seg_ref.shape
-    cos_ref, sin_ref = table_ref.at[0:width], table_ref.at[width : 2 * width]
-    rows_ref = table_ref.at[2 * width :]
     for move in moves[:7]:
         move.wait()
+    rows_ref = table_ref.at[2 * width :]
     start_tables(doc_query, query_len, seg_ref, rows_ref, base_ref)
     row = lax.broadcasted_iota(jnp.int32, usable_ref.shape, 0)
     usable = jnp.zeros(usable_ref.shape, jnp.int32)
@@ -131,30 +130,40 @@
         here = query_len[block // bpq] - block % bpq * rows
         usable = jnp.where(row == j, here, usable)
     usable_ref[...] = usable
+    for slot in range(slots):
+        cos, sin = slot_tables(
+            slot, base_ref, table_ref.at[0:width], table_ref.at[width : 2 * width], rows_ref
+        )
+        cos_ref[slot * width : (slot + 1) * width, :] = cos
+        sin_ref[slot * width : (slot + 1) * width, :] = sin
+    found = [
+        slot_of(2 * order[k] + j, doc_query, block_perm, slots, bpq)
+        for k in range(chunks)
+        for j in range(2)
+    ]
+    for p, slot in enumerate(found):
+        pick_ref[p] = slot
+        q_ref, j = q_refs[p // 2], p % 2
+        var = var_ref[pl.ds(slot, 1), :].astype(F32)
+        q_ref[2 * width :, j * width : (j + 1) * width] = jnp.broadcast_to(
+            var, (EXTRA, width)
+        ).astype(BF)
     parts = rows // LANES
     key_var = key_var_ref[...].astype(F32)
     key_var = jnp.concatenate([key_var, jnp.zeros((EXTRA - parts, LANES), F32)], axis=0)
     packed_ref[2 * rows :, :] = jnp.concatenate([key_var, key_var], axis=1).astype(BF)
-    for move in moves[7:9]:
-        move.wait()
-    y_ref[...] = dot(x_ref[...], w_ref[...])
-    moves[9].wait()
+    moves[7].wait()
     for i in range(rows // cols):
         block = v_ref[i * cols : (i + 1) * cols, :].astype(F32)
         packed_ref[rows + i * cols : rows + (i + 1) * cols, :] = block.T.astype(BF)
-    for k, q_ref in enumerate(q_refs):
-        for j in range(2):
-            slot = slot_of(2 * order[k] + j, doc_query, block_perm, slots, bpq)
-            pick_ref[2 * k + j] = slot
-            cos, sin = slot_tables(slot, base_ref, cos_ref, sin_ref, rows_ref)
-            at = pl.ds(pl.multiple_of(slot * width, width), width)
-            turned = turn(y_ref[at, :], cos, sin)
-            q_ref[j * width : (j + 1) * width, :] = (turned * 0.125).astype(BF)
-            var = var_ref[pl.ds(slot, 1), :].astype(F32)
-            q_ref[2 * width :, j * width : (j + 1) * width] = jnp.broadcast_to(
-                var, (EXTRA, width)
-            ).astype(BF)
-    moves[10].wait()
+    for move in moves[8:]:
+        move.wait()
+    y_ref[...] = dot(x_ref[...], w_ref[...])
+    for p, slot in enumerate(found):
+        q_ref, j = q_refs[p // 2], p % 2
+        at = pl.ds(pl.multiple_of(slot * width, width), width)
+        turned = turn(y_ref[at, :], cos_ref[at, :], sin_ref[at, :])
+        q_ref[j * width : (j + 1) * width, :] = (turned * 0.125).astype(BF)
 
 
 def by_head(query):
@@ -224,7 +233,7 @@
 
 
 def own_kernel(
-    home_any, bias_ref, x_ref, wk_ref, wv_ref, var_ref, table_ref, base_ref,
+    home_any, bias_ref, x_ref, wk_ref, wv_ref, var_ref, cos_ref, sin_ref, base_ref,
     *refs
 ):
     w_ref, out_ref, x_part_ref, count_ref, w_copy_ref, k_ref, v_ref, home_ref, sem = refs[-9:]
@@ -236,15 +245,13 @@
     cols = wk_ref.shape[1]
     home_move = pltpu.make_async_copy(home_any, home_ref, sem)
     home_move.start()
-    cos_ref, sin_ref = table_ref.at[0:width], table_ref.at[width : 2 * width]
-    rows_ref = table_ref.at[2 * width :]
     k_ref[...] = dot(x_ref[...], wk_ref[...])
     v_ref[...] = dot(x_ref[...], wv_ref[...])
     home_move.wait()
     for n in range(slots):
         slot = home_ref[n]
-        cos, sin = slot_tables(slot, base_ref, cos_ref, sin_ref, rows_ref)
         at = pl.ds(pl.multiple_of(slot * width, width), width)
+        cos, sin = cos_ref[at, :], sin_ref[at, :]
         part_at = pl.ds(pl.multiple_of(slot * width + part_start, part), part)
         x_part_ref[n * part : (n + 1) * part, :] = x_ref[part_at, :]
         key = turn(k_ref[at, :], cos, sin).astype(BF)
@@ -484,26 +491,27 @@
 
     w_first = hop(w_out, 1, 2)
 
-    pick, base, usable, packed, *queries = call(
+    pick, base, usable, packed, cos, sin, *queries = call(
         functools.partial(query_kernel, bpq, order),
         [
             sds((blocks,), i32), base_shape, sds((8, width), i32),
-            sds((2 * cache_rows + EXTRA, cols), BF),
+            sds((2 * cache_rows + EXTRA, cols), BF), sds((rows, LANES), F32),
+            sds((rows, LANES), F32),
         ]
         + [chunk_shape] * chunks,
         [HBM] * 11,
         [pltpu.SMEM(ref.shape, i32) for ref in (doc_query, query_len, block_perm)]
         + [pltpu.VMEM(ref.shape, i32) for ref in (seg, var)]
         + [pltpu.VMEM(table.shape, F32), pltpu.VMEM(cache_var.shape, i32)]
-        + [pltpu.VMEM(ref.shape, BF) for ref in (doc_x, w_query, cache_v)]
+        + [pltpu.VMEM(ref.shape, BF) for ref in (cache_v, w_query, doc_x)]
         + [pltpu.VMEM((rows, cols), F32), DMA((11,))],
-        out_specs=[SMEM] + [VMEM] * (chunks + 3),
+        out_specs=[SMEM] + [VMEM] * (chunks + 5),
         work=3.5,
         name="query",
     )(
         *in_hbm(
-            doc_query, query_len, block_perm, seg, var, table, cache_var, doc_x, w_query,
-            cache_v, cache_k,
+            doc_query, query_len, block_perm, seg, var, table, cache_var, cache_v, cache_k,
+            w_query, doc_x,
         )
     )
 
@@ -527,7 +535,7 @@
             sds((slots, cols + 8, width), F32), sds((rows // heads, depth), BF),
             sds((slots, width), F32), sds(w_out.shape, BF),
         ],
-        [ANY] + [VMEM] * (8 + len(home_queries)),
+        [ANY] + [VMEM] * (9 + len(home_queries)),
         [
             pltpu.VMEM((rows, cols), F32), pltpu.VMEM((rows, cols), F32),
             pltpu.SMEM(home.shape, i32), DMA,
@@ -535,7 +543,7 @@
         out_specs=[VMEM] * 4,
         work=4.0,
         name="own_documents",
-    )(home, var_bias, doc_x, w_key, w_value, var, table, base, *home_queries, w_first)
+    )(home, var_bias, doc_x, w_key, w_value, var, cos, sin, base, *home_queries, w_first)
 
     w_second = partner(w_copy, "blk", 1)
     w_third = hop(w_copy, 2, 1)

time: 56.6 us -> 56.6 us (level)
  transfers between devices with their start and end apart: 19 -> 19, of which waited for: 7 -> 7; matrix products, arithmetic and copies ran while one was open for 0% -> 0% of each run, Pallas kernels for 26% -> 25%
where the time goes in v6:
time: 56.6 us; the launch traced here: 56.4 us
  starting transfers between devices  23.5 us (42%)
  Pallas kernels  17.6 us (31%)
  waiting for transfers between devices  14.5 us (26%)
  between operations  0.86 us (2%)
    ppermute x11, starting transfers between devices, partner(): return lax.ppermute(value, axis, [(i, i ^ k) for i in range(count)])  12.7 us
    ppermute x8, starting transfers between devices, hop(): return lax.ppermute(value, ('head', 'blk'), pairs)  10.8 us
    ppermute x11, waiting for transfers between devices, partner(): return lax.ppermute(value, axis, [(i, i ^ k) for i in range(count)])  8.36 us
    ppermute x8, waiting for transfers between devices, hop(): return lax.ppermute(value, ('head', 'blk'), pairs)  6.12 us
    pallas_call x4, Pallas kernels, body(): call(cache_kernel, chunk_shape, [VMEM] * 5 + [ANY] * len(after), out_spec...  6.04 us
    pallas_call x1, Pallas kernels, body(): call(functools.partial(query_kernel, bpq, order), [sds((blocks,), i32), b...  3.98 us
    pallas_call x1, Pallas kernels, body(): call(own_kernel, [sds((slots, cols + 8, width), F32), sds((rows // heads,...  3.88 us
    pallas_call x1, Pallas kernels, body(): call(place_kernel, [sds((rows, cols), F32), sds((1, 2 * slots), F32)], [A...  2.09 us
  transfers between devices with their start and end apart: 19, of which 7 were waited for; matrix products, arithmetic and copies ran while one was open for 0% of the time, Pallas kernels for 25%

profile of v6, /device:TPU:0, one launch (start us, length us, event | category | flops | bytes accessed | tf_op | source)
XLA Modules:
  0.0 56.4 jit_solution(879799610259033931)
XLA Ops:
  0.6 3.0 %collective-permute-start = (bf16[256,1024]{1,0:T(8,128)(2,1)}, bf16[256,1024]{1,0:T(8,128)(2,1)S(1)}, u32[]{:S(2)}, u32[]{:S(2)}) collective-permute-start(bf16[256,1024]{1,0:T(8,128)(2,1)} %refs_8_.3), channel_id=1, source_target_pairs={{0,8},{1,17},{2,10},{3,19},{4,12},{5,21},{6,14},{7,23},{8,0},{9,25... | collective-permute-start | bytes 1572872 | tf_op jit(solution)/shard_map/ppermute | solution.py:446
  3.7 4.0 %query.1 = (s32[8]{0:T(128)S(1)}, f32[5,8,128]{2,1,0:T(8,128)S(1)}, s32[8,128]{1,0:T(8,128)S(1)}, bf16[1040,256]{1,0:T(8,128)(2,1)S(1)}, f32[1024,128]{1,0:T(8,1...) custom-call(s32[128]{0:T(128)} %refs_0_.1, ...), custom_call_target="tpu_custom_call" | custom-call | flops 3500000000 | tf_op jit(solution)/shard_map/query/pallas_call | solution.py:494
  7.7 0.1 collective-permute-start.2
  7.7 1.6 %collective-permute-start.1 = (bf16[272,256]{1,0:T(8,128)(2,1)S(1)}, bf16[272,256]{1,0:T(8,128)(2,1)S(1)}, u32[]{:S(2)}, u32[]{:S(2)}) collective-permute-start(bf16[272,256]{1,0:T(8,128)(2,1)S(1)} %get-tuple-element.36.refs_1_), channel_id=1, source_target_pairs={{0,2},{1,3},{2,0},{3,1},{4,6},{5,7},{6,4},{7,5},{8,10},{9,11},{10,... | collective-permute-start | bytes 417800 | tf_op jit(solution)/shard_map/ppermute | solution.py:437
  9.4 2.6 %collective-permute-start.5 = (bf16[272,256]{1,0:T(8,128)(2,1)S(1)}, bf16[272,256]{1,0:T(8,128)(2,1)S(1)}, u32[]{:S(2)}, u32[]{:S(2)}) collective-permute-start(bf16[272,256]{1,0:T(8,128)(2,1)S(1)} %get-tuple-element.37.refs_2_), channel_id=1, source_target_pairs={{0,4},{1,5},{2,6},{3,7},{4,0},{5,1},{6,2},{7,3},{8,12},{9,13},{10,... | collective-permute-start | bytes 417800 | tf_op jit(solution)/shard_map/ppermute | solution.py:437
  12.0 0.2 collective-permute-start.4
  12.2 0.0 collective-permute-done.refs_4_.refs_9_
  12.2 3.9 %own_documents.1 = (f32[8,264,128]{2,1,0:T(8,128)S(1)}, bf16[256,1024]{1,0:T(8,128)(2,1)S(1)}, f32[8,128]{1,0:T(8,128)S(1)}, bf16[256,1024]{1,0:T(8,128)(2,1)S(1)}) custom-call(s32[8]{0:T(128)S(1)} %get-tuple-element.31.home_any, f32[2,4]{1,0:T(2,128)S(1)} %copy-done.7, bf16[1024,1024]{1,0:T(8,128)(2,1)S(1)} %copy-done, bf16[1024,256]{1,0:T(8,128)(2,1)S(1)} %copy-done.1, ...), custom_call_target="tpu_custom_call" | custom-call | flops 4000000000 | tf_op jit(solution)/shard_map/own_documents/pallas_call | solution.py:532
  16.1 0.1 collective-permute-start.6
  16.2 0.0 collective-permute-done.2.other_ref
  16.2 1.6 %collective-permute-start.7 = (bf16[256,1024]{1,0:T(8,128)(2,1)S(1)}, bf16[256,1024]{1,0:T(8,128)(2,1)S(1)}, u32[]{:S(2)}, u32[]{:S(2)}) collective-permute-start(bf16[256,1024]{1,0:T(8,128)(2,1)S(1)} %get-tuple-element.42), channel_id=1, source_target_pairs={{0,16},{1,9},{2,18},{3,11},{4,20},{5,13},{6,22},{7,15},{8,24},{9,1... | collective-permute-start | bytes 1572872 | tf_op jit(solution)/shard_map/ppermute | solution.py:446
  17.8 1.5 %cache_part.4.refs_0_.got_ref = bf16[272,256]{1,0:T(8,128)(2,1)S(1)} custom-call(s32[8,128]{1,0:T(8,128)S(1)} %get-tuple-element.40.usable_ref, f32[2,4]{1,0:T(2,128)S(1)} %copy-done.7, bf16[272,256]{1,0:T(8,128)(2,1)S(1)} %get-tuple-element.35.refs_0_.q_ref, bf16[1040,256]{1,0:T(8,128)(2,1)S(1)} %get-tuple-element.41.own_ref, ...), custom_call_target="tpu_custom_call" | custom-call | flops 1500000000 | tf_op jit(solution)/shard_map/cache_part/pallas_call | solution.py:553
  19.3 0.0 collective-permute-done.1.q_ref
  19.3 1.5 %cache_part.5.refs_0_ = bf16[272,256]{1,0:T(8,128)(2,1)S(1)} custom-call(s32[8,128]{1,0:T(8,128)S(1)} %get-tuple-element.40.usable_ref, f32[2,4]{1,0:T(2,128)S(1)} %copy-done.7, bf16[272,256]{1,0:T(8,128)(2,1)S(1)} %collective-permute-done.1.q_ref, bf16[1040,256]{1,0:T(8,128)(2,1)S(1)} %get-tuple-element.41.own_ref, ...), custom_call_target="tpu_custom_call" | custom-call | flops 1500000000 | tf_op jit(solution)/shard_map/cache_part/pallas_call | solution.py:553
  20.8 1.0 %collective-permute-start.3 = (bf16[272,256]{1,0:T(8,128)(2,1)S(1)}, bf16[272,256]{1,0:T(8,128)(2,1)S(1)}, u32[]{:S(2)}, u32[]{:S(2)}) collective-permute-start(bf16[272,256]{1,0:T(8,128)(2,1)S(1)} %cache_part.5.refs_0_), channel_id=1, source_target_pairs={{0,2},{1,3},{2,0},{3,1},{4,6},{5,7},{6,4},{7,5},{8,10},{9,11},{10,... | collective-permute-start | bytes 417800 | tf_op jit(solution)/shard_map/ppermute | solution.py:437
  21.8 1.0 %collective-permute-done.5.q_ref = bf16[272,256]{1,0:T(8,128)(2,1)S(1)} collective-permute-done((bf16[272,256]{1,0:T(8,128)(2,1)S(1)}, bf16[272,256]{1,0:T(8,128)(2,1)S(1)}, u32[]{:S(2)}, u32[]{:S(2)}) %collective-permute-start.5) | collective-permute-done | bytes 139296 | tf_op jit(solution)/shard_map/ppermute | solution.py:437
  22.8 1.5 %cache_part.6.refs_0_ = bf16[272,256]{1,0:T(8,128)(2,1)S(1)} custom-call(s32[8,128]{1,0:T(8,128)S(1)} %get-tuple-element.40.usable_ref, f32[2,4]{1,0:T(2,128)S(1)} %copy-done.7, bf16[272,256]{1,0:T(8,128)(2,1)S(1)} %collective-permute-done.5.q_ref, bf16[1040,256]{1,0:T(8,128)(2,1)S(1)} %get-tuple-element.41.own_ref, ...), custom_call_target="tpu_custom_call" | custom-call | flops 1500000000 | tf_op jit(solution)/shard_map/cache_part/pallas_call | solution.py:553
  24.3 2.3 %collective-permute-start.12 = (bf16[272,256]{1,0:T(8,128)(2,1)S(1)}, bf16[272,256]{1,0:T(8,128)(2,1)S(1)}, u32[]{:S(2)}, u32[]{:S(2)}) collective-permute-start(bf16[272,256]{1,0:T(8,128)(2,1)S(1)} %cache_part.6.refs_0_), channel_id=1, source_target_pairs={{0,4},{1,5},{2,6},{3,7},{4,0},{5,1},{6,2},{7,3},{8,12},{9,13},{10,... | collective-permute-start | bytes 417800 | tf_op jit(solution)/shard_map/ppermute | solution.py:437
  26.7 1.5 %cache_part.7.refs_0_ = bf16[272,256]{1,0:T(8,128)(2,1)S(1)} custom-call(s32[8,128]{1,0:T(8,128)S(1)} %get-tuple-element.40.usable_ref, f32[2,4]{1,0:T(2,128)S(1)} %copy-done.7, bf16[272,256]{1,0:T(8,128)(2,1)S(1)} %collective-permute-done.4.q_ref, bf16[1040,256]{1,0:T(8,128)(2,1)S(1)} %get-tuple-element.41.own_ref, ...), custom_call_target="tpu_custom_call" | custom-call | flops 1500000000 | tf_op jit(solution)/shard_map/cache_part/pallas_call | solution.py:553
  28.2 0.3 collective-permute-start.11
  28.5 0.0 collective-permute-done.7.refs_2_.refs_11_
  28.5 0.1 merge.2.refs_0_.refs_1_
  28.6 0.1 last_merge.2
  28.8 1.6 %collective-permute-start.10 = (bf16[128,256]{1,0:T(8,128)(2,1)S(1)}, bf16[128,256]{1,0:T(8,128)(2,1)S(1)}, u32[]{:S(2)}, u32[]{:S(2)}) collective-permute-start(bf16[128,256]{1,0:T(8,128)(2,1)S(1)} %get-tuple-element.46), channel_id=1, source_target_pairs={{0,24},{8,16},{16,8},{24,0},{1,25},{9,17},{17,9},{25,1},{2,26},{10... | collective-permute-start | bytes 196616 | tf_op jit(solution)/shard_map/ppermute | solution.py:437
  30.3 1.5 %collective-permute-start.8 = (bf16[128,256]{1,0:T(8,128)(2,1)S(1)}, bf16[128,256]{1,0:T(8,128)(2,1)S(1)}, u32[]{:S(2)}, u32[]{:S(2)}) collective-permute-start(bf16[128,256]{1,0:T(8,128)(2,1)S(1)} %get-tuple-element.44), channel_id=1, source_target_pairs={{0,8},{1,17},{2,10},{3,19},{4,12},{5,21},{6,14},{7,23},{8,0},{9,25... | collective-permute-start | bytes 196616 | tf_op jit(solution)/shard_map/ppermute | solution.py:446
  31.8 0.5 collective-permute-start.9
  32.3 4.6 %collective-permute-done.12.got_ref = bf16[272,256]{1,0:T(8,128)(2,1)S(1)} collective-permute-done((bf16[272,256]{1,0:T(8,128)(2,1)S(1)}, bf16[272,256]{1,0:T(8,128)(2,1)S(1)}, u32[]{:S(2)}, u32[]{:S(2)}) %collective-permute-start.12) | collective-permute-done | bytes 139296 | tf_op jit(solution)/shard_map/ppermute | solution.py:437
  36.9 0.1 merge.3.refs_0_.refs_1_
  37.0 0.0 copy-start.3
  37.0 0.0 copy-start.5
  37.0 0.0 copy-start.6
  37.1 0.0 collective-permute-done.10.refs_4_.refs_3_
  37.1 0.0 collective-permute-done.8.refs_2_.refs_1_
  37.1 0.1 last_merge.3
  37.2 1.0 %collective-permute-start.13 = (bf16[128,256]{1,0:T(8,128)(2,1)S(1)}, bf16[128,256]{1,0:T(8,128)(2,1)S(1)}, u32[]{:S(2)}, u32[]{:S(2)}) collective-permute-start(bf16[128,256]{1,0:T(8,128)(2,1)S(1)} %get-tuple-element.48), channel_id=1, source_target_pairs={{0,8},{1,17},{2,10},{3,19},{4,12},{5,21},{6,14},{7,23},{8,0},{9,25... | collective-permute-start | bytes 196616 | tf_op jit(solution)/shard_map/ppermute | solution.py:446
  38.3 1.8 %collective-permute-start.14 = (bf16[128,256]{1,0:T(8,128)(2,1)S(1)}, bf16[128,256]{1,0:T(8,128)(2,1)S(1)}, u32[]{:S(2)}, u32[]{:S(2)}) collective-permute-start(bf16[128,256]{1,0:T(8,128)(2,1)S(1)} %get-tuple-element.49), channel_id=1, source_target_pairs={{0,16},{1,9},{2,18},{3,11},{4,20},{5,13},{6,22},{7,15},{8,24},{9,1... | collective-permute-start | bytes 196616 | tf_op jit(solution)/shard_map/ppermute | solution.py:446
  40.0 0.8 %collective-permute-start.15 = (bf16[128,256]{1,0:T(8,128)(2,1)S(1)}, bf16[128,256]{1,0:T(8,128)(2,1)S(1)}, u32[]{:S(2)}, u32[]{:S(2)}) collective-permute-start(bf16[128,256]{1,0:T(8,128)(2,1)S(1)} %get-tuple-element.50), channel_id=1, source_target_pairs={{0,24},{8,16},{16,8},{24,0},{1,25},{9,17},{17,9},{25,1},{2,26},{10... | collective-permute-start | bytes 196616 | tf_op jit(solution)/shard_map/ppermute | solution.py:437
  40.8 0.8 %collective-permute-done.13.refs_5_ = bf16[128,256]{1,0:T(8,128)(2,1)S(1)} collective-permute-done((bf16[128,256]{1,0:T(8,128)(2,1)S(1)}, bf16[128,256]{1,0:T(8,128)(2,1)S(1)}, u32[]{:S(2)}, u32[]{:S(2)}) %collective-permute-start.13) | collective-permute-done | bytes 65568 | tf_op jit(solution)/shard_map/ppermute | solution.py:446
  41.6 1.0 %collective-permute-done.14.refs_6_ = bf16[128,256]{1,0:T(8,128)(2,1)S(1)} collective-permute-done((bf16[128,256]{1,0:T(8,128)(2,1)S(1)}, bf16[128,256]{1,0:T(8,128)(2,1)S(1)}, u32[]{:S(2)}, u32[]{:S(2)}) %collective-permute-start.14) | collective-permute-done | bytes 65568 | tf_op jit(solution)/shard_map/ppermute | solution.py:446
  42.5 2.8 %collective-permute-done.15.refs_7_ = bf16[128,256]{1,0:T(8,128)(2,1)S(1)} collective-permute-done((bf16[128,256]{1,0:T(8,128)(2,1)S(1)}, bf16[128,256]{1,0:T(8,128)(2,1)S(1)}, u32[]{:S(2)}, u32[]{:S(2)}) %collective-permute-start.15) | collective-permute-done | bytes 65568 | tf_op jit(solution)/shard_map/ppermute | solution.py:437
  45.4 1.0 %output.1 = (f32[256,256]{1,0:T(8,128)S(1)}, f32[8,128]{1,0:T(8,128)S(1)}, bf16[272,256]{1,0:T(8,128)(2,1)S(1)}, bf16[272,256]{1,0:T(8,128)(2,1)S(1)}, bf16[272,256]{1,0:T(8,128)(2,1)S(1)}) custom-call(bf16[128,256]{1,0:T(8,128)(2,1)S(1)} %get-tuple-element.43.refs_0_, bf16[128,256]{1,0:T(8,128)(2,1)S(1)} %collective-permute-done.8.refs_2_.refs_1_, ...), custom_call_target="tpu_custom_call" | custom-call | flops 2000000000 | tf_op jit(solution)/shard_map/output/pallas_call | solution.py:611
  46.4 1.4 %collective-permute-start.16 = (bf16[272,256]{1,0:T(8,128)(2,1)S(1)}, bf16[272,256]{1,0:T(8,128)(2,1)S(1)}, u32[]{:S(2)}, u32[]{:S(2)}) collective-permute-start(bf16[272,256]{1,0:T(8,128)(2,1)S(1)} %get-tuple-element.54), channel_id=1, source_target_pairs={{0,8},{1,17},{2,10},{3,19},{4,12},{5,21},{6,14},{7,23},{8,0},{9,25... | collective-permute-start | bytes 417800 | tf_op jit(solution)/shard_map/ppermute | solution.py:446
  47.8 0.0 collective-permute-start.17
  47.8 2.2 %collective-permute-start.18 = (bf16[272,256]{1,0:T(8,128)(2,1)S(1)}, bf16[272,256]{1,0:T(8,128)(2,1)S(1)}, u32[]{:S(2)}, u32[]{:S(2)}) collective-permute-start(bf16[272,256]{1,0:T(8,128)(2,1)S(1)} %get-tuple-element.56), channel_id=1, source_target_pairs={{0,24},{8,16},{16,8},{24,0},{1,25},{9,17},{17,9},{25,1},{2,26},{10... | collective-permute-start | bytes 417800 | tf_op jit(solution)/shard_map/ppermute | solution.py:437
  50.0 1.6 %collective-permute-done.16.refs_0_ = bf16[272,256]{1,0:T(8,128)(2,1)S(1)} collective-permute-done((bf16[272,256]{1,0:T(8,128)(2,1)S(1)}, bf16[272,256]{1,0:T(8,128)(2,1)S(1)}, u32[]{:S(2)}, u32[]{:S(2)}) %collective-permute-start.16) | collective-permute-done | bytes 139296 | tf_op jit(solution)/shard_map/ppermute | solution.py:446
  51.5 2.8 %collective-permute-done.17.refs_1_ = bf16[272,256]{1,0:T(8,128)(2,1)S(1)} collective-permute-done((bf16[272,256]{1,0:T(8,128)(2,1)S(1)}, bf16[272,256]{1,0:T(8,128)(2,1)S(1)}, u32[]{:S(2)}, u32[]{:S(2)}) %collective-permute-start.17) | collective-permute-done | bytes 139296 | tf_op jit(solution)/shard_map/ppermute | solution.py:446
  54.3 0.0 collective-permute-done.18.refs_2_
  54.3 2.1 %place.1 = (f32[1024,256]{1,0:T(8,128)}, f32[1,16]{1,0:T(1,128)}) custom-call(s32[8]{0:T(128)S(1)} %get-tuple-element.31.home_any, f32[256,256]{1,0:T(8,128)S(1)} %get-tuple-element.53.mine_ref, bf16[272,256]{1,0:T(8,128)(2,1)S(1)} %collective-permute-done.16.refs_0_, bf16[272,256]{1,0:T(8,128)(2,1)S(1)} %collective-permute-done.17.refs_1_, ...), custom_call_target="tpu_custom_call" | custom-call | flops 1500000000 | tf_op jit(solution)/shard_map/place/pallas_call | solution.py:623
  (18 shorter events, 0.0 us)
Async XLA Ops:
  0.6 11.6 %collective-permute-start = (bf16[256,1024]{1,0:T(8,128)(2,1)}, bf16[256,1024]{1,0:T(8,128)(2,1)S(1)}, u32[]{:S(2)}, u32[]{:S(2)}) collective-permute-start(bf16[256,1024]{1,0:T(8,128)(2,1)} %refs_8_.3), channel_id=1, source_target_pairs={{0,8},{1,17},{2,10},{3,19},{4,12},{5,21},{6,14},{7,23},{8,0},{9,25... | collective-permute-start | bytes 1572872 | tf_op jit(solution)/shard_map/ppermute | solution.py:446
  3.6 8.6 %copy-start = (bf16[1024,1024]{1,0:T(8,128)(2,1)S(1)}, bf16[1024,1024]{1,0:T(8,128)(2,1)}, u32[]{:S(2)}) copy-start(bf16[1024,1024]{1,0:T(8,128)(2,1)} %x_ref.1) | copy-start | bytes 6291460
  3.6 8.6 %copy-start.1 = (bf16[1024,256]{1,0:T(8,128)(2,1)S(1)}, bf16[1024,256]{1,0:T(8,128)(2,1)}, u32[]{:S(2)}) copy-start(bf16[1024,256]{1,0:T(8,128)(2,1)} %wk_ref.1) | copy-start | bytes 1572868
  3.6 8.6 %copy-start.2 = (bf16[1024,256]{1,0:T(8,128)(2,1)S(1)}, bf16[1024,256]{1,0:T(8,128)(2,1)}, u32[]{:S(2)}) copy-start(bf16[1024,256]{1,0:T(8,128)(2,1)} %wv_ref.1) | copy-start | bytes 1572868
  3.6 8.6 %copy-start.4 = (s32[1024]{0:T(1024)S(1)}, s32[1024]{0:T(1024)}, u32[]{:S(2)}) copy-start(s32[1024]{0:T(1024)} %param.20) | copy-start | bytes 12292
  3.6 8.6 %copy-start.7 = (f32[2,4]{1,0:T(2,128)S(1)}, f32[2,4]{1,0:T(2,128)}, u32[]{:S(2)}) copy-start(f32[2,4]{1,0:T(2,128)} %bias_ref.9) | copy-start | bytes 100
  7.7 8.5 %collective-permute-start.2 = (bf16[1040,256]{1,0:T(8,128)(2,1)S(1)}, bf16[1040,256]{1,0:T(8,128)(2,1)S(1)}, u32[]{:S(2)}, u32[]{:S(2)}) collective-permute-start(bf16[1040,256]{1,0:T(8,128)(2,1)S(1)} %get-tuple-element.41.own_ref), channel_id=1, source_target_pairs={{0,1},{1,0},{2,3},{3,2},{4,5},{5,4},{6,7},{7,6},{8,9},{9,8},{10,11... | collective-permute-start | bytes 1597448 | tf_op jit(solution)/shard_map/ppermute | solution.py:437
  7.7 11.6 %collective-permute-start.1 = (bf16[272,256]{1,0:T(8,128)(2,1)S(1)}, bf16[272,256]{1,0:T(8,128)(2,1)S(1)}, u32[]{:S(2)}, u32[]{:S(2)}) collective-permute-start(bf16[272,256]{1,0:T(8,128)(2,1)S(1)} %get-tuple-element.36.refs_1_), channel_id=1, source_target_pairs={{0,2},{1,3},{2,0},{3,1},{4,6},{5,7},{6,4},{7,5},{8,10},{9,11},{10,... | collective-permute-start | bytes 417800 | tf_op jit(solution)/shard_map/ppermute | solution.py:437
  9.4 13.4 %collective-permute-start.5 = (bf16[272,256]{1,0:T(8,128)(2,1)S(1)}, bf16[272,256]{1,0:T(8,128)(2,1)S(1)}, u32[]{:S(2)}, u32[]{:S(2)}) collective-permute-start(bf16[272,256]{1,0:T(8,128)(2,1)S(1)} %get-tuple-element.37.refs_2_), channel_id=1, source_target_pairs={{0,4},{1,5},{2,6},{3,7},{4,0},{5,1},{6,2},{7,3},{8,12},{9,13},{10,... | collective-permute-start | bytes 417800 | tf_op jit(solution)/shard_map/ppermute | solution.py:437
  12.0 14.7 %collective-permute-start.4 = (bf16[272,256]{1,0:T(8,128)(2,1)S(1)}, bf16[272,256]{1,0:T(8,128)(2,1)S(1)}, u32[]{:S(2)}, u32[]{:S(2)}) collective-permute-start(bf16[272,256]{1,0:T(8,128)(2,1)S(1)} %get-tuple-element.38.refs_3_), channel_id=1, source_target_pairs={{0,6},{1,7},{2,4},{3,5},{4,2},{5,3},{6,0},{7,1},{8,14},{9,15},{10,... | collective-permute-start | bytes 417800 | tf_op jit(solution)/shard_map/ppermute | solution.py:437
  16.1 12.4 %collective-permute-start.6 = (bf16[256,1024]{1,0:T(8,128)(2,1)S(1)}, bf16[256,1024]{1,0:T(8,128)(2,1)S(1)}, u32[]{:S(2)}, u32[]{:S(2)}) collective-permute-start(bf16[256,1024]{1,0:T(8,128)(2,1)S(1)} %get-tuple-element.42), channel_id=1, source_target_pairs={{0,1},{1,0},{2,3},{3,2},{4,5},{5,4},{6,7},{7,6},{8,9},{9,8},{10,11... | collective-permute-start | bytes 1572872 | tf_op jit(solution)/shard_map/ppermute | solution.py:437
  16.2 12.3 %collective-permute-start.7 = (bf16[256,1024]{1,0:T(8,128)(2,1)S(1)}, bf16[256,1024]{1,0:T(8,128)(2,1)S(1)}, u32[]{:S(2)}, u32[]{:S(2)}) collective-permute-start(bf16[256,1024]{1,0:T(8,128)(2,1)S(1)} %get-tuple-element.42), channel_id=1, source_target_pairs={{0,16},{1,9},{2,18},{3,11},{4,20},{5,13},{6,22},{7,15},{8,24},{9,1... | collective-permute-start | bytes 1572872 | tf_op jit(solution)/shard_map/ppermute | solution.py:446
  20.8 7.8 %collective-permute-start.3 = (bf16[272,256]{1,0:T(8,128)(2,1)S(1)}, bf16[272,256]{1,0:T(8,128)(2,1)S(1)}, u32[]{:S(2)}, u32[]{:S(2)}) collective-permute-start(bf16[272,256]{1,0:T(8,128)(2,1)S(1)} %cache_part.5.refs_0_), channel_id=1, source_target_pairs={{0,2},{1,3},{2,0},{3,1},{4,6},{5,7},{6,4},{7,5},{8,10},{9,11},{10,... | collective-permute-start | bytes 417800 | tf_op jit(solution)/shard_map/ppermute | solution.py:437
  24.3 12.6 %collective-permute-start.12 = (bf16[272,256]{1,0:T(8,128)(2,1)S(1)}, bf16[272,256]{1,0:T(8,128)(2,1)S(1)}, u32[]{:S(2)}, u32[]{:S(2)}) collective-permute-start(bf16[272,256]{1,0:T(8,128)(2,1)S(1)} %cache_part.6.refs_0_), channel_id=1, source_target_pairs={{0,4},{1,5},{2,6},{3,7},{4,0},{5,1},{6,2},{7,3},{8,12},{9,13},{10,... | collective-permute-start | bytes 417800 | tf_op jit(solution)/shard_map/ppermute | solution.py:437
  28.2 8.9 %collective-permute-start.11 = (bf16[272,256]{1,0:T(8,128)(2,1)S(1)}, bf16[272,256]{1,0:T(8,128)(2,1)S(1)}, u32[]{:S(2)}, u32[]{:S(2)}) collective-permute-start(bf16[272,256]{1,0:T(8,128)(2,1)S(1)} %cache_part.7.refs_0_), channel_id=1, source_target_pairs={{0,6},{1,7},{2,4},{3,5},{4,2},{5,3},{6,0},{7,1},{8,14},{9,15},{10,... | collective-permute-start | bytes 417800 | tf_op jit(solution)/shard_map/ppermute | solution.py:437
  28.8 8.3 %collective-permute-start.10 = (bf16[128,256]{1,0:T(8,128)(2,1)S(1)}, bf16[128,256]{1,0:T(8,128)(2,1)S(1)}, u32[]{:S(2)}, u32[]{:S(2)}) collective-permute-start(bf16[128,256]{1,0:T(8,128)(2,1)S(1)} %get-tuple-element.46), channel_id=1, source_target_pairs={{0,24},{8,16},{16,8},{24,0},{1,25},{9,17},{17,9},{25,1},{2,26},{10... | collective-permute-start | bytes 196616 | tf_op jit(solution)/shard_map/ppermute | solution.py:437
  30.3 6.8 %collective-permute-start.8 = (bf16[128,256]{1,0:T(8,128)(2,1)S(1)}, bf16[128,256]{1,0:T(8,128)(2,1)S(1)}, u32[]{:S(2)}, u32[]{:S(2)}) collective-permute-start(bf16[128,256]{1,0:T(8,128)(2,1)S(1)} %get-tuple-element.44), channel_id=1, source_target_pairs={{0,8},{1,17},{2,10},{3,19},{4,12},{5,21},{6,14},{7,23},{8,0},{9,25... | collective-permute-start | bytes 196616 | tf_op jit(solution)/shard_map/ppermute | solution.py:446
  31.8 5.3 %collective-permute-start.9 = (bf16[128,256]{1,0:T(8,128)(2,1)S(1)}, bf16[128,256]{1,0:T(8,128)(2,1)S(1)}, u32[]{:S(2)}, u32[]{:S(2)}) collective-permute-start(bf16[128,256]{1,0:T(8,128)(2,1)S(1)} %get-tuple-element.45), channel_id=1, source_target_pairs={{0,16},{1,9},{2,18},{3,11},{4,20},{5,13},{6,22},{7,15},{8,24},{9,1... | collective-permute-start | bytes 196616 | tf_op jit(solution)/shard_map/ppermute | solution.py:446
  37.0 8.3 %copy-start.3 = (bf16[256,1024]{1,0:T(8,128)(2,1)S(1)}, bf16[256,1024]{1,0:T(8,128)(2,1)}, u32[]{:S(2)}) copy-start(bf16[256,1024]{1,0:T(8,128)(2,1)} %refs_8_.3) | copy-start | bytes 1572868
  37.0 8.3 %copy-start.5 = (f32[1024]{0:T(1024)S(1)}, f32[1024]{0:T(1024)}, u32[]{:S(2)}) copy-start(f32[1024]{0:T(1024)} %param.31) | copy-start | bytes 12292
  37.0 8.3 %copy-start.6 = (f32[1024]{0:T(1024)S(1)}, f32[1024]{0:T(1024)}, u32[]{:S(2)}) copy-start(f32[1024]{0:T(1024)} %param.32) | copy-start | bytes 12292
  37.2 4.3 %collective-permute-start.13 = (bf16[128,256]{1,0:T(8,128)(2,1)S(1)}, bf16[128,256]{1,0:T(8,128)(2,1)S(1)}, u32[]{:S(2)}, u32[]{:S(2)}) collective-permute-start(bf16[128,256]{1,0:T(8,128)(2,1)S(1)} %get-tuple-element.48), channel_id=1, source_target_pairs={{0,8},{1,17},{2,10},{3,19},{4,12},{5,21},{6,14},{7,23},{8,0},{9,25... | collective-permute-start | bytes 196616 | tf_op jit(solution)/shard_map/ppermute | solution.py:446
  38.3 4.3 %collective-permute-start.14 = (bf16[128,256]{1,0:T(8,128)(2,1)S(1)}, bf16[128,256]{1,0:T(8,128)(2,1)S(1)}, u32[]{:S(2)}, u32[]{:S(2)}) collective-permute-start(bf16[128,256]{1,0:T(8,128)(2,1)S(1)} %get-tuple-element.49), channel_id=1, source_target_pairs={{0,16},{1,9},{2,18},{3,11},{4,20},{5,13},{6,22},{7,15},{8,24},{9,1... | collective-permute-start | bytes 196616 | tf_op jit(solution)/shard_map/ppermute | solution.py:446
  40.0 5.3 %collective-permute-start.15 = (bf16[128,256]{1,0:T(8,128)(2,1)S(1)}, bf16[128,256]{1,0:T(8,128)(2,1)S(1)}, u32[]{:S(2)}, u32[]{:S(2)}) collective-permute-start(bf16[128,256]{1,0:T(8,128)(2,1)S(1)} %get-tuple-element.50), channel_id=1, source_target_pairs={{0,24},{8,16},{16,8},{24,0},{1,25},{9,17},{17,9},{25,1},{2,26},{10... | collective-permute-start | bytes 196616 | tf_op jit(solution)/shard_map/ppermute | solution.py:437
  46.4 5.1 %collective-permute-start.16 = (bf16[272,256]{1,0:T(8,128)(2,1)S(1)}, bf16[272,256]{1,0:T(8,128)(2,1)S(1)}, u32[]{:S(2)}, u32[]{:S(2)}) collective-permute-start(bf16[272,256]{1,0:T(8,128)(2,1)S(1)} %get-tuple-element.54), channel_id=1, source_target_pairs={{0,8},{1,17},{2,10},{3,19},{4,12},{5,21},{6,14},{7,23},{8,0},{9,25... | collective-permute-start | bytes 417800 | tf_op jit(solution)/shard_map/ppermute | solution.py:446
  47.8 6.5 %collective-permute-start.17 = (bf16[272,256]{1,0:T(8,128)(2,1)S(1)}, bf16[272,256]{1,0:T(8,128)(2,1)S(1)}, u32[]{:S(2)}, u32[]{:S(2)}) collective-permute-start(bf16[272,256]{1,0:T(8,128)(2,1)S(1)} %get-tuple-element.55), channel_id=1, source_target_pairs={{0,16},{1,9},{2,18},{3,11},{4,20},{5,13},{6,22},{7,15},{8,24},{9,1... | collective-permute-start | bytes 417800 | tf_op jit(solution)/shard_map/ppermute | solution.py:446
  47.8 6.5 %collective-permute-start.18 = (bf16[272,256]{1,0:T(8,128)(2,1)S(1)}, bf16[272,256]{1,0:T(8,128)(2,1)S(1)}, u32[]{:S(2)}, u32[]{:S(2)}) collective-permute-start(bf16[272,256]{1,0:T(8,128)(2,1)S(1)} %get-tuple-element.56), channel_id=1, source_target_pairs={{0,24},{8,16},{16,8},{24,0},{1,25},{9,17},{17,9},{25,1},{2,26},{10... | collective-permute-start | bytes 417800 | tf_op jit(solution)/shard_map/ppermute | solution.py:437

commit v7 on v5

--- a/solution.py
+++ b/solution.py
@@ -377,23 +377,23 @@
     part = tokens // slots
     width = stage_ref.shape[0] // slots
     head = lax.axis_index("head")
+    sums = sums_ref[0:1, :]
+    for ref in got_refs:
+        block = ref[tokens:, 0:LANES].astype(F32)
+        sums = sums + (block[0:1] + block[1:2] + block[2:3])
+    moves = []
     for n in range(slots):
         for distance, ref in zip(distances(), (mine_ref, *got_refs)):
             start = pl.multiple_of(n * width + (head ^ distance) * part, part)
             stage_ref[pl.ds(start, part), :] = ref[n * part : (n + 1) * part, :].astype(F32)
-    home_move.wait()
-    moves = []
-    for n in range(slots):
+        if n == 0:
+            home_move.wait()
         to = pl.ds(pl.multiple_of(home_ref[n] * width, width), width)
         move = pltpu.make_async_copy(
             stage_ref.at[n * width : (n + 1) * width], update_hbm.at[to], sems.at[n]
         )
         move.start()
         moves.append(move)
-    sums = sums_ref[0:1, :]
-    for ref in got_refs:
-        block = ref[tokens:, 0:LANES].astype(F32)
-        sums = sums + (block[0:1] + block[1:2] + block[2:3])
     lane = lax.broadcasted_iota(jnp.int32, (1, LANES), 1)
     pooled = jnp.zeros((1, LANES), F32)
     for n in range(slots):

time: 56.6 us -> 56.6 us (level)
  no operation moved by 1% of the time
where the time goes in v7:
time: 56.6 us; the launch traced here: 56.5 us
  starting transfers between devices  23.3 us (41%)
  Pallas kernels  17.8 us (31%)
  waiting for transfers between devices  14.4 us (25%)
  between operations  0.87 us (2%)
    ppermute x11, starting transfers between devices, partner(): return lax.ppermute(value, axis, [(i, i ^ k) for i in range(count)])  12.6 us
    ppermute x8, starting transfers between devices, hop(): return lax.ppermute(value, ('head', 'blk'), pairs)  10.8 us
    ppermute x11, waiting for transfers between devices, partner(): return lax.ppermute(value, axis, [(i, i ^ k) for i in range(count)])  8.47 us
    pallas_call x4, Pallas kernels, body(): call(cache_kernel, chunk_shape, [VMEM] * 5 + [ANY] * len(after), out_spec...  6.01 us
    ppermute x8, waiting for transfers between devices, hop(): return lax.ppermute(value, ('head', 'blk'), pairs)  5.93 us
    pallas_call x1, Pallas kernels, body(): call(functools.partial(query_kernel, bpq, order), [sds((blocks,), i32), b...  4.11 us
    pallas_call x1, Pallas kernels, body(): call(own_kernel, [sds((slots, cols + 8, width), F32), sds((rows // heads,...  3.92 us
    pallas_call x1, Pallas kernels, body(): call(place_kernel, [sds((rows, cols), F32), sds((1, 2 * slots), F32)], [A...  2.14 us
  transfers between devices with their start and end apart: 19, of which 7 were waited for; matrix products, arithmetic and copies ran while one was open for 0% of the time, Pallas kernels for 26%

profile of v7, /device:TPU:0, one launch (start us, length us, event | category | flops | bytes accessed | tf_op | source)
XLA Modules:
  0.0 56.5 jit_solution(4709106283629365926)
XLA Ops:
  0.6 3.0 %collective-permute-start = (bf16[256,1024]{1,0:T(8,128)(2,1)}, bf16[256,1024]{1,0:T(8,128)(2,1)S(1)}, u32[]{:S(2)}, u32[]{:S(2)}) collective-permute-start(bf16[256,1024]{1,0:T(8,128)(2,1)} %refs_8_.3), channel_id=1, source_target_pairs={{0,8},{1,17},{2,10},{3,19},{4,12},{5,21},{6,14},{7,23},{8,0},{9,25... | collective-permute-start | bytes 1572872 | tf_op jit(solution)/shard_map/ppermute | solution.py:439
  3.7 0.0 copy-start.8
  3.7 4.1 %query.1 = (s32[8]{0:T(128)S(1)}, f32[5,8,128]{2,1,0:T(8,128)S(1)}, s32[8,128]{1,0:T(8,128)S(1)}, bf16[1040,256]{1,0:T(8,128)(2,1)S(1)}, bf16[272,256]{1,0:T(8,1...) custom-call(s32[128]{0:T(128)} %refs_0_.1, s32[8]{0:T(128)} %refs_1_.1, ...), custom_call_target="tpu_custom_call" | custom-call | flops 3500000000 | tf_op jit(solution)/shard_map/query/pallas_call | solution.py:487
  7.8 0.1 collective-permute-start.2
  7.9 1.6 %collective-permute-start.1 = (bf16[272,256]{1,0:T(8,128)(2,1)S(1)}, bf16[272,256]{1,0:T(8,128)(2,1)S(1)}, u32[]{:S(2)}, u32[]{:S(2)}) collective-permute-start(bf16[272,256]{1,0:T(8,128)(2,1)S(1)} %get-tuple-element.32.refs_1_), channel_id=1, source_target_pairs={{0,2},{1,3},{2,0},{3,1},{4,6},{5,7},{6,4},{7,5},{8,10},{9,11},{10,... | collective-permute-start | bytes 417800 | tf_op jit(solution)/shard_map/ppermute | solution.py:430
  9.5 2.6 %collective-permute-start.5 = (bf16[272,256]{1,0:T(8,128)(2,1)S(1)}, bf16[272,256]{1,0:T(8,128)(2,1)S(1)}, u32[]{:S(2)}, u32[]{:S(2)}) collective-permute-start(bf16[272,256]{1,0:T(8,128)(2,1)S(1)} %get-tuple-element.33.refs_2_), channel_id=1, source_target_pairs={{0,4},{1,5},{2,6},{3,7},{4,0},{5,1},{6,2},{7,3},{8,12},{9,13},{10,... | collective-permute-start | bytes 417800 | tf_op jit(solution)/shard_map/ppermute | solution.py:430
  12.1 0.2 collective-permute-start.4
  12.4 3.9 %own_documents.1 = (f32[8,264,128]{2,1,0:T(8,128)S(1)}, bf16[256,1024]{1,0:T(8,128)(2,1)S(1)}, f32[8,128]{1,0:T(8,128)S(1)}, bf16[256,1024]{1,0:T(8,128)(2,1)S(1)}) custom-call(s32[8]{0:T(128)S(1)} %get-tuple-element.29.home_any, f32[2,4]{1,0:T(2,128)S(1)} %copy-done.7, bf16[1024,1024]{1,0:T(8,128)(2,1)S(1)} %copy-done, bf16[1024,256]{1,0:T(8,128)(2,1)S(1)} %copy-done.1, ...), custom_call_target="tpu_custom_call" | custom-call | flops 4000000000 | tf_op jit(solution)/shard_map/own_documents/pallas_call | solution.py:524
  16.3 0.1 collective-permute-start.6
  16.4 1.6 %collective-permute-start.7 = (bf16[256,1024]{1,0:T(8,128)(2,1)S(1)}, bf16[256,1024]{1,0:T(8,128)(2,1)S(1)}, u32[]{:S(2)}, u32[]{:S(2)}) collective-permute-start(bf16[256,1024]{1,0:T(8,128)(2,1)S(1)} %get-tuple-element.38), channel_id=1, source_target_pairs={{0,16},{1,9},{2,18},{3,11},{4,20},{5,13},{6,22},{7,15},{8,24},{9,1... | collective-permute-start | bytes 1572872 | tf_op jit(solution)/shard_map/ppermute | solution.py:439
  18.0 1.5 %cache_part.4.refs_0_.got_ref = bf16[272,256]{1,0:T(8,128)(2,1)S(1)} custom-call(s32[8,128]{1,0:T(8,128)S(1)} %get-tuple-element.36.usable_ref, f32[2,4]{1,0:T(2,128)S(1)} %copy-done.7, bf16[272,256]{1,0:T(8,128)(2,1)S(1)} %get-tuple-element.31.refs_0_.q_ref, bf16[1040,256]{1,0:T(8,128)(2,1)S(1)} %get-tuple-element.37.own_ref, ...), custom_call_target="tpu_custom_call" | custom-call | flops 1500000000 | tf_op jit(solution)/shard_map/cache_part/pallas_call | solution.py:545
  19.5 1.5 %cache_part.5.refs_0_ = bf16[272,256]{1,0:T(8,128)(2,1)S(1)} custom-call(s32[8,128]{1,0:T(8,128)S(1)} %get-tuple-element.36.usable_ref, f32[2,4]{1,0:T(2,128)S(1)} %copy-done.7, bf16[272,256]{1,0:T(8,128)(2,1)S(1)} %collective-permute-done.1.q_ref, bf16[1040,256]{1,0:T(8,128)(2,1)S(1)} %get-tuple-element.37.own_ref, ...), custom_call_target="tpu_custom_call" | custom-call | flops 1500000000 | tf_op jit(solution)/shard_map/cache_part/pallas_call | solution.py:545
  21.0 0.9 %collective-permute-start.3 = (bf16[272,256]{1,0:T(8,128)(2,1)S(1)}, bf16[272,256]{1,0:T(8,128)(2,1)S(1)}, u32[]{:S(2)}, u32[]{:S(2)}) collective-permute-start(bf16[272,256]{1,0:T(8,128)(2,1)S(1)} %cache_part.5.refs_0_), channel_id=1, source_target_pairs={{0,2},{1,3},{2,0},{3,1},{4,6},{5,7},{6,4},{7,5},{8,10},{9,11},{10,... | collective-permute-start | bytes 417800 | tf_op jit(solution)/shard_map/ppermute | solution.py:430
  21.9 1.1 %collective-permute-done.5.q_ref = bf16[272,256]{1,0:T(8,128)(2,1)S(1)} collective-permute-done((bf16[272,256]{1,0:T(8,128)(2,1)S(1)}, bf16[272,256]{1,0:T(8,128)(2,1)S(1)}, u32[]{:S(2)}, u32[]{:S(2)}) %collective-permute-start.5) | collective-permute-done | bytes 139296 | tf_op jit(solution)/shard_map/ppermute | solution.py:430
  22.9 1.5 %cache_part.6.refs_0_ = bf16[272,256]{1,0:T(8,128)(2,1)S(1)} custom-call(s32[8,128]{1,0:T(8,128)S(1)} %get-tuple-element.36.usable_ref, f32[2,4]{1,0:T(2,128)S(1)} %copy-done.7, bf16[272,256]{1,0:T(8,128)(2,1)S(1)} %collective-permute-done.5.q_ref, bf16[1040,256]{1,0:T(8,128)(2,1)S(1)} %get-tuple-element.37.own_ref, ...), custom_call_target="tpu_custom_call" | custom-call | flops 1500000000 | tf_op jit(solution)/shard_map/cache_part/pallas_call | solution.py:545
  24.5 2.4 %collective-permute-start.12 = (bf16[272,256]{1,0:T(8,128)(2,1)S(1)}, bf16[272,256]{1,0:T(8,128)(2,1)S(1)}, u32[]{:S(2)}, u32[]{:S(2)}) collective-permute-start(bf16[272,256]{1,0:T(8,128)(2,1)S(1)} %cache_part.6.refs_0_), channel_id=1, source_target_pairs={{0,4},{1,5},{2,6},{3,7},{4,0},{5,1},{6,2},{7,3},{8,12},{9,13},{10,... | collective-permute-start | bytes 417800 | tf_op jit(solution)/shard_map/ppermute | solution.py:430
  26.8 0.0 collective-permute-done.4.q_ref
  26.8 1.5 %cache_part.7.refs_0_ = bf16[272,256]{1,0:T(8,128)(2,1)S(1)} custom-call(s32[8,128]{1,0:T(8,128)S(1)} %get-tuple-element.36.usable_ref, f32[2,4]{1,0:T(2,128)S(1)} %copy-done.7, bf16[272,256]{1,0:T(8,128)(2,1)S(1)} %collective-permute-done.4.q_ref, bf16[1040,256]{1,0:T(8,128)(2,1)S(1)} %get-tuple-element.37.own_ref, ...), custom_call_target="tpu_custom_call" | custom-call | flops 1500000000 | tf_op jit(solution)/shard_map/cache_part/pallas_call | solution.py:545
  28.3 0.3 collective-permute-start.11
  28.6 0.0 collective-permute-done.6.refs_1_.refs_10_
  28.6 0.0 collective-permute-done.7.refs_2_.refs_11_
  28.6 0.1 merge.2.refs_0_.refs_1_
  28.8 0.1 last_merge.2
  28.9 1.5 %collective-permute-start.10 = (bf16[128,256]{1,0:T(8,128)(2,1)S(1)}, bf16[128,256]{1,0:T(8,128)(2,1)S(1)}, u32[]{:S(2)}, u32[]{:S(2)}) collective-permute-start(bf16[128,256]{1,0:T(8,128)(2,1)S(1)} %get-tuple-element.42), channel_id=1, source_target_pairs={{0,24},{8,16},{16,8},{24,0},{1,25},{9,17},{17,9},{25,1},{2,26},{10... | collective-permute-start | bytes 196616 | tf_op jit(solution)/shard_map/ppermute | solution.py:430
  30.5 1.5 %collective-permute-start.8 = (bf16[128,256]{1,0:T(8,128)(2,1)S(1)}, bf16[128,256]{1,0:T(8,128)(2,1)S(1)}, u32[]{:S(2)}, u32[]{:S(2)}) collective-permute-start(bf16[128,256]{1,0:T(8,128)(2,1)S(1)} %get-tuple-element.40), channel_id=1, source_target_pairs={{0,8},{1,17},{2,10},{3,19},{4,12},{5,21},{6,14},{7,23},{8,0},{9,25... | collective-permute-start | bytes 196616 | tf_op jit(solution)/shard_map/ppermute | solution.py:439
  32.0 0.5 collective-permute-start.9
  32.5 4.5 %collective-permute-done.12.got_ref = bf16[272,256]{1,0:T(8,128)(2,1)S(1)} collective-permute-done((bf16[272,256]{1,0:T(8,128)(2,1)S(1)}, bf16[272,256]{1,0:T(8,128)(2,1)S(1)}, u32[]{:S(2)}, u32[]{:S(2)}) %collective-permute-start.12) | collective-permute-done | bytes 139296 | tf_op jit(solution)/shard_map/ppermute | solution.py:430
  37.0 0.1 merge.3.refs_0_.refs_1_
  37.2 0.0 copy-start.3
  37.2 0.0 copy-start.5
  37.2 0.0 copy-start.6
  37.2 0.0 collective-permute-done.10.refs_4_.refs_3_
  37.2 0.0 collective-permute-done.8.refs_2_.refs_1_
  37.2 0.1 last_merge.3
  37.4 1.0 %collective-permute-start.13 = (bf16[128,256]{1,0:T(8,128)(2,1)S(1)}, bf16[128,256]{1,0:T(8,128)(2,1)S(1)}, u32[]{:S(2)}, u32[]{:S(2)}) collective-permute-start(bf16[128,256]{1,0:T(8,128)(2,1)S(1)} %get-tuple-element.44), channel_id=1, source_target_pairs={{0,8},{1,17},{2,10},{3,19},{4,12},{5,21},{6,14},{7,23},{8,0},{9,25... | collective-permute-start | bytes 196616 | tf_op jit(solution)/shard_map/ppermute | solution.py:439
  38.4 1.8 %collective-permute-start.14 = (bf16[128,256]{1,0:T(8,128)(2,1)S(1)}, bf16[128,256]{1,0:T(8,128)(2,1)S(1)}, u32[]{:S(2)}, u32[]{:S(2)}) collective-permute-start(bf16[128,256]{1,0:T(8,128)(2,1)S(1)} %get-tuple-element.45), channel_id=1, source_target_pairs={{0,16},{1,9},{2,18},{3,11},{4,20},{5,13},{6,22},{7,15},{8,24},{9,1... | collective-permute-start | bytes 196616 | tf_op jit(solution)/shard_map/ppermute | solution.py:439
  40.2 0.7 %collective-permute-start.15 = (bf16[128,256]{1,0:T(8,128)(2,1)S(1)}, bf16[128,256]{1,0:T(8,128)(2,1)S(1)}, u32[]{:S(2)}, u32[]{:S(2)}) collective-permute-start(bf16[128,256]{1,0:T(8,128)(2,1)S(1)} %get-tuple-element.46), channel_id=1, source_target_pairs={{0,24},{8,16},{16,8},{24,0},{1,25},{9,17},{17,9},{25,1},{2,26},{10... | collective-permute-start | bytes 196616 | tf_op jit(solution)/shard_map/ppermute | solution.py:430
  41.0 0.8 %collective-permute-done.13.refs_5_ = bf16[128,256]{1,0:T(8,128)(2,1)S(1)} collective-permute-done((bf16[128,256]{1,0:T(8,128)(2,1)S(1)}, bf16[128,256]{1,0:T(8,128)(2,1)S(1)}, u32[]{:S(2)}, u32[]{:S(2)}) %collective-permute-start.13) | collective-permute-done | bytes 65568 | tf_op jit(solution)/shard_map/ppermute | solution.py:439
  41.7 1.0 %collective-permute-done.14.refs_6_ = bf16[128,256]{1,0:T(8,128)(2,1)S(1)} collective-permute-done((bf16[128,256]{1,0:T(8,128)(2,1)S(1)}, bf16[128,256]{1,0:T(8,128)(2,1)S(1)}, u32[]{:S(2)}, u32[]{:S(2)}) %collective-permute-start.14) | collective-permute-done | bytes 65568 | tf_op jit(solution)/shard_map/ppermute | solution.py:439
  42.7 2.8 %collective-permute-done.15.refs_7_ = bf16[128,256]{1,0:T(8,128)(2,1)S(1)} collective-permute-done((bf16[128,256]{1,0:T(8,128)(2,1)S(1)}, bf16[128,256]{1,0:T(8,128)(2,1)S(1)}, u32[]{:S(2)}, u32[]{:S(2)}) %collective-permute-start.15) | collective-permute-done | bytes 65568 | tf_op jit(solution)/shard_map/ppermute | solution.py:430
  45.5 1.0 %output.1 = (f32[256,256]{1,0:T(8,128)S(1)}, f32[8,128]{1,0:T(8,128)S(1)}, bf16[272,256]{1,0:T(8,128)(2,1)S(1)}, bf16[272,256]{1,0:T(8,128)(2,1)S(1)}, bf16[272,256]{1,0:T(8,128)(2,1)S(1)}) custom-call(bf16[128,256]{1,0:T(8,128)(2,1)S(1)} %get-tuple-element.39.refs_0_, bf16[128,256]{1,0:T(8,128)(2,1)S(1)} %collective-permute-done.8.refs_2_.refs_1_, ...), custom_call_target="tpu_custom_call" | custom-call | flops 2000000000 | tf_op jit(solution)/shard_map/output/pallas_call | solution.py:603
  46.6 1.2 %collective-permute-start.16 = (bf16[272,256]{1,0:T(8,128)(2,1)S(1)}, bf16[272,256]{1,0:T(8,128)(2,1)S(1)}, u32[]{:S(2)}, u32[]{:S(2)}) collective-permute-start(bf16[272,256]{1,0:T(8,128)(2,1)S(1)} %get-tuple-element.50), channel_id=1, source_target_pairs={{0,8},{1,17},{2,10},{3,19},{4,12},{5,21},{6,14},{7,23},{8,0},{9,25... | collective-permute-start | bytes 417800 | tf_op jit(solution)/shard_map/ppermute | solution.py:439
  47.8 0.1 collective-permute-start.17
  47.9 2.2 %collective-permute-start.18 = (bf16[272,256]{1,0:T(8,128)(2,1)S(1)}, bf16[272,256]{1,0:T(8,128)(2,1)S(1)}, u32[]{:S(2)}, u32[]{:S(2)}) collective-permute-start(bf16[272,256]{1,0:T(8,128)(2,1)S(1)} %get-tuple-element.52), channel_id=1, source_target_pairs={{0,24},{8,16},{16,8},{24,0},{1,25},{9,17},{17,9},{25,1},{2,26},{10... | collective-permute-start | bytes 417800 | tf_op jit(solution)/shard_map/ppermute | solution.py:430
  50.1 1.6 %collective-permute-done.16.refs_0_ = bf16[272,256]{1,0:T(8,128)(2,1)S(1)} collective-permute-done((bf16[272,256]{1,0:T(8,128)(2,1)S(1)}, bf16[272,256]{1,0:T(8,128)(2,1)S(1)}, u32[]{:S(2)}, u32[]{:S(2)}) %collective-permute-start.16) | collective-permute-done | bytes 139296 | tf_op jit(solution)/shard_map/ppermute | solution.py:439
  51.7 2.6 %collective-permute-done.17.refs_1_ = bf16[272,256]{1,0:T(8,128)(2,1)S(1)} collective-permute-done((bf16[272,256]{1,0:T(8,128)(2,1)S(1)}, bf16[272,256]{1,0:T(8,128)(2,1)S(1)}, u32[]{:S(2)}, u32[]{:S(2)}) %collective-permute-start.17) | collective-permute-done | bytes 139296 | tf_op jit(solution)/shard_map/ppermute | solution.py:439
  54.3 0.0 collective-permute-done.18.refs_2_
  54.3 2.1 %place.1 = (f32[1024,256]{1,0:T(8,128)}, f32[1,16]{1,0:T(1,128)}) custom-call(s32[8]{0:T(128)S(1)} %get-tuple-element.29.home_any, f32[256,256]{1,0:T(8,128)S(1)} %get-tuple-element.49.mine_ref, bf16[272,256]{1,0:T(8,128)(2,1)S(1)} %collective-permute-done.16.refs_0_, bf16[272,256]{1,0:T(8,128)(2,1)S(1)} %collective-permute-done.17.refs_1_, ...), custom_call_target="tpu_custom_call" | custom-call | flops 1500000000 | tf_op jit(solution)/shard_map/place/pallas_call | solution.py:615
  (20 shorter events, 0.0 us)
Async XLA Ops:
  0.6 11.7 %collective-permute-start = (bf16[256,1024]{1,0:T(8,128)(2,1)}, bf16[256,1024]{1,0:T(8,128)(2,1)S(1)}, u32[]{:S(2)}, u32[]{:S(2)}) collective-permute-start(bf16[256,1024]{1,0:T(8,128)(2,1)} %refs_8_.3), channel_id=1, source_target_pairs={{0,8},{1,17},{2,10},{3,19},{4,12},{5,21},{6,14},{7,23},{8,0},{9,25... | collective-permute-start | bytes 1572872 | tf_op jit(solution)/shard_map/ppermute | solution.py:439
  3.6 8.7 %copy-start = (bf16[1024,1024]{1,0:T(8,128)(2,1)S(1)}, bf16[1024,1024]{1,0:T(8,128)(2,1)}, u32[]{:S(2)}) copy-start(bf16[1024,1024]{1,0:T(8,128)(2,1)} %x_ref.1) | copy-start | bytes 6291460
  3.6 8.7 %copy-start.1 = (bf16[1024,256]{1,0:T(8,128)(2,1)S(1)}, bf16[1024,256]{1,0:T(8,128)(2,1)}, u32[]{:S(2)}) copy-start(bf16[1024,256]{1,0:T(8,128)(2,1)} %wk_ref.1) | copy-start | bytes 1572868
  3.6 8.7 %copy-start.2 = (bf16[1024,256]{1,0:T(8,128)(2,1)S(1)}, bf16[1024,256]{1,0:T(8,128)(2,1)}, u32[]{:S(2)}) copy-start(bf16[1024,256]{1,0:T(8,128)(2,1)} %wv_ref.1) | copy-start | bytes 1572868
  3.6 8.7 %copy-start.4 = (s32[1024]{0:T(1024)S(1)}, s32[1024]{0:T(1024)}, u32[]{:S(2)}) copy-start(s32[1024]{0:T(1024)} %param.20) | copy-start | bytes 12292
  3.6 8.7 %copy-start.7 = (f32[2,4]{1,0:T(2,128)S(1)}, f32[2,4]{1,0:T(2,128)}, u32[]{:S(2)}) copy-start(f32[2,4]{1,0:T(2,128)} %bias_ref.9) | copy-start | bytes 100
  3.7 8.7 %copy-start.8 = (f32[264,128]{1,0:T(8,128)S(1)}, f32[264,128]{1,0:T(8,128)}, u32[]{:S(2)}) copy-start(f32[264,128]{1,0:T(8,128)} %constant.2.clone.refs_5_.table_ref) | copy-start | bytes 405508
  7.8 8.6 %collective-permute-start.2 = (bf16[1040,256]{1,0:T(8,128)(2,1)S(1)}, bf16[1040,256]{1,0:T(8,128)(2,1)S(1)}, u32[]{:S(2)}, u32[]{:S(2)}) collective-permute-start(bf16[1040,256]{1,0:T(8,128)(2,1)S(1)} %get-tuple-element.37.own_ref), channel_id=1, source_target_pairs={{0,1},{1,0},{2,3},{3,2},{4,5},{5,4},{6,7},{7,6},{8,9},{9,8},{10,11... | collective-permute-start | bytes 1597448 | tf_op jit(solution)/shard_map/ppermute | solution.py:430
  7.9 11.6 %collective-permute-start.1 = (bf16[272,256]{1,0:T(8,128)(2,1)S(1)}, bf16[272,256]{1,0:T(8,128)(2,1)S(1)}, u32[]{:S(2)}, u32[]{:S(2)}) collective-permute-start(bf16[272,256]{1,0:T(8,128)(2,1)S(1)} %get-tuple-element.32.refs_1_), channel_id=1, source_target_pairs={{0,2},{1,3},{2,0},{3,1},{4,6},{5,7},{6,4},{7,5},{8,10},{9,11},{10,... | collective-permute-start | bytes 417800 | tf_op jit(solution)/shard_map/ppermute | solution.py:430
  9.5 13.4 %collective-permute-start.5 = (bf16[272,256]{1,0:T(8,128)(2,1)S(1)}, bf16[272,256]{1,0:T(8,128)(2,1)S(1)}, u32[]{:S(2)}, u32[]{:S(2)}) collective-permute-start(bf16[272,256]{1,0:T(8,128)(2,1)S(1)} %get-tuple-element.33.refs_2_), channel_id=1, source_target_pairs={{0,4},{1,5},{2,6},{3,7},{4,0},{5,1},{6,2},{7,3},{8,12},{9,13},{10,... | collective-permute-start | bytes 417800 | tf_op jit(solution)/shard_map/ppermute | solution.py:430
  12.1 14.7 %collective-permute-start.4 = (bf16[272,256]{1,0:T(8,128)(2,1)S(1)}, bf16[272,256]{1,0:T(8,128)(2,1)S(1)}, u32[]{:S(2)}, u32[]{:S(2)}) collective-permute-start(bf16[272,256]{1,0:T(8,128)(2,1)S(1)} %get-tuple-element.34.refs_3_), channel_id=1, source_target_pairs={{0,6},{1,7},{2,4},{3,5},{4,2},{5,3},{6,0},{7,1},{8,14},{9,15},{10,... | collective-permute-start | bytes 417800 | tf_op jit(solution)/shard_map/ppermute | solution.py:430
  16.3 12.3 %collective-permute-start.6 = (bf16[256,1024]{1,0:T(8,128)(2,1)S(1)}, bf16[256,1024]{1,0:T(8,128)(2,1)S(1)}, u32[]{:S(2)}, u32[]{:S(2)}) collective-permute-start(bf16[256,1024]{1,0:T(8,128)(2,1)S(1)} %get-tuple-element.38), channel_id=1, source_target_pairs={{0,1},{1,0},{2,3},{3,2},{4,5},{5,4},{6,7},{7,6},{8,9},{9,8},{10,11... | collective-permute-start | bytes 1572872 | tf_op jit(solution)/shard_map/ppermute | solution.py:430
  16.4 12.2 %collective-permute-start.7 = (bf16[256,1024]{1,0:T(8,128)(2,1)S(1)}, bf16[256,1024]{1,0:T(8,128)(2,1)S(1)}, u32[]{:S(2)}, u32[]{:S(2)}) collective-permute-start(bf16[256,1024]{1,0:T(8,128)(2,1)S(1)} %get-tuple-element.38), channel_id=1, source_target_pairs={{0,16},{1,9},{2,18},{3,11},{4,20},{5,13},{6,22},{7,15},{8,24},{9,1... | collective-permute-start | bytes 1572872 | tf_op jit(solution)/shard_map/ppermute | solution.py:439
  21.0 7.8 %collective-permute-start.3 = (bf16[272,256]{1,0:T(8,128)(2,1)S(1)}, bf16[272,256]{1,0:T(8,128)(2,1)S(1)}, u32[]{:S(2)}, u32[]{:S(2)}) collective-permute-start(bf16[272,256]{1,0:T(8,128)(2,1)S(1)} %cache_part.5.refs_0_), channel_id=1, source_target_pairs={{0,2},{1,3},{2,0},{3,1},{4,6},{5,7},{6,4},{7,5},{8,10},{9,11},{10,... | collective-permute-start | bytes 417800 | tf_op jit(solution)/shard_map/ppermute | solution.py:430
  24.5 12.6 %collective-permute-start.12 = (bf16[272,256]{1,0:T(8,128)(2,1)S(1)}, bf16[272,256]{1,0:T(8,128)(2,1)S(1)}, u32[]{:S(2)}, u32[]{:S(2)}) collective-permute-start(bf16[272,256]{1,0:T(8,128)(2,1)S(1)} %cache_part.6.refs_0_), channel_id=1, source_target_pairs={{0,4},{1,5},{2,6},{3,7},{4,0},{5,1},{6,2},{7,3},{8,12},{9,13},{10,... | collective-permute-start | bytes 417800 | tf_op jit(solution)/shard_map/ppermute | solution.py:430
  28.3 8.9 %collective-permute-start.11 = (bf16[272,256]{1,0:T(8,128)(2,1)S(1)}, bf16[272,256]{1,0:T(8,128)(2,1)S(1)}, u32[]{:S(2)}, u32[]{:S(2)}) collective-permute-start(bf16[272,256]{1,0:T(8,128)(2,1)S(1)} %cache_part.7.refs_0_), channel_id=1, source_target_pairs={{0,6},{1,7},{2,4},{3,5},{4,2},{5,3},{6,0},{7,1},{8,14},{9,15},{10,... | collective-permute-start | bytes 417800 | tf_op jit(solution)/shard_map/ppermute | solution.py:430
  28.9 8.3 %collective-permute-start.10 = (bf16[128,256]{1,0:T(8,128)(2,1)S(1)}, bf16[128,256]{1,0:T(8,128)(2,1)S(1)}, u32[]{:S(2)}, u32[]{:S(2)}) collective-permute-start(bf16[128,256]{1,0:T(8,128)(2,1)S(1)} %get-tuple-element.42), channel_id=1, source_target_pairs={{0,24},{8,16},{16,8},{24,0},{1,25},{9,17},{17,9},{25,1},{2,26},{10... | collective-permute-start | bytes 196616 | tf_op jit(solution)/shard_map/ppermute | solution.py:430
  30.5 6.8 %collective-permute-start.8 = (bf16[128,256]{1,0:T(8,128)(2,1)S(1)}, bf16[128,256]{1,0:T(8,128)(2,1)S(1)}, u32[]{:S(2)}, u32[]{:S(2)}) collective-permute-start(bf16[128,256]{1,0:T(8,128)(2,1)S(1)} %get-tuple-element.40), channel_id=1, source_target_pairs={{0,8},{1,17},{2,10},{3,19},{4,12},{5,21},{6,14},{7,23},{8,0},{9,25... | collective-permute-start | bytes 196616 | tf_op jit(solution)/shard_map/ppermute | solution.py:439
  32.0 5.3 %collective-permute-start.9 = (bf16[128,256]{1,0:T(8,128)(2,1)S(1)}, bf16[128,256]{1,0:T(8,128)(2,1)S(1)}, u32[]{:S(2)}, u32[]{:S(2)}) collective-permute-start(bf16[128,256]{1,0:T(8,128)(2,1)S(1)} %get-tuple-element.41), channel_id=1, source_target_pairs={{0,16},{1,9},{2,18},{3,11},{4,20},{5,13},{6,22},{7,15},{8,24},{9,1... | collective-permute-start | bytes 196616 | tf_op jit(solution)/shard_map/ppermute | solution.py:439
  37.2 8.3 %copy-start.3 = (bf16[256,1024]{1,0:T(8,128)(2,1)S(1)}, bf16[256,1024]{1,0:T(8,128)(2,1)}, u32[]{:S(2)}) copy-start(bf16[256,1024]{1,0:T(8,128)(2,1)} %refs_8_.3) | copy-start | bytes 1572868
  37.2 8.3 %copy-start.5 = (f32[1024]{0:T(1024)S(1)}, f32[1024]{0:T(1024)}, u32[]{:S(2)}) copy-start(f32[1024]{0:T(1024)} %param.31) | copy-start | bytes 12292
  37.2 8.3 %copy-start.6 = (f32[1024]{0:T(1024)S(1)}, f32[1024]{0:T(1024)}, u32[]{:S(2)}) copy-start(f32[1024]{0:T(1024)} %param.32) | copy-start | bytes 12292
  37.4 4.3 %collective-permute-start.13 = (bf16[128,256]{1,0:T(8,128)(2,1)S(1)}, bf16[128,256]{1,0:T(8,128)(2,1)S(1)}, u32[]{:S(2)}, u32[]{:S(2)}) collective-permute-start(bf16[128,256]{1,0:T(8,128)(2,1)S(1)} %get-tuple-element.44), channel_id=1, source_target_pairs={{0,8},{1,17},{2,10},{3,19},{4,12},{5,21},{6,14},{7,23},{8,0},{9,25... | collective-permute-start | bytes 196616 | tf_op jit(solution)/shard_map/ppermute | solution.py:439
  38.4 4.3 %collective-permute-start.14 = (bf16[128,256]{1,0:T(8,128)(2,1)S(1)}, bf16[128,256]{1,0:T(8,128)(2,1)S(1)}, u32[]{:S(2)}, u32[]{:S(2)}) collective-permute-start(bf16[128,256]{1,0:T(8,128)(2,1)S(1)} %get-tuple-element.45), channel_id=1, source_target_pairs={{0,16},{1,9},{2,18},{3,11},{4,20},{5,13},{6,22},{7,15},{8,24},{9,1... | collective-permute-start | bytes 196616 | tf_op jit(solution)/shard_map/ppermute | solution.py:439
  40.2 5.3 %collective-permute-start.15 = (bf16[128,256]{1,0:T(8,128)(2,1)S(1)}, bf16[128,256]{1,0:T(8,128)(2,1)S(1)}, u32[]{:S(2)}, u32[]{:S(2)}) collective-permute-start(bf16[128,256]{1,0:T(8,128)(2,1)S(1)} %get-tuple-element.46), channel_id=1, source_target_pairs={{0,24},{8,16},{16,8},{24,0},{1,25},{9,17},{17,9},{25,1},{2,26},{10... | collective-permute-start | bytes 196616 | tf_op jit(solution)/shard_map/ppermute | solution.py:430
  46.6 5.1 %collective-permute-start.16 = (bf16[272,256]{1,0:T(8,128)(2,1)S(1)}, bf16[272,256]{1,0:T(8,128)(2,1)S(1)}, u32[]{:S(2)}, u32[]{:S(2)}) collective-permute-start(bf16[272,256]{1,0:T(8,128)(2,1)S(1)} %get-tuple-element.50), channel_id=1, source_target_pairs={{0,8},{1,17},{2,10},{3,19},{4,12},{5,21},{6,14},{7,23},{8,0},{9,25... | collective-permute-start | bytes 417800 | tf_op jit(solution)/shard_map/ppermute | solution.py:439
  47.8 6.5 %collective-permute-start.17 = (bf16[272,256]{1,0:T(8,128)(2,1)S(1)}, bf16[272,256]{1,0:T(8,128)(2,1)S(1)}, u32[]{:S(2)}, u32[]{:S(2)}) collective-permute-start(bf16[272,256]{1,0:T(8,128)(2,1)S(1)} %get-tuple-element.51), channel_id=1, source_target_pairs={{0,16},{1,9},{2,18},{3,11},{4,20},{5,13},{6,22},{7,15},{8,24},{9,1... | collective-permute-start | bytes 417800 | tf_op jit(solution)/shard_map/ppermute | solution.py:439
  47.9 6.4 %collective-permute-start.18 = (bf16[272,256]{1,0:T(8,128)(2,1)S(1)}, bf16[272,256]{1,0:T(8,128)(2,1)S(1)}, u32[]{:S(2)}, u32[]{:S(2)}) collective-permute-start(bf16[272,256]{1,0:T(8,128)(2,1)S(1)} %get-tuple-element.52), channel_id=1, source_target_pairs={{0,24},{8,16},{16,8},{24,0},{1,25},{9,17},{17,9},{25,1},{2,26},{10... | collective-permute-start | bytes 417800 | tf_op jit(solution)/shard_map/ppermute | solution.py:430
